TPU v7x, 256 devices: a whole 4x4x8 slice. The times are simulated.
256 devices in a mesh: dom: 16 (over z, core), sub: 16 (over x, y).
Axes of the slice: x: 4, y: 4, z: 8, core: 2. Of those that a mesh axis runs over, the one named last changes fastest.
Arguments:
- a_blocks: bfloat16 [21504, 7, 64, 64], P(('dom', 'sub')), may hold values from -0.75 to 0.75
- a_cols: int32 [21504, 7], P(('dom', 'sub')), may hold values from 0 to 21503, as said below
- p_blocks: bfloat16 [21504, 3, 64, 64], P(('dom', 'sub')), may hold values from -0.75 to 0.75
- p_cols: int32 [21504, 3], P(('dom', 'sub')), may hold values from 0 to 6143, as said below
- c_cols: int32 [6144, 8], P(('dom', 'sub')), may hold values from 0 to 6143, as said below
Outputs:
- coarse_blocks: bfloat16 [6144, 8, 64, 64], P(('dom', 'sub'))
Inputs may be any that keep to these rules, and one draw needn't show every extreme that they name: a_cols[i,0] is i; the entries of a row are distinct; each is a fine block row held by the device of row i, by the device with the next or previous dom index and the same sub index, or by the device with the next or previous sub index and the same dom index (indices wrap around). Rows of the device with the next dom index read only rows of aggregate set 6 - 1 of this device, rows of the device with the previous dom index only rows of set 6 - 2, the device with the next sub index only the rows whose prolongator columns lie on it, the device with the previous sub index only rows of sets 0 and 1; set of a row here means its coarse columns' aggregate set. `p_cols`: the 3 entries of a row are distinct coarse block rows of one aggregate set, the rows 4 * j to 4 * j + 3 for some j; they are owned by the device of the fine row, or they are the first 4 coarse rows owned by the device with the next sub index and the same dom index (wrapping around); each device holds 14 fine rows of each of its sets 1 to 5, half of 14 of its set 0, and half of 14 rows of the next sub device's set 0. A row holds 8 distinct coarse block rows: the 4 rows of its own aggregate set, then the 4 rows of one other set; all rows of one aggregate set list the same 8 coarse rows, in any order; for all i, k, p, q the coarse row p_cols[a_cols[i,k], q] appears in row p_cols[i,p] of c_cols.
All inputs are finite; a program needn't handle non-finite values.
Results may differ from a plain program's by a relative error of at most 0.0054.
Values may be sent and summed in bfloat16 or wider, within the bound.
No kernel may reach another device: no remote copies, remote signals or barrier semaphores. Data moves between devices by JAX's collectives and lax.ppermute only.
A program may use at most 256 MiB of HBM per device.

v0:
```python
import jax
import jax.numpy as jnp
from jax import lax
from jax.sharding import PartitionSpec as P

KG = 4
FS = 14


def passed_along(block, axis, distance):
    devices = range(lax.axis_size(axis))
    route = [((i - distance) % len(devices), i) for i in devices]
    return lax.ppermute(block, axis, route)


def locate(a_cols, row_base, rows_here, remote_ids, pool_c):
    inside = (a_cols >= row_base) & (a_cols < row_base + rows_here)
    local_index = jnp.clip(a_cols - row_base, 0, rows_here - 1)
    found = a_cols[:, :, None] == remote_ids[None, None, :]
    slot_pos = jnp.sum(
        jnp.where(found, jnp.arange(remote_ids.shape[0], dtype=jnp.int32), 0), axis=-1
    )
    source_rows = jnp.where(inside, local_index, rows_here + slot_pos)
    return (source_rows, pool_c[source_rows])


def pick_rows(mask, count):
    return jnp.nonzero(mask, size=count, fill_value=0)[0].astype(jnp.int32)


def partial_sums(a_rows, p_rows, targets, pool_p, source_rows, col_coarse, pattern, out_rows):
    rows_here = a_rows.shape[0]
    block_width = a_rows.shape[-1]
    prolong_count = pool_p.shape[1]
    slots = pattern.shape[2]
    block_rows = rows_here // 4
    pool_flat = pool_p.reshape((-1, block_width, block_width))
    pool_flat = jnp.concatenate(
        [pool_flat, jnp.zeros((1, block_width, block_width), pool_flat.dtype)], axis=0
    )
    blank = pool_flat.shape[0] - 1
    leading = pattern[:, 0, :]
    hits = col_coarse[:, :, :, None] == leading[:, None, None, :]
    choose = jnp.sum(
        jnp.where(hits, jnp.arange(prolong_count, dtype=jnp.int32)[None, None, :, None] + 1, 0),
        axis=2,
    )
    picks = jnp.where(
        choose > 0, source_rows[:, :, None] * prolong_count + choose - 1, blank
    ).astype(jnp.int32)
    same = pattern[:, :, :, None] == leading[:, None, None, :]
    slot_of = jnp.sum(
        jnp.where(same, jnp.arange(slots, dtype=jnp.int32)[None, None, :, None], 0), axis=2
    )
    flat_target = targets[:, :, None] * slots + slot_of
    running = jnp.zeros((out_rows * slots, block_width, block_width), jnp.float32)
    for quarter in range(4):
        first_row = quarter * block_rows
        last_row = first_row + block_rows
        selected = pool_flat[picks[first_row:last_row]]
        merged = jnp.einsum(
            "ikab,ikubc->iuac",
            a_rows[first_row:last_row],
            selected,
            preferred_element_type=jnp.float32,
        ).astype(jnp.bfloat16)
        coarse_terms = jnp.einsum(
            "ipab,iuac->ipubc",
            p_rows[first_row:last_row],
            merged,
            preferred_element_type=jnp.float32,
        )
        running = running.at[flat_target[first_row:last_row].reshape(-1)].add(
            coarse_terms.reshape((-1, block_width, block_width))
        )
    return running.reshape((out_rows, slots, block_width, block_width))


def shards(a_blocks, a_cols, p_blocks, p_cols, c_cols):
    rows_here = a_cols.shape[0]
    coarse_here = c_cols.shape[0]
    sets_here = coarse_here // KG
    sub_count = lax.axis_size("sub")
    dom_index = lax.axis_index("dom")
    sub_index = lax.axis_index("sub")
    device = dom_index * sub_count + sub_index
    row_base = device * rows_here
    coarse_base = device * coarse_here
    next_base = (dom_index * sub_count + (sub_index + 1) % sub_count) * coarse_here
    half = FS // 2
    lead_col = p_cols[:, 0] - coarse_base
    owns_row = (lead_col >= 0) & (lead_col < coarse_here)
    set_of = jnp.where(owns_row, lead_col // KG, -1)
    up_rows = pick_rows(set_of == sets_here - 1, FS)
    down_rows = pick_rows(set_of == sets_here - 2, FS)
    fore_rows = pick_rows(jnp.logical_not(owns_row), half)
    back_rows = pick_rows((set_of == 0) | (set_of == 1), FS + half)
    up_ids = up_rows + row_base
    down_ids = down_rows + row_base
    fore_ids = fore_rows + row_base
    back_ids = back_rows + row_base
    below = passed_along((p_blocks[up_rows], p_cols[up_rows], up_ids), "dom", 1)
    above = passed_along((p_blocks[down_rows], p_cols[down_rows], down_ids), "dom", -1)
    before = passed_along((p_blocks[fore_rows], p_cols[fore_rows], fore_ids), "sub", 1)
    after = passed_along((p_blocks[back_rows], p_cols[back_rows], back_ids, c_cols[:KG]), "sub", -1)
    pool_p = jnp.concatenate([p_blocks, below[0], above[0], before[0], after[0]], axis=0)
    pool_c = jnp.concatenate([p_cols, below[1], above[1], before[1], after[1]], axis=0)
    remote_ids = jnp.concatenate([below[2], above[2], before[2], after[2]], axis=0)
    source_rows, col_coarse = locate(a_cols, row_base, rows_here, remote_ids, pool_c)
    owned = (p_cols >= coarse_base) & (p_cols < coarse_base + coarse_here)
    targets = jnp.where(owned, p_cols - coarse_base, coarse_here + p_cols - next_base)
    table = jnp.concatenate([c_cols, after[3]], axis=0)
    pattern = table[targets]
    running = partial_sums(
        a_blocks, p_blocks, targets, pool_p, source_rows, col_coarse, pattern, coarse_here + KG
    )
    incoming = passed_along(running[coarse_here:].astype(jnp.bfloat16), "sub", 1).astype(
        jnp.float32
    )
    total = running[:coarse_here].at[:KG].add(incoming)
    return total.astype(jnp.bfloat16)


def solution(mesh):
    in_specs = (
        P(("dom", "sub"), None, None, None),
        P(("dom", "sub"), None),
        P(("dom", "sub"), None, None, None),
        P(("dom", "sub"), None),
        P(("dom", "sub"), None),
    )
    out_specs = P(("dom", "sub"), None, None, None)
    return jax.shard_map(shards, mesh=mesh, in_specs=in_specs, out_specs=out_specs, check_vma=False)
```

profile of v0, /device:TPU:96, one launch (start us, length us, event | category | flops | bytes accessed | tf_op | source)
XLA Modules:
  0.0 810.6 jit_solution(6518801655010305848)
XLA Ops:
  0.0 5.2 collective-permute-start
  5.2 0.7 slice.102
  6.2 8.6 %copy.111 = bf16[84,3,64,64]{3,2,1,0:T(8,128)(2,1)} copy(bf16[84,3,64,64]{0,3,2,1:T(8,128)(2,1)} %param.9) | data formatting | bytes 4128768 | tf_op args[2]
  15.0 1.1 scatter_custom_fusion
  16.4 0.6 fusion.35
  17.0 0.7 fusion.36
  17.9 1.1 scatter_custom_fusion.1
  19.3 1.2 fusion.37
  20.4 3.7 gather_fusion.1
  24.8 3.3 collective-permute-start.5
  28.3 1.1 scatter_custom_fusion.2
  29.6 0.6 fusion.41
  30.9 0.6 fusion.39
  31.6 3.7 gather_fusion.2
  35.8 2.8 gather_fusion.3
  39.4 1.1 scatter_custom_fusion.3
  40.7 0.8 remainder_reduce_fusion
  41.5 3.9 gather_fusion.4
  45.9 0.6 fusion.43
  46.9 0.7 fusion.40
  47.6 21.3 %fusion.53 = (bf16[21,7,64,64]{0,3,2,1:T(8,128)(2,1)}, bf16[21,7,64,64]{0,3,2,1:T(8,128)(2,1)}, bf16[21,7,64,64]{0,3,2,1:T(8,128)(2,1)}, bf16[21,7,64,64]{0,3,2,1:T(8,128)(2,1)}) fusion(bf16[84,7,64,64]{0,3,2,1:T(8,128)(2,1)} %param.7), kind=kLoop, calls=%fused_computation.154 | loop fusion | bytes 9633792 | tf_op jit(solution)/shard_map/slice | solution.py:63
  68.8 8.6 %copy.176 = bf16[21,7,64,64]{3,2,1,0:T(8,128)(2,1)} copy(bf16[21,7,64,64]{0,3,2,1:T(8,128)(2,1)} %get-tuple-element.25) | data formatting | bytes 2408448
  77.4 8.6 %copy.177 = bf16[21,7,64,64]{3,2,1,0:T(8,128)(2,1)} copy(bf16[21,7,64,64]{0,3,2,1:T(8,128)(2,1)} %get-tuple-element.24) | data formatting | bytes 2408448
  86.0 8.6 %copy.178 = bf16[21,7,64,64]{3,2,1,0:T(8,128)(2,1)} copy(bf16[21,7,64,64]{0,3,2,1:T(8,128)(2,1)} %get-tuple-element.23) | data formatting | bytes 2408448
  94.7 8.6 %copy.179 = bf16[21,7,64,64]{3,2,1,0:T(8,128)(2,1)} copy(bf16[21,7,64,64]{0,3,2,1:T(8,128)(2,1)} %get-tuple-element.22) | data formatting | bytes 2408448
  103.8 5.3 collective-permute-start.12
  109.1 1.0 collective-permute-start.6
  111.4 5.6 collective-permute-start.8
  117.2 0.7 gather_fusion
  118.7 0.6 compare_select_fusion.11
  120.3 0.6 compare_select_fusion.9
  121.1 5.3 collective-permute-start.4
  126.7 1.6 gather_fusion.9
  130.0 5.2 collective-permute-done.3
  135.2 3.9 copy.118
  139.1 4.1 copy.116
  143.2 4.1 copy.117
  147.3 2.1 collective-permute-done.4
  149.4 4.3 copy.119
  153.7 17.8 %concatenate.18 = bf16[140,3,64,64]{0,3,2,1:T(8,128)(2,1)} concatenate(bf16[84,3,64,64]{0,3,2,1:T(8,128)(2,1)S(1)} %copy-done, bf16[14,3,64,64]{0,3,2,1:T(8,128)(2,1)} %copy.116, bf16[14,3,64,64]{0,3,2,1:T(8,128)(2,1)} %copy.117, bf16[7,3,64,64]{0,3,2,1:T(8,128)(2,1)} %copy.118, bf16[21,3,64,64]{0,3,2,1:T(8,128)(2,1)} %copy.119), dimensions={0} | concatenate | bytes 6881280 | tf_op jit(solution)/shard_map/concatenate | solution.py:106
  171.5 12.1 %copy.120 = bf16[140,3,64,64]{3,2,1,0:T(8,128)(2,1)} copy(bf16[140,3,64,64]{0,3,2,1:T(8,128)(2,1)} %concatenate.18) | data formatting | bytes 6881280 | tf_op jit(solution)/shard_map/concatenate | solution.py:106
  183.6 7.5 concatenate.19
  191.2 35.6 %gather_fusion.10 = bf16[1176,64,64]{2,1,0:T(8,128)(2,1)} fusion(bf16[421,64,64]{2,1,0:T(8,128)(2,1)} %concatenate.19, s32[2048]{0:T(1024)S(1)} %pad_clamp_fusion.3), kind=kCustom, calls=%fused_computation.10 | custom fusion | bytes 19272288 | tf_op jit(solution)/shard_map/gather | solution.py:60
  226.8 17.5 %convolution_bitcast_fusion.3 = f32[21,3,8,64,64]{3,4,1,2,0:T(8,128)} fusion(bf16[21,7,8,64,64]{4,3,2,1,0:T(8,128)(2,1)} %bitcast.167, bf16[21,7,64,64]{3,2,1,0:T(8,128)(2,1)S(1)} %copy-done.4, bf16[84,3,64,64]{3,2,1,0:T(8,128)(2,1)} %copy.111), kind=kOutput, calls=%fused_computation.25 | convolution fusion | flops 881491968 | bytes 29761536 | tf_op jit(solution)/shard_map/ipab,iuac->ipubc/dot_general | solution.py:67
  244.3 17.1 %copy.133 = f32[21,3,8,64,64]{4,3,2,1,0:T(8,128)} copy(f32[21,3,8,64,64]{3,4,1,2,0:T(8,128)} %convolution_bitcast_fusion.3) | data formatting | bytes 16515072 | tf_op jit(solution)/shard_map/ipab,iuac->ipubc/transpose | solution.py:67
  261.3 35.6 %gather_fusion.11 = bf16[1176,64,64]{2,1,0:T(8,128)(2,1)} fusion(bf16[421,64,64]{2,1,0:T(8,128)(2,1)} %concatenate.19, s32[2048]{0:T(1024)S(1)} %pad_clamp_fusion.2), kind=kCustom, calls=%fused_computation.11 | custom fusion | bytes 19272288 | tf_op jit(solution)/shard_map/gather | solution.py:60
  296.9 17.6 %convolution_bitcast_fusion.2 = f32[21,3,8,64,64]{3,4,1,2,0:T(8,128)} fusion(bf16[21,7,8,64,64]{4,3,2,1,0:T(8,128)(2,1)} %bitcast.168, bf16[21,7,64,64]{3,2,1,0:T(8,128)(2,1)S(1)} %copy-done.3, bf16[84,3,64,64]{3,2,1,0:T(8,128)(2,1)} %copy.111), kind=kOutput, calls=%fused_computation.24 | convolution fusion | flops 881491968 | bytes 29761536 | tf_op jit(solution)/shard_map/ipab,iuac->ipubc/dot_general | solution.py:67
  314.5 17.0 %copy.139 = f32[21,3,8,64,64]{4,3,2,1,0:T(8,128)} copy(f32[21,3,8,64,64]{3,4,1,2,0:T(8,128)} %convolution_bitcast_fusion.2) | data formatting | bytes 16515072 | tf_op jit(solution)/shard_map/ipab,iuac->ipubc/transpose | solution.py:67
  331.6 35.6 %gather_fusion.12 = bf16[1176,64,64]{2,1,0:T(8,128)(2,1)} fusion(bf16[421,64,64]{2,1,0:T(8,128)(2,1)} %concatenate.19, s32[2048]{0:T(1024)S(1)} %pad_clamp_fusion.1), kind=kCustom, calls=%fused_computation.12 | custom fusion | bytes 19272288 | tf_op jit(solution)/shard_map/gather | solution.py:60
  367.2 17.7 %convolution_bitcast_fusion.1 = f32[21,3,8,64,64]{3,4,1,2,0:T(8,128)} fusion(bf16[21,7,8,64,64]{4,3,2,1,0:T(8,128)(2,1)} %bitcast.169, bf16[21,7,64,64]{3,2,1,0:T(8,128)(2,1)S(1)} %copy-done.2, bf16[84,3,64,64]{3,2,1,0:T(8,128)(2,1)} %copy.111), kind=kOutput, calls=%fused_computation.23 | convolution fusion | flops 881491968 | bytes 29761536 | tf_op jit(solution)/shard_map/ipab,iuac->ipubc/dot_general | solution.py:67
  384.9 17.0 %copy.145 = f32[21,3,8,64,64]{4,3,2,1,0:T(8,128)} copy(f32[21,3,8,64,64]{3,4,1,2,0:T(8,128)} %convolution_bitcast_fusion.1) | data formatting | bytes 16515072 | tf_op jit(solution)/shard_map/ipab,iuac->ipubc/transpose | solution.py:67
  401.9 35.6 %gather_fusion.13 = bf16[1176,64,64]{2,1,0:T(8,128)(2,1)} fusion(bf16[421,64,64]{2,1,0:T(8,128)(2,1)} %concatenate.19, s32[2048]{0:T(1024)S(1)} %pad_clamp_fusion), kind=kCustom, calls=%fused_computation.13 | custom fusion | bytes 19272288 | tf_op jit(solution)/shard_map/gather | solution.py:60
  437.5 17.5 %convolution_bitcast_fusion = f32[21,3,8,64,64]{3,4,1,2,0:T(8,128)} fusion(bf16[21,7,8,64,64]{4,3,2,1,0:T(8,128)(2,1)} %bitcast.166, bf16[21,7,64,64]{3,2,1,0:T(8,128)(2,1)S(1)} %copy-done.1, bf16[84,3,64,64]{3,2,1,0:T(8,128)(2,1)} %copy.111), kind=kOutput, calls=%fused_computation.22 | convolution fusion | flops 881491968 | bytes 29761536 | tf_op jit(solution)/shard_map/ipab,iuac->ipubc/dot_general | solution.py:67
  455.0 17.1 %copy.151 = f32[21,3,8,64,64]{4,3,2,1,0:T(8,128)} copy(f32[21,3,8,64,64]{3,4,1,2,0:T(8,128)} %convolution_bitcast_fusion) | data formatting | bytes 16515072 | tf_op jit(solution)/shard_map/ipab,iuac->ipubc/transpose | solution.py:67
  472.1 3.9 broadcast_in_dim.115
  475.9 78.8 %scatter_fusion = f32[224,64,64]{2,1,0:T(8,128)} fusion(f32[224,64,64]{2,1,0:T(8,128)} %broadcast_in_dim.115, s32[504]{0:T(512)S(1)} %bitcast.180, f32[504,64,64]{2,1,0:T(8,128)} %bitcast.170), kind=kCustom, calls=%fused_computation.18 | custom fusion | flops 2064384 | bytes 24774624 | tf_op jit(solution)/shard_map/scatter-add | solution.py:73
  554.7 78.8 %scatter_fusion.1 = f32[224,64,64]{2,1,0:T(8,128)} fusion(f32[224,64,64]{2,1,0:T(8,128)} %scatter_fusion, s32[504]{0:T(512)S(1)} %bitcast.181, f32[504,64,64]{2,1,0:T(8,128)} %bitcast.171), kind=kCustom, calls=%fused_computation.19 | custom fusion | flops 2064384 | bytes 24774624 | tf_op jit(solution)/shard_map/scatter-add | solution.py:73
  633.5 78.7 %scatter_fusion.2 = f32[224,64,64]{2,1,0:T(8,128)} fusion(f32[224,64,64]{2,1,0:T(8,128)} %scatter_fusion.1, s32[504]{0:T(512)S(1)} %bitcast.182, f32[504,64,64]{2,1,0:T(8,128)} %bitcast.172), kind=kCustom, calls=%fused_computation.20 | custom fusion | flops 2064384 | bytes 24774624 | tf_op jit(solution)/shard_map/scatter-add | solution.py:73
  712.2 78.7 %scatter_fusion.3 = f32[224,64,64]{2,1,0:T(8,128)} fusion(f32[224,64,64]{2,1,0:T(8,128)} %scatter_fusion.2, s32[504]{0:T(512)S(1)} %bitcast.183, f32[504,64,64]{2,1,0:T(8,128)} %bitcast.173), kind=kCustom, calls=%fused_computation.21 | custom fusion | flops 2064384 | bytes 24774624 | tf_op jit(solution)/shard_map/scatter-add | solution.py:73
  790.9 1.3 slice.179
  792.3 5.3 slice.163
  797.6 1.3 slice.164
  798.9 10.6 %collective-permute-done.13 = bf16[4,8,64,64]{3,2,1,0:T(8,128)(2,1)S(1)} collective-permute-done((bf16[4,8,64,64]{3,2,1,0:T(8,128)(2,1)S(1)}, bf16[4,8,64,64]{3,2,1,0:T(8,128)(2,1)S(1)}, u32[]{:S(2)}, u32[]{:S(2)}) %collective-permute-start.13) | collective-permute-done | bytes 262176 | tf_op jit(solution)/shard_map/ppermute | solution.py:13
  809.5 1.0 add_dynamic-update-slice_fusion
  (117 shorter events, 11.0 us)
Async XLA Ops:
  0.0 24.1 %copy-start.9 = (s32[84,3]{0,1:T(4,128)S(1)}, s32[84,3]{0,1:T(4,128)}, u32[]{:S(2)}) copy-start(s32[84,3]{0,1:T(4,128)} %param.10) | copy-start | bytes 3028
  0.0 111.4 %collective-permute-start = (s32[4,8]{0,1:T(8,128)}, s32[4,8]{0,1:T(8,128)S(1)}, u32[]{:S(2)}, u32[]{:S(2)}) collective-permute-start(s32[4,8]{0,1:T(8,128)} %bitcast.184), channel_id=1, source_target_pairs={{1,0},{2,1},{3,2},{4,3},{5,4},{6,5},{7,6},{8,7},{9,8},{10,9},{11,1... | collective-permute-start | bytes 392 | tf_op jit(solution)/shard_map/ppermute | solution.py:13
  24.1 114.9 %collective-permute-start.1 = (bf16[14,3,64,64]{3,2,1,0:T(8,128)(2,1)}, bf16[14,3,64,64]{3,2,1,0:T(8,128)(2,1)}, u32[]{:S(2)}, u32[]{:S(2)}) collective-permute-start(bf16[14,3,64,64]{3,2,1,0:T(8,128)(2,1)} %gather_fusion.1), channel_id=1, source_target_pairs={{240,0},{0,16},{16,32},{32,48},{48,64},{64,80},{80,96},{96,112},{1... | collective-permute-start | bytes 1032200 | tf_op jit(solution)/shard_map/ppermute | solution.py:13
  24.8 96.2 %collective-permute-start.5 = (s32[14,3]{1,0:T(8,128)S(1)}, s32[14,3]{1,0:T(8,128)S(1)}, u32[]{:S(2)}, u32[]{:S(2)}) collective-permute-start(s32[14,3]{1,0:T(8,128)S(1)} %gather_fusion.5), channel_id=1, source_target_pairs={{240,0},{0,16},{16,32},{32,48},{48,64},{64,80},{80,96},{96,112},{1... | collective-permute-start | bytes 512 | tf_op jit(solution)/shard_map/ppermute | solution.py:13
  30.2 73.1 %collective-permute-start.11 = (s32[7]{0:T(128)S(1)}, s32[7]{0:T(128)S(1)}, u32[]{:S(2)}, u32[]{:S(2)}) collective-permute-start(s32[7]{0:T(128)S(1)} %fusion.41), channel_id=1, source_target_pairs={{15,0},{0,1},{1,2},{2,3},{3,4},{4,5},{5,6},{6,7},{7,8},{8,9},{9,10... | collective-permute-start | bytes 92 | tf_op jit(solution)/shard_map/ppermute | solution.py:13
  30.9 72.9 %collective-permute-start.10 = (s32[14]{0:T(128)S(1)}, s32[14]{0:T(128)S(1)}, u32[]{:S(2)}, u32[]{:S(2)}) collective-permute-start(s32[14]{0:T(128)S(1)} %fusion.42), channel_id=1, source_target_pairs={{16,0},{32,16},{48,32},{64,48},{80,64},{96,80},{112,96},{128,112},... | collective-permute-start | bytes 176 | tf_op jit(solution)/shard_map/ppermute | solution.py:13
  86.0 24.9 %copy-start.5 = (s32[84,7]{0,1:T(8,128)S(1)}, s32[84,7]{0,1:T(8,128)}, u32[]{:S(2)}) copy-start(s32[84,7]{0,1:T(8,128)} %param.8) | copy-start | bytes 7060
  94.7 22.4 %copy-start.10 = (s32[24,8]{0,1:T(8,128)S(1)}, s32[24,8]{0,1:T(8,128)}, u32[]{:S(2)}) copy-start(s32[24,8]{0,1:T(8,128)} %param.11) | copy-start | bytes 2308
  103.3 5.8 collective-permute-start.9
  103.8 6.6 collective-permute-start.12
  109.1 11.9 %collective-permute-start.6 = (s32[14,3]{1,0:T(8,128)S(1)}, s32[14,3]{1,0:T(8,128)S(1)}, u32[]{:S(2)}, u32[]{:S(2)}) collective-permute-start(s32[14,3]{1,0:T(8,128)S(1)} %gather_fusion.6), channel_id=1, source_target_pairs={{16,0},{32,16},{48,32},{64,48},{80,64},{96,80},{112,96},{128,112},... | collective-permute-start | bytes 512 | tf_op jit(solution)/shard_map/ppermute | solution.py:13
  110.4 10.5 %collective-permute-start.7 = (s32[7,3]{1,0:T(8,128)S(1)}, s32[7,3]{1,0:T(8,128)S(1)}, u32[]{:S(2)}, u32[]{:S(2)}) collective-permute-start(s32[7,3]{1,0:T(8,128)S(1)} %gather_fusion.7), channel_id=1, source_target_pairs={{15,0},{0,1},{1,2},{2,3},{3,4},{4,5},{5,6},{6,7},{7,8},{8,9},{9,10... | collective-permute-start | bytes 260 | tf_op jit(solution)/shard_map/ppermute | solution.py:13
  111.4 15.0 %collective-permute-start.8 = (s32[21,3]{1,0:T(8,128)S(1)}, s32[21,3]{1,0:T(8,128)S(1)}, u32[]{:S(2)}, u32[]{:S(2)}) collective-permute-start(s32[21,3]{1,0:T(8,128)S(1)} %gather_fusion.8), channel_id=1, source_target_pairs={{1,0},{2,1},{3,2},{4,3},{5,4},{6,5},{7,6},{8,7},{9,8},{10,9},{11,1... | collective-permute-start | bytes 764 | tf_op jit(solution)/shard_map/ppermute | solution.py:13
  121.0 22.2 %collective-permute-start.2 = (bf16[14,3,64,64]{3,2,1,0:T(8,128)(2,1)}, bf16[14,3,64,64]{3,2,1,0:T(8,128)(2,1)}, u32[]{:S(2)}, u32[]{:S(2)}) collective-permute-start(bf16[14,3,64,64]{3,2,1,0:T(8,128)(2,1)} %gather_fusion.2), channel_id=1, source_target_pairs={{16,0},{32,16},{48,32},{64,48},{80,64},{96,80},{112,96},{128,112},... | collective-permute-start | bytes 1032200 | tf_op jit(solution)/shard_map/ppermute | solution.py:13
  121.0 14.2 %collective-permute-start.3 = (bf16[7,3,64,64]{3,2,1,0:T(8,128)(2,1)S(1)}, bf16[7,3,64,64]{3,2,1,0:T(8,128)(2,1)}, u32[]{:S(2)}, u32[]{:S(2)}) collective-permute-start(bf16[7,3,64,64]{3,2,1,0:T(8,128)(2,1)S(1)} %gather_fusion.3), channel_id=1, source_target_pairs={{15,0},{0,1},{1,2},{2,3},{3,4},{4,5},{5,6},{6,7},{7,8},{8,9},{9,10... | collective-permute-start | bytes 516104 | tf_op jit(solution)/shard_map/ppermute | solution.py:13
  121.1 28.3 %collective-permute-start.4 = (bf16[21,3,64,64]{3,2,1,0:T(8,128)(2,1)}, bf16[21,3,64,64]{3,2,1,0:T(8,128)(2,1)}, u32[]{:S(2)}, u32[]{:S(2)}) collective-permute-start(bf16[21,3,64,64]{3,2,1,0:T(8,128)(2,1)} %gather_fusion.4), channel_id=1, source_target_pairs={{1,0},{2,1},{3,2},{4,3},{5,4},{6,5},{7,6},{8,7},{9,8},{10,9},{11,1... | collective-permute-start | bytes 1548296 | tf_op jit(solution)/shard_map/ppermute | solution.py:13
  130.0 23.7 %copy-start = (bf16[84,3,64,64]{0,3,2,1:T(8,128)(2,1)S(1)}, bf16[84,3,64,64]{0,3,2,1:T(8,128)(2,1)}, u32[]{:S(2)}) copy-start(bf16[84,3,64,64]{0,3,2,1:T(8,128)(2,1)} %param.9) | copy-start | bytes 6193156
  191.2 35.6 %copy-start.4 = (bf16[21,7,64,64]{3,2,1,0:T(8,128)(2,1)S(1)}, bf16[21,7,64,64]{3,2,1,0:T(8,128)(2,1)}, u32[]{:S(2)}) copy-start(bf16[21,7,64,64]{3,2,1,0:T(8,128)(2,1)} %copy.176) | copy-start | bytes 3612676
  261.3 35.6 %copy-start.3 = (bf16[21,7,64,64]{3,2,1,0:T(8,128)(2,1)S(1)}, bf16[21,7,64,64]{3,2,1,0:T(8,128)(2,1)}, u32[]{:S(2)}) copy-start(bf16[21,7,64,64]{3,2,1,0:T(8,128)(2,1)} %copy.177) | copy-start | bytes 3612676
  331.6 35.6 %copy-start.2 = (bf16[21,7,64,64]{3,2,1,0:T(8,128)(2,1)S(1)}, bf16[21,7,64,64]{3,2,1,0:T(8,128)(2,1)}, u32[]{:S(2)}) copy-start(bf16[21,7,64,64]{3,2,1,0:T(8,128)(2,1)} %copy.178) | copy-start | bytes 3612676
  401.9 35.6 %copy-start.1 = (bf16[21,7,64,64]{3,2,1,0:T(8,128)(2,1)S(1)}, bf16[21,7,64,64]{3,2,1,0:T(8,128)(2,1)}, u32[]{:S(2)}) copy-start(bf16[21,7,64,64]{3,2,1,0:T(8,128)(2,1)} %copy.179) | copy-start | bytes 3612676
  475.9 78.8 %copy-start.6 = (s32[504,1]{0,1:T(1,128)S(1)}, s32[504,1]{0,1:T(1,128)}, u32[]{:S(2)}) copy-start(s32[504,1]{0,1:T(1,128)} %compare_select_fusion.11) | copy-start | bytes 6052
  554.7 78.8 %copy-start.7 = (s32[504,1]{0,1:T(1,128)S(1)}, s32[504,1]{0,1:T(1,128)}, u32[]{:S(2)}) copy-start(s32[504,1]{0,1:T(1,128)} %compare_select_fusion.10) | copy-start | bytes 6052
  633.5 78.7 %copy-start.8 = (s32[504,1]{0,1:T(1,128)S(1)}, s32[504,1]{0,1:T(1,128)}, u32[]{:S(2)}) copy-start(s32[504,1]{0,1:T(1,128)} %compare_select_fusion.9) | copy-start | bytes 6052
  792.2 17.3 %collective-permute-start.13 = (bf16[4,8,64,64]{3,2,1,0:T(8,128)(2,1)S(1)}, bf16[4,8,64,64]{3,2,1,0:T(8,128)(2,1)S(1)}, u32[]{:S(2)}, u32[]{:S(2)}) collective-permute-start(bf16[4,8,64,64]{3,2,1,0:T(8,128)(2,1)S(1)} %bitcast.177), channel_id=1, source_target_pairs={{15,0},{0,1},{1,2},{2,3},{3,4},{4,5},{5,6},{6,7},{7,8},{8,9},{9,10... | collective-permute-start | bytes 786440 | tf_op jit(solution)/shard_map/ppermute | solution.py:13
where the time goes:
time: 826 us; the launch traced here: 811 us
  local copies, waits for them, and re-layouts  364 us (44%)
  other arithmetic  331 us (40%)
  matrix products  70.3 us (9%)
  starting transfers between devices  26.9 us (3%)
  waiting for transfers between devices  18.2 us (2%)
    scatter-add x4, other arithmetic, partial_sums(): running.at[flat_target[first_row:last_row].reshape(-1)]  315 us
    gather x4, local copies, waits for them, and re-layouts, partial_sums(): selected = pool_flat[picks[first_row:last_row]]  142 us
    dot_general x4, matrix products, partial_sums(): jnp.einsum('ipab,iuac->ipubc', p_rows[first_row:last_row], merged, prefer...  70.3 us
    transpose x4, local copies, waits for them, and re-layouts, partial_sums(): jnp.einsum('ipab,iuac->ipubc', p_rows[first_row:last_row], merged, prefer...  68.2 us
    unnamed x28, local copies, waits for them, and re-layouts  43.2 us
    concatenate x2, local copies, waits for them, and re-layouts, shards(): jnp.concatenate([p_blocks, below[0], above[0], before[0], after[0]], axis=0)  29.9 us
    ppermute x14, starting transfers between devices, passed_along(): return lax.ppermute(block, axis, route)  26.9 us
    slice x1, local copies, waits for them, and re-layouts, partial_sums(): a_rows[first_row:last_row]  21.3 us
  transfers between devices with their start and end apart: 14, of which 4 were waited for; matrix products, arithmetic and copies ran while one was open for 15% of the time, Pallas kernels for 0%

commit v1 on v0

v1 whole, which is shorter than its diff:
```python
import functools

import jax
import jax.numpy as jnp
from jax import lax
from jax.experimental import pallas as pl
from jax.experimental.pallas import tpu as pltpu
from jax.sharding import PartitionSpec as P

KG = 4
FS = 14
HALF = FS // 2
ROWS = 84
PAD = 88
SETS = 6
B = 64
POOL = ROWS + FS + FS + HALF + HALF + FS
F32 = jnp.float32
BF16 = jnp.bfloat16
VMEM_BYTES = 56 * 1024 * 1024


def passed_along(block, axis, distance):
    n = lax.axis_size(axis)
    return lax.ppermute(block, axis, [((i - distance) % n, i) for i in range(n)])


def iota(shape, dim):
    return lax.broadcasted_iota(jnp.int32, shape, dim)


def ranks(lead, set_base):
    group = (lead >> 2) - set_base
    own = (group >= 0) & (group < SETS)
    key = jnp.where(own, jnp.where(group > 0, group + 1, 0), 1)
    order = (key * 128 + iota((1, ROWS), 1)).astype(F32)
    wide = jnp.broadcast_to(order, (ROWS, ROWS))
    diagonal = iota((ROWS, ROWS), 0) == iota((ROWS, ROWS), 1)
    column = jnp.sum(jnp.where(diagonal, wide, 0.0), axis=1, keepdims=True)
    return jnp.sum(jnp.where(column < wide, 1.0, 0.0), axis=0, keepdims=True)


def selector(rank):
    return jnp.where(rank.astype(jnp.int32) == iota((PAD, ROWS), 0), 1.0, 0.0).astype(BF16)


def nt(x, y):
    return lax.dot_general(x, y, (((1,), (1,)), ((), ())), preferred_element_type=F32)


def prolong_kernel(base_ref, cols_ref, p_ref, pool_ref, up_ref, down_ref, fore_ref, back_ref,
                   sel_out_ref, sel_ref, t0_ref, t1_ref):
    @pl.when(pl.program_id(0) == 0)
    def _():
        sel = selector(ranks(cols_ref[0:1, :], base_ref[0]))
        sel_ref[...] = sel
        sel_out_ref[...] = sel

    sel = sel_ref[...]
    place = cols_ref[...] & 3
    weights = [
        [jnp.where(place[q:q + 1, :] == r, 1.0, 0.0).astype(BF16) for q in range(3)]
        for r in range(KG)
    ]
    chunk = p_ref.shape[1]
    for b in range(chunk):
        x = [p_ref[q, b] for q in range(3)]
        y = [x[0] * w[0] + x[1] * w[1] + x[2] * w[2] for w in weights]
        t = nt(sel, jnp.concatenate(y, axis=0))
        t0_ref[b * PAD:(b + 1) * PAD, :] = t[:, :128]
        t1_ref[b * PAD:(b + 1) * PAD, :] = t[:, 128:]
    for i in range(ROWS):
        v = jnp.concatenate(
            [t_ref[pl.ds(i, chunk, stride=PAD), :] for t_ref in (t0_ref, t1_ref)], axis=1
        ).astype(BF16)
        pool_ref[i] = v
        if i >= 70:
            up_ref[i - 70] = v
        elif i >= 56:
            down_ref[i - 56] = v
        elif 7 <= i < 14:
            fore_ref[i - 7] = v
        elif i < 7:
            back_ref[i] = v
        elif i < 28:
            back_ref[i - 7] = v


def prolong(base, cols_t, p_t):
    steps = 4
    chunk = B // steps

    def rows(n):
        return pl.BlockSpec((n, chunk, 4 * B), lambda g: (0, g, 0))

    def shape(n):
        return jax.ShapeDtypeStruct((n, B, 4 * B), BF16)

    return pl.pallas_call(
        prolong_kernel,
        grid=(steps,),
        in_specs=[
            pl.BlockSpec(memory_space=pltpu.SMEM),
            pl.BlockSpec((3, ROWS), lambda g: (0, 0)),
            pl.BlockSpec((3, chunk, B, ROWS), lambda g: (0, g, 0, 0)),
        ],
        out_specs=[rows(84), rows(14), rows(14), rows(7), rows(21),
                   pl.BlockSpec((PAD, ROWS), lambda g: (0, 0))],
        out_shape=[shape(84), shape(14), shape(14), shape(7), shape(21),
                   jax.ShapeDtypeStruct((PAD, ROWS), BF16)],
        scratch_shapes=[
            pltpu.VMEM((PAD, ROWS), BF16),
            pltpu.VMEM((chunk * PAD, 128), F32),
            pltpu.VMEM((chunk * PAD, 128), F32),
        ],
        compiler_params=pltpu.CompilerParams(vmem_limit_bytes=VMEM_BYTES),
        cost_estimate=pl.CostEstimate(flops=400_000_000, bytes_accessed=8_000_000, transcendentals=0),
        name="prolong",
    )(base, cols_t, p_t)


def operator_kernel(sel_ref, a_ref, out_ref, *t_refs):
    sel = sel_ref[...]
    chunk = a_ref.shape[1]
    for a in range(chunk):
        first = jnp.concatenate([a_ref[k, a] for k in range(4)], axis=0)
        zero = jnp.zeros((B, ROWS), BF16)
        last = jnp.concatenate([a_ref[k, a] for k in range(4, 7)] + [zero], axis=0)
        t = [nt(sel, first), nt(sel, last)]
        for h in range(4):
            t_refs[h][a * PAD:(a + 1) * PAD, :] = t[h // 2][:, h % 2 * 128:h % 2 * 128 + 128]
    for i in range(ROWS):
        out_ref[i] = jnp.concatenate(
            [t_ref[pl.ds(i, chunk, stride=PAD), :] for t_ref in t_refs], axis=1
        ).astype(BF16)


def operator(sel, a_t):
    steps = 4
    chunk = B // steps
    return pl.pallas_call(
        operator_kernel,
        grid=(steps,),
        in_specs=[
            pl.BlockSpec((PAD, ROWS), lambda g: (0, 0)),
            pl.BlockSpec((7, chunk, B, ROWS), lambda g: (0, g, 0, 0)),
        ],
        out_specs=pl.BlockSpec((ROWS, chunk, 8 * B), lambda g: (0, g, 0)),
        out_shape=jax.ShapeDtypeStruct((ROWS, B, 8 * B), BF16),
        scratch_shapes=[pltpu.VMEM((chunk * PAD, 128), F32)] * 4,
        compiler_params=pltpu.CompilerParams(vmem_limit_bytes=VMEM_BYTES),
        cost_estimate=pl.CostEstimate(flops=700_000_000, bytes_accessed=13_000_000, transcendentals=0),
        name="operator",
    )(sel, a_t)


def route_kernel(ids_ref, a_cols_ref, own_ref, below_ref, above_ref, before_ref, after_ref,
                 sel_ref, src_ref, mask_ref):
    refs = (own_ref, below_ref, above_ref, before_ref, after_ref)
    rank_rows = [ranks(ref[0:1, :], ids_ref[n] * SETS) for n, ref in enumerate(refs)]
    diagonal = iota((ROWS, ROWS), 0) == iota((ROWS, ROWS), 1)
    after_rank = rank_rows[4]
    rank_rows[1] = rank_rows[1] + (84 - 70)
    rank_rows[2] = rank_rows[2] + (98 - 56)
    rank_rows[3] = rank_rows[3] + (112 - 7)
    rank_rows[4] = after_rank + jnp.where(after_rank < 7, 119.0, 119.0 - 7.0)
    slot_cols = [
        jnp.sum(jnp.where(diagonal, jnp.broadcast_to(r, (ROWS, ROWS)), 0.0), axis=1, keepdims=True)
        for r in rank_rows
    ]
    row = iota((ROWS, ROWS), 0)
    sources = []
    for k in range(7):
        column = a_cols_ref[k:k + 1, :]
        total = jnp.zeros((ROWS, ROWS), F32)
        for n in range(5):
            total = total + jnp.where(column - ids_ref[n] * ROWS == row, slot_cols[n], 0.0)
        sources.append(jnp.sum(total, axis=0, keepdims=True))
    src = jnp.concatenate(sources + [sources[0]], axis=0)

    def set_name(slot):
        name = jnp.where(slot < 7, 0.0, 1.0)
        for start, value in ((14, 2.0), (28, 3.0), (42, 4.0), (56, 5.0), (70, 6.0), (84, 7.0),
                             (98, 8.0), (112, 0.0), (119, 1.0), (126, 9.0)):
            name = jnp.where(slot >= start, value, name)
        return name

    own = jnp.where(set_name(src) == set_name(rank_rows[0]), 1.0, 0.0)
    sel = sel_ref[...]
    src_ref[...] = nt(src.astype(BF16), sel).astype(jnp.int32)
    by_row = nt(sel, own.astype(BF16)).astype(BF16)
    spread = jnp.where(iota((8, 8 * B), 1) >> 6 == iota((8, 8 * B), 0), 1.0, 0.0).astype(BF16)
    mask_ref[...] = jnp.dot(by_row, spread, preferred_element_type=F32)


def route(ids, a_cols_t, cols, sel):
    vmem = pl.BlockSpec(memory_space=pltpu.VMEM)
    return pl.pallas_call(
        route_kernel,
        in_specs=[pl.BlockSpec(memory_space=pltpu.SMEM)] + [vmem] * 7,
        out_specs=[vmem, vmem],
        out_shape=[jax.ShapeDtypeStruct((8, PAD), jnp.int32),
                   jax.ShapeDtypeStruct((PAD, 8 * B), F32)],
        cost_estimate=pl.CostEstimate(flops=10_000_000, bytes_accessed=300_000, transcendentals=0),
        name="route",
    )(ids, a_cols_t, *cols, sel)


def load_pool(parts, pool_ref, sems):
    copies = []
    start = 0
    for n, part in enumerate(parts):
        copies.append(pltpu.make_async_copy(part, pool_ref.at[pl.ds(start, part.shape[0])], sems.at[n]))
        start += part.shape[0]
    for copy in copies:
        copy.start()
    for copy in copies:
        copy.wait()


def merge_row(i, place, row, src_ref, mask_ref, a_ref, pool_ref, merged_ref):
    index = [src_ref[k, row] for k in range(7)]
    w = jnp.concatenate([pool_ref[j] for j in index] + [pool_ref[index[0]]], axis=0)
    a = a_ref[i]
    mask = jnp.broadcast_to(mask_ref[pl.ds(row, 1), :], a.shape).astype(BF16)
    a_own = a * mask
    both = jnp.concatenate([a_own, a - a_own], axis=0)
    merged = jnp.dot(both, w, preferred_element_type=F32).astype(BF16)
    if isinstance(place, int):
        rows = slice(place * B, place * B + B)
    else:
        rows = pl.ds(pl.multiple_of(place * B, B), B)
    merged_ref[rows, :4 * B] = merged[:B]
    merged_ref[rows, 4 * B:] = merged[B:]


def tn(x, y):
    return lax.dot_general(x, y, (((0,), (0,)), ((), ())), preferred_element_type=F32)


def straddle_kernel(src_ref, mask_ref, a_ref, *refs):
    parts, (out_ref, pool_ref, merged_ref, sems) = refs[:5], refs[5:]
    load_pool(parts, pool_ref, sems)
    for i in range(HALF):
        merge_row(i, i, HALF + i, src_ref, mask_ref, a_ref, pool_ref, merged_ref)
    own = pool_ref[HALF:FS].reshape(HALF * B, KG * B)
    out_ref[...] = tn(own, merged_ref[...]).astype(BF16)


def straddle(src, mask, a_rows, parts):
    anywhere = pl.BlockSpec(memory_space=pl.ANY)
    return pl.pallas_call(
        straddle_kernel,
        grid=(1,),
        in_specs=[
            pl.BlockSpec(memory_space=pltpu.SMEM),
            pl.BlockSpec((PAD, 8 * B), lambda g: (0, 0)),
            pl.BlockSpec((HALF, B, 8 * B), lambda g: (1, 0, 0)),
        ] + [anywhere] * 5,
        out_specs=pl.BlockSpec((KG * B, 8 * B), lambda g: (0, 0)),
        out_shape=jax.ShapeDtypeStruct((KG * B, 8 * B), BF16),
        scratch_shapes=[
            pltpu.VMEM((POOL, B, KG * B), BF16),
            pltpu.VMEM((HALF * B, 8 * B), BF16),
            pltpu.SemaphoreType.DMA((5,)),
        ],
        compiler_params=pltpu.CompilerParams(vmem_limit_bytes=VMEM_BYTES),
        cost_estimate=pl.CostEstimate(flops=300_000_000, bytes_accessed=6_000_000, transcendentals=0),
        name="straddle",
    )(src, mask, a_rows, *parts)


def order_slots(c_cols_ref, set_id, first_row, place_ref):
    for r in range(KG):
        for s in range(8):
            c = c_cols_ref[s, first_row + r]
            u = (c & 3) + jnp.where((c >> 2) == set_id, 0, 4)
            place_ref[r, u] = s


def store_blocks(total, place_ref, out_ref):
    for r in range(KG):
        for u in range(8):
            block = total[r * B:(r + 1) * B, u * B:(u + 1) * B]
            out_ref[r, place_ref[r, u]] = block.astype(BF16)


def sets_kernel(base_ref, src_ref, c_cols_ref, mask_ref, a_ref, *refs):
    parts, (out_ref, first_ref, pool_ref, merged_ref, place_ref, sems) = refs[:5], refs[5:]
    s = pl.program_id(0)

    @pl.when(s == 0)
    def _():
        load_pool(parts, pool_ref, sems)
        merged_ref[HALF * B:, :] = jnp.zeros((HALF * B, 8 * B), BF16)

    for i in range(HALF):
        merge_row(i, i, s * FS + i, src_ref, mask_ref, a_ref, pool_ref, merged_ref)

    @pl.when(s > 0)
    def _():
        for i in range(HALF, FS):
            merge_row(i, i, s * FS + i, src_ref, mask_ref, a_ref, pool_ref, merged_ref)

    own = pool_ref[pl.ds(s * FS, FS)].reshape(FS * B, KG * B)
    total = tn(own, merged_ref[...])

    @pl.when(s == 0)
    def _():
        first_ref[...] = total

    order_slots(c_cols_ref, base_ref[0] + s, s * KG, place_ref)
    store_blocks(total, place_ref, out_ref)


def sets(base, src, c_cols_t, mask, a_rows, parts):
    anywhere = pl.BlockSpec(memory_space=pl.ANY)
    smem = pl.BlockSpec(memory_space=pltpu.SMEM)
    return pl.pallas_call(
        sets_kernel,
        grid=(SETS,),
        in_specs=[
            smem, smem, smem,
            pl.BlockSpec((PAD, 8 * B), lambda s: (0, 0)),
            pl.BlockSpec((FS, B, 8 * B), lambda s: (s, 0, 0)),
        ] + [anywhere] * 5,
        out_specs=[
            pl.BlockSpec((KG, 8, B, B), lambda s: (s, 0, 0, 0)),
            pl.BlockSpec((KG * B, 8 * B), lambda s: (0, 0)),
        ],
        out_shape=[
            jax.ShapeDtypeStruct((SETS * KG, 8, B, B), BF16),
            jax.ShapeDtypeStruct((KG * B, 8 * B), F32),
        ],
        scratch_shapes=[
            pltpu.VMEM((POOL, B, KG * B), BF16),
            pltpu.VMEM((FS * B, 8 * B), BF16),
            pltpu.SMEM((KG, 8), jnp.int32),
            pltpu.SemaphoreType.DMA((5,)),
        ],
        compiler_params=pltpu.CompilerParams(vmem_limit_bytes=VMEM_BYTES),
        cost_estimate=pl.CostEstimate(flops=4_000_000_000, bytes_accessed=14_000_000, transcendentals=0),
        name="sets",
    )(base, src, c_cols_t, mask, a_rows, *parts)


def finish_kernel(base_ref, c_cols_ref, first_ref, incoming_ref, whole_ref, out_ref, place_ref):
    order_slots(c_cols_ref, base_ref[0], 0, place_ref)
    store_blocks(first_ref[...] + incoming_ref[...].astype(F32), place_ref, out_ref)


def finish(base, c_cols_t, first, incoming, whole):
    smem = pl.BlockSpec(memory_space=pltpu.SMEM)
    return pl.pallas_call(
        finish_kernel,
        grid=(1,),
        in_specs=[
            smem, smem,
            pl.BlockSpec((KG * B, 8 * B), lambda g: (0, 0)),
            pl.BlockSpec((KG * B, 8 * B), lambda g: (0, 0)),
            pl.BlockSpec(memory_space=pl.ANY),
        ],
        out_specs=pl.BlockSpec((KG, 8, B, B), lambda g: (0, 0, 0, 0)),
        out_shape=jax.ShapeDtypeStruct((SETS * KG, 8, B, B), BF16),
        scratch_shapes=[pltpu.SMEM((KG, 8), jnp.int32)],
        input_output_aliases={4: 0},
        compiler_params=pltpu.CompilerParams(vmem_limit_bytes=VMEM_BYTES),
        name="finish",
    )(base, c_cols_t, first, incoming, whole)


def shards(a_blocks, a_cols, p_blocks, p_cols, c_cols):
    dom_count = lax.axis_size("dom")
    sub_count = lax.axis_size("sub")
    dom = lax.axis_index("dom")
    sub = lax.axis_index("sub")
    device = dom * sub_count + sub
    ids = jnp.stack([
        device,
        (dom + dom_count - 1) % dom_count * sub_count + sub,
        (dom + 1) % dom_count * sub_count + sub,
        dom * sub_count + (sub + sub_count - 1) % sub_count,
        dom * sub_count + (sub + 1) % sub_count,
    ]).astype(jnp.int32)
    base = ids[:1] * SETS
    cols_t = p_cols.T
    moves = (("dom", 1), ("dom", -1), ("sub", 1), ("sub", -1))
    cols = [cols_t] + [passed_along(cols_t, axis, step) for axis, step in moves]
    pool, up, down, fore, back, sel = prolong(base, cols_t, p_blocks.transpose(1, 2, 3, 0))
    parts = [pool] + [
        passed_along(rows, axis, step) for rows, (axis, step) in zip((up, down, fore, back), moves)
    ]
    a_rows = operator(sel, a_blocks.transpose(1, 2, 3, 0))
    src, mask = route(ids, a_cols.T, cols, sel)
    partial = straddle(src, mask, a_rows, parts)
    incoming = passed_along(partial, "sub", 1)
    whole, first = sets(base, src, c_cols.T, mask, a_rows, parts)
    return finish(base, c_cols.T, first, incoming, whole)


def solution(mesh):
    spec4 = P(("dom", "sub"), None, None, None)
    spec2 = P(("dom", "sub"), None)
    return jax.shard_map(
        shards, mesh=mesh, in_specs=(spec4, spec2, spec4, spec2, spec2), out_specs=spec4,
        check_vma=False,
    )
```

time: 826 us -> 68.7 us (0.08)
  the two profiles are of different devices: /device:TPU:96 before, /device:TPU:30 now
where the time goes in v1:
time: 68.7 us; the launch traced here: 68.4 us
  Pallas kernels  37.4 us (54%)
  starting transfers between devices  19.7 us (29%)
  waiting for transfers between devices  8.17 us (12%)
  local copies, waits for them, and re-layouts  3.08 us (4%)
    ppermute x9, starting transfers between devices, passed_along(): lax.ppermute(block, axis, [((i - distance) % n, i) for i in range(n)])  19.7 us
    pallas_call x1, Pallas kernels, sets(): pl.pallas_call(sets_kernel, grid=(SETS,), in_specs=[smem, smem, smem, pl....  13.4 us
    pallas_call x1, Pallas kernels, operator(): pl.pallas_call(operator_kernel, grid=(steps,), in_specs=[pl.BlockSpec((PA...  8.42 us
    ppermute x9, waiting for transfers between devices, passed_along(): lax.ppermute(block, axis, [((i - distance) % n, i) for i in range(n)])  8.17 us
    pallas_call x1, Pallas kernels, prolong(): pl.pallas_call(prolong_kernel, grid=(steps,), in_specs=[pl.BlockSpec(memo...  6.4 us
    pallas_call x1, Pallas kernels, straddle(): pl.pallas_call(straddle_kernel, grid=(1,), in_specs=[pl.BlockSpec(memory_...  4.77 us
    unnamed x20, local copies, waits for them, and re-layouts  2.45 us
    pallas_call x1, Pallas kernels, route(): pl.pallas_call(route_kernel, in_specs=[pl.BlockSpec(memory_space=pltpu.SM...  2.22 us
  transfers between devices with their start and end apart: 9, of which 4 were waited for; matrix products, arithmetic and copies ran while one was open for 1% of the time, Pallas kernels for 35%

profile of v1, /device:TPU:30, one launch (start us, length us, event | category | flops | bytes accessed | tf_op | source)
XLA Modules:
  0.0 68.4 jit_solution(5860441477239789805)
XLA Ops:
  0.0 0.0 copy-start.5
  0.0 6.4 %prolong.1 = (bf16[84,64,256]{2,1,0:T(8,128)(2,1)}, bf16[14,64,256]{2,1,0:T(8,128)(2,1)}, bf16[14,64,256]{2,1,0:T(8,128)(2,1)}, bf16[7,64,256]{2,1,0:T(8,128)(2,...) custom-call(s32[1]{0:T(128)S(6)} %mul.15.base_ref, s32[3,84]{1,0:T(4,128)} %bitcast.12, ...), custom_call_target="tpu_custom_call" | custom-call | flops 400000000 | bytes 8000000 | tf_op jit(solution)/shard_map/prolong/pallas_call | solution.py:99
  6.4 0.8 %collective-permute-start.7 = (bf16[21,64,256]{2,1,0:T(8,128)(2,1)}, bf16[21,64,256]{2,1,0:T(8,128)(2,1)S(1)}, u32[]{:S(2)}, u32[]{:S(2)}) collective-permute-start(bf16[21,64,256]{2,1,0:T(8,128)(2,1)} %get-tuple-element.22), channel_id=1, source_target_pairs={{1,0},{2,1},{3,2},{4,3},{5,4},{6,5},{7,6},{8,7},{9,8},{10,9},{11,1... | collective-permute-start | bytes 2064392 | tf_op jit(solution)/shard_map/ppermute | solution.py:25
  7.2 0.0 collective-permute-start.4
  7.2 5.0 %collective-permute-start.5 = (bf16[14,64,256]{2,1,0:T(8,128)(2,1)}, bf16[14,64,256]{2,1,0:T(8,128)(2,1)S(1)}, u32[]{:S(2)}, u32[]{:S(2)}) collective-permute-start(bf16[14,64,256]{2,1,0:T(8,128)(2,1)} %get-tuple-element.20), channel_id=1, source_target_pairs={{16,0},{32,16},{48,32},{64,48},{80,64},{96,80},{112,96},{128,112},... | collective-permute-start | bytes 1376264 | tf_op jit(solution)/shard_map/ppermute | solution.py:25
  12.2 4.6 %collective-permute-start.6 = (bf16[7,64,256]{2,1,0:T(8,128)(2,1)}, bf16[7,64,256]{2,1,0:T(8,128)(2,1)S(1)}, u32[]{:S(2)}, u32[]{:S(2)}) collective-permute-start(bf16[7,64,256]{2,1,0:T(8,128)(2,1)} %get-tuple-element.21), channel_id=1, source_target_pairs={{15,0},{0,1},{1,2},{2,3},{3,4},{4,5},{5,6},{6,7},{7,8},{8,9},{9,10... | collective-permute-start | bytes 688136 | tf_op jit(solution)/shard_map/ppermute | solution.py:25
  16.8 0.0 copy-done.5
  16.8 0.0 collective-permute-start.3
  16.9 8.4 %operator.1.a_ref = bf16[84,64,512]{2,1,0:T(8,128)(2,1)} custom-call(bf16[88,84]{1,0:T(8,128)(2,1)} %get-tuple-element.15.sel_ref, bf16[7,64,64,84]{3,2,1,0:T(8,128)(2,1)} %bitcast.10), custom_call_target="tpu_custom_call" | custom-call | flops 700000000 | bytes 13000000 | tf_op jit(solution)/shard_map/operator/pallas_call | solution.py:141
  25.3 2.0 %collective-permute-done.3.after_ref = s32[3,84]{1,0:T(4,128)S(1)} collective-permute-done((s32[3,84]{1,0:T(4,128)S(1)}, s32[3,84]{1,0:T(4,128)S(1)}, u32[]{:S(2)}, u32[]{:S(2)}) %collective-permute-start.3) | collective-permute-done | bytes 1040 | tf_op jit(solution)/shard_map/ppermute | solution.py:25
  27.2 0.0 copy-start.6
  27.2 3.4 %collective-permute-start.2 = (s32[3,84]{1,0:T(4,128)S(1)}, s32[3,84]{1,0:T(4,128)S(1)}, u32[]{:S(2)}, u32[]{:S(2)}) collective-permute-start(s32[3,84]{1,0:T(4,128)S(1)} %bitcast.15), channel_id=1, source_target_pairs={{15,0},{0,1},{1,2},{2,3},{3,4},{4,5},{5,6},{6,7},{7,8},{8,9},{9,10... | collective-permute-start | bytes 3032 | tf_op jit(solution)/shard_map/ppermute | solution.py:25
  30.6 1.3 %collective-permute-done.2.before_ref = s32[3,84]{1,0:T(4,128)S(1)} collective-permute-done((s32[3,84]{1,0:T(4,128)S(1)}, s32[3,84]{1,0:T(4,128)S(1)}, u32[]{:S(2)}, u32[]{:S(2)}) %collective-permute-start.2) | collective-permute-done | bytes 1040 | tf_op jit(solution)/shard_map/ppermute | solution.py:25
  31.9 0.0 copy-start.7
  31.9 2.2 %collective-permute-start.1 = (s32[3,84]{1,0:T(4,128)S(1)}, s32[3,84]{1,0:T(4,128)S(1)}, u32[]{:S(2)}, u32[]{:S(2)}) collective-permute-start(s32[3,84]{1,0:T(4,128)S(1)} %bitcast.16), channel_id=1, source_target_pairs={{16,0},{32,16},{48,32},{64,48},{80,64},{96,80},{112,96},{128,112},... | collective-permute-start | bytes 3032 | tf_op jit(solution)/shard_map/ppermute | solution.py:25
  34.1 1.3 %collective-permute-done.1.above_ref = s32[3,84]{1,0:T(4,128)S(1)} collective-permute-done((s32[3,84]{1,0:T(4,128)S(1)}, s32[3,84]{1,0:T(4,128)S(1)}, u32[]{:S(2)}, u32[]{:S(2)}) %collective-permute-start.1) | collective-permute-done | bytes 1040 | tf_op jit(solution)/shard_map/ppermute | solution.py:25
  35.4 0.0 copy-start.8
  35.4 0.0 collective-permute-start
  35.4 0.6 stack.23.ids_ref
  36.0 3.6 %collective-permute-done.below_ref = s32[3,84]{1,0:T(4,128)S(1)} collective-permute-done((s32[3,84]{1,0:T(4,128)S(1)}, s32[3,84]{1,0:T(4,128)S(1)}, u32[]{:S(2)}, u32[]{:S(2)}) %collective-permute-start) | collective-permute-done | bytes 1040 | tf_op jit(solution)/shard_map/ppermute | solution.py:25
  39.6 0.0 copy-start.9
  39.6 0.0 copy-done.6
  39.6 0.0 copy-done.7
  39.6 0.0 copy-done.8
  39.6 0.5 copy-done.9
  40.2 2.2 %route.1 = (s32[8,88]{1,0:T(8,128)}, f32[88,512]{1,0:T(8,128)}) custom-call(s32[5]{0:T(128)} %stack.23.ids_ref, s32[7,84]{1,0:T(8,128)} %bitcast.20, s32[3,84]{1,0:T(4,128)} %bitcast.13, s32[3,84]{1,0:T(4,128)} %copy-done.9, s32[3,84]{1,0:T(4,128)} %copy-done.8, s32[3,84]{1,0:T(4,128)} %copy-done.7, s32[3,84]{1,0:T(4,128)} %copy-done.6, ...), custom_call_target="tpu_custom_call" | custom-call | flops 10000000 | bytes 300000 | tf_op jit(solution)/shard_map/route/pallas_call | solution.py:198
  42.4 0.0 collective-permute-done.6.refs_3_
  42.4 0.0 copy-start.4
  42.4 0.0 collective-permute-done.4.refs_1_
  42.4 0.0 copy-start.1
  42.4 0.0 collective-permute-done.5.refs_2_
  42.4 0.0 copy-start.2
  42.4 0.0 collective-permute-done.7.refs_4_
  42.4 0.0 copy-start
  42.5 0.6 copy-done.4
  43.1 0.2 copy-done.1
  43.2 0.1 copy-done.2
  43.4 0.3 copy-done
  43.7 4.8 %straddle.1 = bf16[256,512]{1,0:T(8,128)(2,1)} custom-call(s32[8,88]{1,0:T(8,128)} %get-tuple-element.16.src_ref, f32[88,512]{1,0:T(8,128)} %get-tuple-element.17.mask_ref, bf16[84,64,512]{2,1,0:T(8,128)(2,1)} %operator.1.a_ref, bf16[84,64,256]{2,1,0:T(8,128)(2,1)} %get-tuple-element.18.refs_0_, bf16[14,64,256]{2,1,0:T(8,128)(2,1)} %copy-done.1, ...), custom_call_target="tpu_custom_call" | custom-call | flops 300000000 | bytes 6000000 | tf_op jit(solution)/shard_map/straddle/pallas_call | solution.py:252
  48.4 3.7 %collective-permute-start.8 = (bf16[256,512]{1,0:T(8,128)(2,1)}, bf16[256,512]{1,0:T(8,128)(2,1)S(1)}, u32[]{:S(2)}, u32[]{:S(2)}) collective-permute-start(bf16[256,512]{1,0:T(8,128)(2,1)} %straddle.1), channel_id=1, source_target_pairs={{15,0},{0,1},{1,2},{2,3},{3,4},{4,5},{5,6},{6,7},{7,8},{8,9},{9,10... | collective-permute-start | bytes 786440 | tf_op jit(solution)/shard_map/ppermute | solution.py:25
  52.1 13.4 %sets.1 = (bf16[24,8,64,64]{3,2,1,0:T(8,128)(2,1)}, f32[256,512]{1,0:T(8,128)}) custom-call(s32[1]{0:T(128)S(6)} %mul.15.base_ref, s32[8,88]{1,0:T(8,128)} %get-tuple-element.16.src_ref, s32[8,24]{1,0:T(8,128)} %bitcast.18, f32[88,512]{1,0:T(8,128)} %get-tuple-element.17.mask_ref, bf16[84,64,512]{2,1,0:T(8,128)(2,1)} %operator.1.a_ref, ...), custom_call_target="tpu_custom_call" | custom-call | flops 4000000000 | bytes 14000000 | tf_op jit(solution)/shard_map/sets/pallas_call | solution.py:319
  65.6 0.0 collective-permute-done.8.incoming_ref
  65.6 0.0 copy-start.3
  65.6 0.7 %copy-done.3 = bf16[256,512]{1,0:T(8,128)(2,1)} copy-done((bf16[256,512]{1,0:T(8,128)(2,1)}, bf16[256,512]{1,0:T(8,128)(2,1)S(1)}, u32[]{:S(2)}) %copy-start.3) | copy-done | bytes 262168
  66.3 2.1 %finish.1 = bf16[24,8,64,64]{3,2,1,0:T(8,128)(2,1)} custom-call(s32[1]{0:T(128)S(6)} %mul.15.base_ref, s32[8,24]{1,0:T(8,128)} %bitcast.19, f32[256,512]{1,0:T(8,128)} %get-tuple-element.23.first_ref, bf16[256,512]{1,0:T(8,128)(2,1)} %copy-done.3, bf16[24,8,64,64]{3,2,1,0:T(8,128)(2,1)} %get-tuple-element.24.whole_ref), custom_call_target="tpu_custom_call", output_to_operand_aliasing={{}: (4, {})} | custom-call | tf_op jit(solution)/shard_map/finish/pallas_call | solution.py:354
Async XLA Ops:
  0.0 16.8 %copy-start.5 = (s32[84,3]{0,1:T(4,128)S(1)}, s32[84,3]{0,1:T(4,128)}, u32[]{:S(2)}) copy-start(s32[84,3]{0,1:T(4,128)} %param.8) | copy-start | bytes 3028
  6.4 36.0 %collective-permute-start.7 = (bf16[21,64,256]{2,1,0:T(8,128)(2,1)}, bf16[21,64,256]{2,1,0:T(8,128)(2,1)S(1)}, u32[]{:S(2)}, u32[]{:S(2)}) collective-permute-start(bf16[21,64,256]{2,1,0:T(8,128)(2,1)} %get-tuple-element.22), channel_id=1, source_target_pairs={{1,0},{2,1},{3,2},{4,3},{5,4},{6,5},{7,6},{8,7},{9,8},{10,9},{11,1... | collective-permute-start | bytes 2064392 | tf_op jit(solution)/shard_map/ppermute | solution.py:25
  7.2 35.2 %collective-permute-start.4 = (bf16[14,64,256]{2,1,0:T(8,128)(2,1)}, bf16[14,64,256]{2,1,0:T(8,128)(2,1)S(1)}, u32[]{:S(2)}, u32[]{:S(2)}) collective-permute-start(bf16[14,64,256]{2,1,0:T(8,128)(2,1)} %get-tuple-element.19), channel_id=1, source_target_pairs={{240,0},{0,16},{16,32},{32,48},{48,64},{64,80},{80,96},{96,112},{1... | collective-permute-start | bytes 1376264 | tf_op jit(solution)/shard_map/ppermute | solution.py:25
  7.2 35.2 %collective-permute-start.5 = (bf16[14,64,256]{2,1,0:T(8,128)(2,1)}, bf16[14,64,256]{2,1,0:T(8,128)(2,1)S(1)}, u32[]{:S(2)}, u32[]{:S(2)}) collective-permute-start(bf16[14,64,256]{2,1,0:T(8,128)(2,1)} %get-tuple-element.20), channel_id=1, source_target_pairs={{16,0},{32,16},{48,32},{64,48},{80,64},{96,80},{112,96},{128,112},... | collective-permute-start | bytes 1376264 | tf_op jit(solution)/shard_map/ppermute | solution.py:25
  12.2 30.1 %collective-permute-start.6 = (bf16[7,64,256]{2,1,0:T(8,128)(2,1)}, bf16[7,64,256]{2,1,0:T(8,128)(2,1)S(1)}, u32[]{:S(2)}, u32[]{:S(2)}) collective-permute-start(bf16[7,64,256]{2,1,0:T(8,128)(2,1)} %get-tuple-element.21), channel_id=1, source_target_pairs={{15,0},{0,1},{1,2},{2,3},{3,4},{4,5},{5,6},{6,7},{7,8},{8,9},{9,10... | collective-permute-start | bytes 688136 | tf_op jit(solution)/shard_map/ppermute | solution.py:25
  16.8 10.4 %collective-permute-start.3 = (s32[3,84]{1,0:T(4,128)S(1)}, s32[3,84]{1,0:T(4,128)S(1)}, u32[]{:S(2)}, u32[]{:S(2)}) collective-permute-start(s32[3,84]{1,0:T(4,128)S(1)} %bitcast.14), channel_id=1, source_target_pairs={{1,0},{2,1},{3,2},{4,3},{5,4},{6,5},{7,6},{8,7},{9,8},{10,9},{11,1... | collective-permute-start | bytes 3032 | tf_op jit(solution)/shard_map/ppermute | solution.py:25
  27.2 12.4 %copy-start.6 = (s32[3,84]{1,0:T(4,128)}, s32[3,84]{1,0:T(4,128)S(1)}, u32[]{:S(2)}) copy-start(s32[3,84]{1,0:T(4,128)S(1)} %collective-permute-done.3.after_ref) | copy-start | bytes 3028
  27.2 4.7 %collective-permute-start.2 = (s32[3,84]{1,0:T(4,128)S(1)}, s32[3,84]{1,0:T(4,128)S(1)}, u32[]{:S(2)}, u32[]{:S(2)}) collective-permute-start(s32[3,84]{1,0:T(4,128)S(1)} %bitcast.15), channel_id=1, source_target_pairs={{15,0},{0,1},{1,2},{2,3},{3,4},{4,5},{5,6},{6,7},{7,8},{8,9},{9,10... | collective-permute-start | bytes 3032 | tf_op jit(solution)/shard_map/ppermute | solution.py:25
  31.9 7.7 %copy-start.7 = (s32[3,84]{1,0:T(4,128)}, s32[3,84]{1,0:T(4,128)S(1)}, u32[]{:S(2)}) copy-start(s32[3,84]{1,0:T(4,128)S(1)} %collective-permute-done.2.before_ref) | copy-start | bytes 3028
  31.9 3.5 %collective-permute-start.1 = (s32[3,84]{1,0:T(4,128)S(1)}, s32[3,84]{1,0:T(4,128)S(1)}, u32[]{:S(2)}, u32[]{:S(2)}) collective-permute-start(s32[3,84]{1,0:T(4,128)S(1)} %bitcast.16), channel_id=1, source_target_pairs={{16,0},{32,16},{48,32},{64,48},{80,64},{96,80},{112,96},{128,112},... | collective-permute-start | bytes 3032 | tf_op jit(solution)/shard_map/ppermute | solution.py:25
  35.4 4.2 %copy-start.8 = (s32[3,84]{1,0:T(4,128)}, s32[3,84]{1,0:T(4,128)S(1)}, u32[]{:S(2)}) copy-start(s32[3,84]{1,0:T(4,128)S(1)} %collective-permute-done.1.above_ref) | copy-start | bytes 3028
  35.4 4.2 %collective-permute-start = (s32[3,84]{1,0:T(4,128)S(1)}, s32[3,84]{1,0:T(4,128)S(1)}, u32[]{:S(2)}, u32[]{:S(2)}) collective-permute-start(s32[3,84]{1,0:T(4,128)S(1)} %bitcast.17), channel_id=1, source_target_pairs={{240,0},{0,16},{16,32},{32,48},{48,64},{64,80},{80,96},{96,112},{1... | collective-permute-start | bytes 3032 | tf_op jit(solution)/shard_map/ppermute | solution.py:25
  39.6 0.5 copy-start.9
  42.4 0.7 %copy-start.4 = (bf16[7,64,256]{2,1,0:T(8,128)(2,1)}, bf16[7,64,256]{2,1,0:T(8,128)(2,1)S(1)}, u32[]{:S(2)}) copy-start(bf16[7,64,256]{2,1,0:T(8,128)(2,1)S(1)} %collective-permute-done.6.refs_3_) | copy-start | bytes 688132
  42.4 0.8 %copy-start.1 = (bf16[14,64,256]{2,1,0:T(8,128)(2,1)}, bf16[14,64,256]{2,1,0:T(8,128)(2,1)S(1)}, u32[]{:S(2)}) copy-start(bf16[14,64,256]{2,1,0:T(8,128)(2,1)S(1)} %collective-permute-done.4.refs_1_) | copy-start | bytes 1376260
  42.4 1.0 %copy-start.2 = (bf16[14,64,256]{2,1,0:T(8,128)(2,1)}, bf16[14,64,256]{2,1,0:T(8,128)(2,1)S(1)}, u32[]{:S(2)}) copy-start(bf16[14,64,256]{2,1,0:T(8,128)(2,1)S(1)} %collective-permute-done.5.refs_2_) | copy-start | bytes 1376260
  42.4 1.2 %copy-start = (bf16[21,64,256]{2,1,0:T(8,128)(2,1)}, bf16[21,64,256]{2,1,0:T(8,128)(2,1)S(1)}, u32[]{:S(2)}) copy-start(bf16[21,64,256]{2,1,0:T(8,128)(2,1)S(1)} %collective-permute-done.7.refs_4_) | copy-start | bytes 2064388
  48.4 17.1 %collective-permute-start.8 = (bf16[256,512]{1,0:T(8,128)(2,1)}, bf16[256,512]{1,0:T(8,128)(2,1)S(1)}, u32[]{:S(2)}, u32[]{:S(2)}) collective-permute-start(bf16[256,512]{1,0:T(8,128)(2,1)} %straddle.1), channel_id=1, source_target_pairs={{15,0},{0,1},{1,2},{2,3},{3,4},{4,5},{5,6},{6,7},{7,8},{8,9},{9,10... | collective-permute-start | bytes 786440 | tf_op jit(solution)/shard_map/ppermute | solution.py:25
  65.6 0.7 %copy-start.3 = (bf16[256,512]{1,0:T(8,128)(2,1)}, bf16[256,512]{1,0:T(8,128)(2,1)S(1)}, u32[]{:S(2)}) copy-start(bf16[256,512]{1,0:T(8,128)(2,1)S(1)} %collective-permute-done.8.incoming_ref) | copy-start | bytes 786436

commit v2 on v0

v2 whole, which is shorter than its diff:
```python
import jax
import jax.numpy as jnp
from jax import lax
from jax.experimental import pallas as pl
from jax.experimental.pallas import tpu as pltpu
from jax.sharding import PartitionSpec as P

KG = 4
FS = 14
HALF = FS // 2
ROWS = 84
PAD = 88
SETS = 6
B = 64
POOL = ROWS + FS + FS + HALF + HALF + FS
F32 = jnp.float32
BF16 = jnp.bfloat16
VMEM_BYTES = 56 * 1024 * 1024


def passed_along(block, axis, distance):
    n = lax.axis_size(axis)
    return lax.ppermute(block, axis, [((i - distance) % n, i) for i in range(n)])


def iota(shape, dim):
    return lax.broadcasted_iota(jnp.int32, shape, dim)


QUARTERS = 4
CHUNK = B // QUARTERS
STRIDE = 89
SENDS = (((70, 14),), ((56, 14),), ((7, 7),), ((0, 7), (14, 14)))
ANY = pl.BlockSpec(memory_space=pl.ANY)
SMEM = pl.BlockSpec(memory_space=pltpu.SMEM)
VMEM = pl.BlockSpec(memory_space=pltpu.VMEM)


def call(kernel, name, ins, outs, scratch, flops, nbytes, aliases=None):
    return pl.pallas_call(
        kernel,
        in_specs=ins,
        out_specs=[spec for spec, _ in outs],
        out_shape=[jax.ShapeDtypeStruct(*shape) for _, shape in outs],
        scratch_shapes=scratch,
        input_output_aliases=aliases or {},
        compiler_params=pltpu.CompilerParams(vmem_limit_bytes=VMEM_BYTES),
        cost_estimate=pl.CostEstimate(flops=flops, bytes_accessed=nbytes, transcendentals=0),
        name=name,
    )


def groups(lead, set_base):
    group = (lead >> 2) - set_base
    own = (group >= 0) & (group < SETS)
    return jnp.where(own, jnp.where(group > 0, group + 1, 0), 1)


def to_column(row):
    wide = jnp.broadcast_to(row, (ROWS, ROWS))
    diagonal = iota((ROWS, ROWS), 0) == iota((ROWS, ROWS), 1)
    return jnp.sum(jnp.where(diagonal, wide, 0.0), axis=1, keepdims=True)


def ranks(key):
    order = (key * 128 + iota((1, ROWS), 1)).astype(F32)
    return jnp.sum(jnp.where(to_column(order) < order, 1.0, 0.0), axis=0, keepdims=True)


def nt(x, y):
    return lax.dot_general(x, y, (((1,), (1,)), ((), ())), preferred_element_type=F32)


def tn(x, y):
    return lax.dot_general(x, y, (((0,), (0,)), ((), ())), preferred_element_type=F32)


def quarter(c):
    return pl.ds(pl.multiple_of(c * CHUNK, CHUNK), CHUNK)


def send_copies(c, pool_ref, send_refs, sems):
    copies = []
    for ref, runs in zip(send_refs, SENDS):
        total = sum(n for _, n in runs)
        done = 0
        for first, n in runs:
            copies.append(pltpu.make_async_copy(
                pool_ref.at[pl.ds(first, n), quarter(c)],
                ref.at[pl.ds(c * total + done, n)],
                sems.at[c, len(copies)],
            ))
            done += n
    return copies


def prolong_kernel(base_ref, cols_ref, p_hbm, pool_hbm, up_hbm, down_hbm, fore_hbm, back_hbm,
                   sel_ref, order_ref, p_ref, pool_ref, ids_ref, t0_ref, t1_ref,
                   in_sems, out_sems, id_sems):
    def fetch(c):
        return pltpu.make_async_copy(p_hbm.at[:, quarter(c)], p_ref.at[:, quarter(c)], in_sems.at[c])

    sends = (up_hbm, down_hbm, fore_hbm, back_hbm)

    def stores(c):
        whole = pltpu.make_async_copy(
            pool_ref.at[:, quarter(c)], pool_hbm.at[:, quarter(c)], out_sems.at[c, 5])
        return send_copies(c, pool_ref, sends, out_sems) + [whole]

    for c in range(QUARTERS):
        fetch(c).start()
    rank = ranks(groups(cols_ref[0:1, :], base_ref[0]))
    sel = jnp.where(rank.astype(jnp.int32) == iota((PAD, ROWS), 0), 1.0, 0.0).astype(BF16)
    sel_ref[...] = sel
    order = nt(iota((16, ROWS), 1).astype(F32).astype(BF16), sel)
    order_ref[...] = order[:8].astype(jnp.int32)
    ids_ref[...] = jnp.zeros((16, KG * B), BF16)
    ids_ref[:, :PAD] = order.astype(BF16)
    id_copies = []
    for n, ref in enumerate(sends):
        id_copies.append(pltpu.make_async_copy(ids_ref, ref.at[ref.shape[0] - 1], id_sems.at[n]))
    for copy in id_copies:
        copy.start()
    place = cols_ref[...] & 3
    weights = [
        [jnp.where(place[q:q + 1, :] == r, 1.0, 0.0).astype(BF16) for q in range(3)]
        for r in range(KG)
    ]

    def step(c, carry):
        fetch(c).wait()
        for b in range(CHUNK):
            x = [p_ref[q, c * CHUNK + b] for q in range(3)]
            y = [x[0] * w[0] + x[1] * w[1] + x[2] * w[2] for w in weights]
            t = nt(sel, jnp.concatenate(y, axis=0))
            t0_ref[b * STRIDE:b * STRIDE + PAD, :] = t[:, :128]
            t1_ref[b * STRIDE:b * STRIDE + PAD, :] = t[:, 128:]
        for i in range(ROWS):
            pool_ref[i, quarter(c), :] = jnp.concatenate(
                [t[pl.ds(i, CHUNK, stride=STRIDE), :] for t in (t0_ref, t1_ref)], axis=1
            ).astype(BF16)
        for copy in stores(c):
            copy.start()
        return carry

    lax.fori_loop(0, QUARTERS, step, 0)
    for copy in id_copies:
        copy.wait()
    for c in range(QUARTERS):
        for copy in stores(c):
            copy.wait()


def prolong(base, cols_t, p_t):
    def rows(n):
        return ANY, ((QUARTERS * n + 1, CHUNK, KG * B), BF16)

    return call(
        prolong_kernel, "prolong", [SMEM, VMEM, ANY],
        [(ANY, ((ROWS, B, KG * B), BF16)), rows(14), rows(14), rows(7), rows(21),
         (VMEM, ((PAD, ROWS), BF16)), (VMEM, ((8, PAD), jnp.int32))],
        [
            pltpu.VMEM((3, B, B, ROWS), BF16),
            pltpu.VMEM((ROWS, B, KG * B), BF16),
            pltpu.VMEM((16, KG * B), BF16),
            pltpu.VMEM((CHUNK * STRIDE, 128), F32),
            pltpu.VMEM((CHUNK * STRIDE, 128), F32),
            pltpu.SemaphoreType.DMA((QUARTERS,)),
            pltpu.SemaphoreType.DMA((QUARTERS, 6)),
            pltpu.SemaphoreType.DMA((4,)),
        ],
        400_000_000, 8_000_000,
    )(base, cols_t, p_t)


def set_name(slot):
    name = jnp.where(slot < 7, 0.0, 1.0)
    for start, value in ((14, 2.0), (28, 3.0), (42, 4.0), (56, 5.0), (70, 6.0), (84, 7.0),
                         (98, 8.0), (112, 0.0), (119, 1.0), (126, 9.0)):
        name = jnp.where(slot >= start, value, name)
    return name


def own_mask(src, key, sel):
    own = jnp.where(set_name(src) == key, 1.0, 0.0)
    by_row = nt(sel, own.astype(BF16)).astype(BF16)
    spread = jnp.where(iota((8, 8 * B), 1) >> 6 == iota((8, 8 * B), 0), 1.0, 0.0).astype(BF16)
    return jnp.dot(by_row, spread, preferred_element_type=F32)


def sorted_slots(src, sel):
    return nt(jnp.maximum(src, 0.0).astype(BF16), sel).astype(jnp.int32)


def merge_row(i, place, row, src_ref, mask_ref, a_ref, pool_ref, merged_ref):
    index = [src_ref[k, row] for k in range(7)]
    w = jnp.concatenate([pool_ref[j] for j in index] + [pool_ref[index[0]]], axis=0)
    a = a_ref[i]
    mask = jnp.broadcast_to(mask_ref[pl.ds(row, 1), :], a.shape).astype(BF16)
    a_own = a * mask
    both = jnp.concatenate([a_own, a - a_own], axis=0)
    merged = jnp.dot(both, w, preferred_element_type=F32).astype(BF16)
    merged_ref[place * B:place * B + B, :KG * B] = merged[:B]
    merged_ref[place * B:place * B + B, KG * B:] = merged[B:]


def order_slots(c_cols_ref, set_id, first_row, place_ref):
    for r in range(KG):
        for s in range(8):
            c = c_cols_ref[s, first_row + r]
            u = (c & 3) + jnp.where((c >> 2) == set_id, 0, 4)
            place_ref[r, u] = s


def store_blocks(total, first_row, place_ref, out_ref):
    total = total.astype(BF16)
    for r in range(KG):
        for u in range(8):
            out_ref[first_row + r, place_ref[r, u]] = total[r * B:(r + 1) * B, u * B:(u + 1) * B]


def one_set(s, set_base, src_ref, c_cols_ref, mask_ref, a_ref, pool_ref, merged_ref, place_ref,
            blocks_ref):
    first = s * FS
    order_slots(c_cols_ref, set_base + s, s * KG, place_ref)
    for i in range(FS):
        merge_row(first + i, i, first + i, src_ref, mask_ref, a_ref, pool_ref, merged_ref)
    own = pool_ref[pl.ds(first, FS)].reshape(FS * B, KG * B)
    store_blocks(tn(own, merged_ref[...]), s * KG, place_ref, blocks_ref)


def operator_kernel(base_ref, order_ref, c_cols_ref, cols_ref, a_cols_ref, sel_ref, a_hbm, pool_hbm,
                    a_rows_hbm, out_hbm, local_ref, flags_ref,
                    a_ref, rows_ref, pool_ref, blocks_ref, merged_ref, mask_ref, src_v, src_ref,
                    flag_s, place_ref, t0, t1, t2, t3, in_sems, sems, out_sems):
    def fetch(c):
        return pltpu.make_async_copy(a_hbm.at[:, quarter(c)], a_ref.at[:, quarter(c)], in_sems.at[c])

    for c in range(QUARTERS):
        fetch(c).start()
    load = pltpu.make_async_copy(pool_hbm, pool_ref, sems.at[0])
    load.start()

    key = groups(cols_ref[0:1, :], base_ref[0])
    rank = to_column(ranks(key)) + 1.0
    row = iota((ROWS, ROWS), 0)
    first_row = base_ref[0] // SETS * ROWS
    sources = [
        jnp.sum(jnp.where(a_cols_ref[k:k + 1, :] - first_row == row, rank, 0.0), axis=0,
                keepdims=True) - 1.0
        for k in range(7)
    ]
    src = jnp.concatenate(sources + [sources[0]], axis=0)
    keys = key.astype(F32)
    local_ref[...] = jnp.where(iota((8, ROWS), 0) < 7, src, keys)
    away = jnp.max(jnp.where(src < 0.0, 1.0, 0.0), axis=0, keepdims=True)
    away = jnp.sum(jnp.where(iota((8, ROWS), 0).astype(F32) == keys, away, 0.0), axis=1, keepdims=True)
    flags_ref[...] = jnp.broadcast_to(away, (8, 128)).astype(jnp.int32)
    sel = sel_ref[...]
    src_v[:, :PAD] = sorted_slots(src, sel)
    src_v[:, PAD:] = jnp.zeros((8, 128 - PAD), jnp.int32)
    mask_ref[...] = own_mask(src, keys, sel)
    to_smem = [pltpu.make_async_copy(src_v, src_ref, sems.at[1]),
               pltpu.make_async_copy(flags_ref, flag_s, sems.at[2])]
    for copy in to_smem:
        copy.start()

    t_refs = (t0, t1, t2, t3)

    def step(c, carry):
        fetch(c).wait()
        for a in range(CHUNK):
            zero = jnp.zeros((B, ROWS), BF16)
            x = [a_ref[k, c * CHUNK + a] for k in range(7)] + [zero]
            for h in range(4):
                pair = jnp.concatenate(x[2 * h:2 * h + 2], axis=0)
                t_refs[h][a * STRIDE:a * STRIDE + ROWS, :] = jnp.transpose(pair).astype(F32)
        for i in range(ROWS):
            rows_ref[i, quarter(c), :] = jnp.concatenate(
                [t[pl.ds(order_ref[0, i], CHUNK, stride=STRIDE), :] for t in t_refs], axis=1
            ).astype(BF16)
        return carry

    lax.fori_loop(0, QUARTERS, step, 0)
    keep = pltpu.make_async_copy(rows_ref, a_rows_hbm, sems.at[3])
    keep.start()
    load.wait()
    for copy in to_smem:
        copy.wait()

    def store(s):
        rows = pl.ds(s * KG, KG)
        return pltpu.make_async_copy(blocks_ref.at[rows], out_hbm.at[rows], out_sems.at[s])

    def work(s, carry):
        @pl.when(flag_s[s + 1, 0] == 0)
        def _():
            one_set(s, base_ref[0], src_ref, c_cols_ref, mask_ref, rows_ref, pool_ref, merged_ref,
                    place_ref, blocks_ref)
            store(s).start()
        return carry

    lax.fori_loop(1, SETS, work, 0)

    def end(s, carry):
        @pl.when(flag_s[s + 1, 0] == 0)
        def _():
            store(s).wait()
        return carry

    lax.fori_loop(1, SETS, end, 0)
    keep.wait()


def operator(base, order, c_cols_t, cols_t, a_cols_t, sel, a_t, pool):
    return call(
        operator_kernel, "operator", [SMEM, SMEM, SMEM, VMEM, VMEM, VMEM, ANY, ANY],
        [(ANY, ((ROWS, B, 8 * B), BF16)), (ANY, ((SETS * KG, 8, B, B), BF16)),
         (VMEM, ((8, ROWS), F32)), (VMEM, ((8, 128), jnp.int32))],
        [
            pltpu.VMEM((7, B, B, ROWS), BF16),
            pltpu.VMEM((ROWS, B, 8 * B), BF16),
            pltpu.VMEM((ROWS, B, KG * B), BF16),
            pltpu.VMEM((SETS * KG, 8, B, B), BF16),
            pltpu.VMEM((FS * B, 8 * B), BF16),
            pltpu.VMEM((PAD, 8 * B), F32),
            pltpu.VMEM((8, 128), jnp.int32),
            pltpu.SMEM((8, 128), jnp.int32),
            pltpu.SMEM((8, 128), jnp.int32),
            pltpu.SMEM((KG, 8), jnp.int32),
        ] + [pltpu.VMEM((CHUNK * STRIDE, 128), F32)] * 4 + [
            pltpu.SemaphoreType.DMA((QUARTERS,)),
            pltpu.SemaphoreType.DMA((4,)),
            pltpu.SemaphoreType.DMA((SETS,)),
        ],
        4_000_000_000, 18_000_000,
    )(base, order, c_cols_t, cols_t, a_cols_t, sel, a_t, pool)


def pool_copies(parts, pool_ref, sems):
    copies = [pltpu.make_async_copy(parts[0], pool_ref.at[pl.ds(0, ROWS)], sems.at[0, 0])]
    start = ROWS
    for n, part in enumerate(parts[1:]):
        rows = (part.shape[0] - 1) // QUARTERS
        for c in range(QUARTERS):
            copies.append(pltpu.make_async_copy(
                part.at[pl.ds(c * rows, rows)],
                pool_ref.at[pl.ds(start, rows), pl.ds(c * CHUNK, CHUNK)],
                sems.at[n + 1, c],
            ))
        start += rows
    return copies


def straddle_kernel(ids_ref, a_cols_ref, local_ref, sel_ref, a_rows_hbm, *refs):
    parts = refs[:5]
    (out_ref, src_out, mask_ref, pool_ref, rows_ref, names_ref, merged_ref, src_ref, sems,
     name_sems, extra_sems) = refs[5:]
    names = [
        pltpu.make_async_copy(part.at[part.shape[0] - 1], names_ref.at[n], name_sems.at[n])
        for n, part in enumerate(parts[1:])
    ]
    for copy in names:
        copy.start()
    loads = pool_copies(parts, pool_ref, sems)
    loads.append(pltpu.make_async_copy(a_rows_hbm.at[pl.ds(HALF, HALF)], rows_ref, extra_sems.at[0]))
    for copy in loads:
        copy.start()
    for copy in names:
        copy.wait()
    shifts = (((70, 84, 84 - 70),), ((56, 70, 98 - 56),), ((7, 14, 112 - 7),),
              ((0, 7, 119), (14, 28, 126 - 14)))
    near = ((64, 88), (56, 72), (0, 16), (0, 32))
    found = [jnp.zeros((1, ROWS), F32)] * 7
    for n in range(4):
        low, high = near[n]
        column = jnp.transpose(names_ref[n][:, :128].astype(F32))[low:high, 0:1].astype(jnp.int32)
        row = iota((high - low, 1), 0) + low
        slot = jnp.zeros((high - low, 1), jnp.int32)
        for first, last, shift in shifts[n]:
            slot = jnp.where((row >= first) & (row < last), row + shift + 1, slot)
        column = jnp.where(slot > 0, column + ids_ref[n + 1] * ROWS, -1)
        slot = slot.astype(F32)
        for k in range(7):
            found[k] = found[k] + jnp.sum(
                jnp.where(a_cols_ref[k:k + 1, :] == column, slot, 0.0), axis=0, keepdims=True)
    local = local_ref[...]
    away = jnp.concatenate(found + [found[0]], axis=0) - 1.0
    src = jnp.where(local >= 0.0, local, away)
    src = jnp.where(iota((8, ROWS), 0) < 7, src, jnp.broadcast_to(src[0:1, :], (8, ROWS)))
    sel = sel_ref[...]
    src_out[:, :PAD] = sorted_slots(src, sel)
    src_out[:, PAD:] = jnp.zeros((8, 128 - PAD), jnp.int32)
    to_smem = pltpu.make_async_copy(src_out, src_ref, extra_sems.at[1])
    to_smem.start()
    mask_ref[...] = own_mask(src, local[7:8, :], sel)
    to_smem.wait()
    for copy in loads:
        copy.wait()
    for i in range(HALF):
        merge_row(i, i, HALF + i, src_ref, mask_ref, rows_ref, pool_ref, merged_ref)
    own = pool_ref[HALF:FS].reshape(HALF * B, KG * B)
    out_ref[...] = tn(own, merged_ref[...]).astype(BF16)


def straddle(ids, a_cols_t, local, sel, a_rows, parts):
    return call(
        straddle_kernel, "straddle", [SMEM, VMEM, VMEM, VMEM, ANY] + [ANY] * 5,
        [(VMEM, ((KG * B, 8 * B), BF16)), (VMEM, ((8, 128), jnp.int32)), (VMEM, ((PAD, 8 * B), F32))],
        [
            pltpu.VMEM((POOL, B, KG * B), BF16),
            pltpu.VMEM((HALF, B, 8 * B), BF16),
            pltpu.VMEM((4, 16, KG * B), BF16),
            pltpu.VMEM((HALF * B, 8 * B), BF16),
            pltpu.SMEM((8, 128), jnp.int32),
            pltpu.SemaphoreType.DMA((5, QUARTERS)),
            pltpu.SemaphoreType.DMA((4,)),
            pltpu.SemaphoreType.DMA((2,)),
        ],
        300_000_000, 6_000_000,
    )(ids, a_cols_t, local, sel, a_rows, *parts)


def sets_kernel(base_ref, src_ref, flag_ref, c_cols_ref, mask_ref, a_rows_hbm, *refs):
    parts = refs[:5]
    (_, out_hbm, first_ref, pool_ref, rows_ref, blocks_ref, merged_ref, place_ref, sems, row_sems,
     out_sems) = refs[5:]
    loads = pool_copies(parts, pool_ref, sems)

    def fetch(s):
        rows = pl.ds(s * FS, FS)
        return pltpu.make_async_copy(a_rows_hbm.at[rows], rows_ref.at[rows], row_sems.at[s])

    def store(s):
        rows = pl.ds(s * KG, KG)
        return pltpu.make_async_copy(blocks_ref.at[rows], out_hbm.at[rows], out_sems.at[s])

    def here(s):
        return flag_ref[s + 1, 0] != 0

    fetch(0).start()
    for copy in loads:
        copy.start()
    for s in range(1, SETS):
        @pl.when(here(s))
        def _(s=s):
            fetch(s).start()
    fetch(0).wait()
    for copy in loads:
        copy.wait()
    for i in range(HALF):
        merge_row(i, i, i, src_ref, mask_ref, rows_ref, pool_ref, merged_ref)
    own = pool_ref[:HALF].reshape(HALF * B, KG * B)
    first_ref[...] = tn(own, merged_ref[:HALF * B, :])

    def work(s, carry):
        @pl.when(here(s))
        def _():
            fetch(s).wait()
            one_set(s, base_ref[0], src_ref, c_cols_ref, mask_ref, rows_ref, pool_ref, merged_ref,
                    place_ref, blocks_ref)
            store(s).start()
        return carry

    lax.fori_loop(1, SETS, work, 0)

    def end(s, carry):
        @pl.when(here(s))
        def _():
            store(s).wait()
        return carry

    lax.fori_loop(1, SETS, end, 0)


def sets(base, src, flags, c_cols_t, mask, a_rows, parts, whole):
    return call(
        sets_kernel, "sets", [SMEM, SMEM, SMEM, SMEM, VMEM, ANY] + [ANY] * 6,
        [(ANY, ((SETS * KG, 8, B, B), BF16)), (VMEM, ((KG * B, 8 * B), F32))],
        [
            pltpu.VMEM((POOL, B, KG * B), BF16),
            pltpu.VMEM((ROWS, B, 8 * B), BF16),
            pltpu.VMEM((SETS * KG, 8, B, B), BF16),
            pltpu.VMEM((FS * B, 8 * B), BF16),
            pltpu.SMEM((KG, 8), jnp.int32),
            pltpu.SemaphoreType.DMA((5, QUARTERS)),
            pltpu.SemaphoreType.DMA((SETS,)),
            pltpu.SemaphoreType.DMA((SETS,)),
        ],
        2_500_000_000, 12_000_000, aliases={11: 0},
    )(base, src, flags, c_cols_t, mask, a_rows, *parts, whole)


def finish_kernel(base_ref, c_cols_ref, first_ref, incoming_ref, _, out_hbm, blocks_ref, place_ref,
                  sem):
    order_slots(c_cols_ref, base_ref[0], 0, place_ref)
    store_blocks(first_ref[...] + incoming_ref[...].astype(F32), 0, place_ref, blocks_ref)
    copy = pltpu.make_async_copy(blocks_ref, out_hbm.at[pl.ds(0, KG)], sem)
    copy.start()
    copy.wait()


def finish(base, c_cols_t, first, incoming, whole):
    return call(
        finish_kernel, "finish", [SMEM, SMEM, VMEM, VMEM, ANY],
        [(ANY, ((SETS * KG, 8, B, B), BF16))],
        [pltpu.VMEM((KG, 8, B, B), BF16), pltpu.SMEM((KG, 8), jnp.int32), pltpu.SemaphoreType.DMA],
        1_000_000, 1_500_000, aliases={4: 0},
    )(base, c_cols_t, first, incoming, whole)[0]


def shards(a_blocks, a_cols, p_blocks, p_cols, c_cols):
    dom_count = lax.axis_size("dom")
    sub_count = lax.axis_size("sub")
    dom = lax.axis_index("dom")
    sub = lax.axis_index("sub")
    device = dom * sub_count + sub
    ids = jnp.stack([
        device,
        (dom + dom_count - 1) % dom_count * sub_count + sub,
        (dom + 1) % dom_count * sub_count + sub,
        dom * sub_count + (sub + sub_count - 1) % sub_count,
        dom * sub_count + (sub + 1) % sub_count,
    ]).astype(jnp.int32)
    base = ids[:1] * SETS
    cols_t, a_cols_t, c_cols_t = p_cols.T, a_cols.T, c_cols.T
    moves = (("dom", 1), ("dom", -1), ("sub", 1), ("sub", -1))
    pool, *sends, sel, order = prolong(base, cols_t, p_blocks.transpose(1, 2, 3, 0))
    parts = [pool] + [passed_along(rows, axis, step) for rows, (axis, step) in zip(sends, moves)]
    a_rows, whole, local, flags = operator(
        base, order, c_cols_t, cols_t, a_cols_t, sel, a_blocks.transpose(1, 2, 3, 0), pool)
    partial, src, mask = straddle(ids, a_cols_t, local, sel, a_rows, parts)
    incoming = passed_along(partial, "sub", 1)
    whole, first = sets(base, src, flags, c_cols_t, mask, a_rows, parts, whole)
    return finish(base, c_cols_t, first, incoming, whole)


def solution(mesh):
    spec4 = P(("dom", "sub"), None, None, None)
    spec2 = P(("dom", "sub"), None)
    return jax.shard_map(
        shards, mesh=mesh, in_specs=(spec4, spec2, spec4, spec2, spec2), out_specs=spec4,
        check_vma=False,
    )
```

time: 826 us -> 48.1 us (0.06); the launches traced: 811 us -> 47.6 us
  local copies, waits for them, and re-layouts: 364 us -> 2.26 us
  other arithmetic: 331 us -> 0 us
  matrix products: 70.3 us -> 0 us
  Pallas kernels: 0 us -> 33.3 us
  starting transfers between devices: 26.9 us -> 7.12 us
  waiting for transfers between devices: 18.2 us -> 4.89 us
    scatter-add x9 -> x0, other arithmetic: 320 us -> none  [the longest x4 315 us: partial_sums(): running.at[flat_target[first_row:last_row].reshape(-1)]]
    gather x19 -> x0, local copies, waits for them, and re-layouts: 161 us -> none  [the longest x4 142 us: partial_sums(): selected = pool_flat[picks[first_row:last_row]]]
    dot_general x4 -> x0, matrix products: 70.3 us -> none  [partial_sums(): jnp.einsum('ipab,iuac->ipubc', p_rows[first_row:last_row], merged, prefer...]
    transpose x4 -> x0, local copies, waits for them, and re-layouts: 68.2 us -> none  [partial_sums(): jnp.einsum('ipab,iuac->ipubc', p_rows[first_row:last_row], merged, prefer...]
    unnamed x28 -> x10, local copies, waits for them, and re-layouts: 43.2 us -> 1.59 us
    concatenate x5 -> x0, local copies, waits for them, and re-layouts: 37.9 us -> none  [the longest x2 29.9 us: shards(): jnp.concatenate([p_blocks, below[0], above[0], before[0], after[0]], axis=0)]
    pallas_call x0 -> x5, Pallas kernels: none -> 33.3 us  [the longest x1 9.62 us: operator(): call(operator_kernel, 'operator', [SMEM, SMEM, SMEM, VMEM, VMEM, VMEM, AN...]
    slice x12 -> x0, local copies, waits for them, and re-layouts: 29.2 us -> none  [the longest x1 21.3 us: partial_sums(): a_rows[first_row:last_row]]
  transfers between devices with their start and end apart: 14 -> 5, of which waited for: 4 -> 3; matrix products, arithmetic and copies ran while one was open for 15% -> 1% of each run, Pallas kernels for 0% -> 40%
where the time goes in v2:
time: 48.1 us; the launch traced here: 47.6 us
  Pallas kernels  33.3 us (69%)
  starting transfers between devices  7.12 us (15%)
  waiting for transfers between devices  4.89 us (10%)
  local copies, waits for them, and re-layouts  2.26 us (5%)
    pallas_call x1, Pallas kernels, operator(): call(operator_kernel, 'operator', [SMEM, SMEM, SMEM, VMEM, VMEM, VMEM, AN...  9.62 us
    pallas_call x1, Pallas kernels, sets(): call(sets_kernel, 'sets', [SMEM, SMEM, SMEM, SMEM, VMEM, ANY] + [ANY] * 6...  9.56 us
    ppermute x5, starting transfers between devices, passed_along(): lax.ppermute(block, axis, [((i - distance) % n, i) for i in range(n)])  7.12 us
    pallas_call x1, Pallas kernels, prolong(): call(prolong_kernel, 'prolong', [SMEM, VMEM, ANY], [(ANY, ((ROWS, B, KG *...  6.61 us
    pallas_call x1, Pallas kernels, straddle(): call(straddle_kernel, 'straddle', [SMEM, VMEM, VMEM, VMEM, ANY] + [ANY] *...  5.4 us
    ppermute x5, waiting for transfers between devices, passed_along(): lax.ppermute(block, axis, [((i - distance) % n, i) for i in range(n)])  4.89 us
    pallas_call x1, Pallas kernels, finish(): call(finish_kernel, 'finish', [SMEM, SMEM, VMEM, VMEM, ANY], [(ANY, ((SET...  2.12 us
    unnamed x10, local copies, waits for them, and re-layouts  1.59 us
  transfers between devices with their start and end apart: 5, of which 3 were waited for; matrix products, arithmetic and copies ran while one was open for 1% of the time, Pallas kernels for 40%

profile of v2, /device:TPU:96, one launch (start us, length us, event | category | flops | bytes accessed | tf_op | source)
XLA Modules:
  0.0 47.6 jit_solution(1257057467538154825)
XLA Ops:
  0.0 6.6 %prolong.1 = (bf16[84,64,256]{2,1,0:T(8,128)(2,1)}, bf16[57,16,256]{2,1,0:T(8,128)(2,1)}, bf16[57,16,256]{2,1,0:T(8,128)(2,1)}, bf16[29,16,256]{2,1,0:T(8,128)(2...) custom-call(s32[1]{0:T(128)S(6)} %mul.15.base_ref, s32[3,84]{1,0:T(4,128)} %bitcast.16, ...), custom_call_target="tpu_custom_call" | custom-call | flops 400000000 | bytes 8000000 | tf_op jit(solution)/shard_map/prolong/pallas_call | solution.py:158
  6.6 5.3 %collective-permute-start.3 = (bf16[85,16,256]{2,1,0:T(8,128)(2,1)}, bf16[85,16,256]{2,1,0:T(8,128)(2,1)S(1)}, u32[]{:S(2)}, u32[]{:S(2)}) collective-permute-start(bf16[85,16,256]{2,1,0:T(8,128)(2,1)} %get-tuple-element.29), channel_id=1, source_target_pairs={{1,0},{2,1},{3,2},{4,3},{5,4},{6,5},{7,6},{8,7},{9,8},{10,9},{11,1... | collective-permute-start | bytes 2088968 | tf_op jit(solution)/shard_map/ppermute | solution.py:23
  11.9 0.0 collective-permute-start
  11.9 1.7 %collective-permute-start.1 = (bf16[57,16,256]{2,1,0:T(8,128)(2,1)}, bf16[57,16,256]{2,1,0:T(8,128)(2,1)S(1)}, u32[]{:S(2)}, u32[]{:S(2)}) collective-permute-start(bf16[57,16,256]{2,1,0:T(8,128)(2,1)} %get-tuple-element.27), channel_id=1, source_target_pairs={{16,0},{32,16},{48,32},{64,48},{80,64},{96,80},{112,96},{128,112},... | collective-permute-start | bytes 1400840 | tf_op jit(solution)/shard_map/ppermute | solution.py:23
  13.7 0.0 collective-permute-start.2
  13.7 0.7 %stack.23.ids_ref = s32[5]{0:T(128)} concatenate(s32[1]{0:T(128)} %bitcast, s32[1]{0:T(128)} %bitcast.2, s32[1]{0:T(128)} %bitcast.3, s32[1]{0:T(128)} %bitcast.4, s32[1]{0:T(128)} %bitcast.5), dimensions={0} | concatenate | bytes 40 | tf_op jit(solution)/shard_map/stack | solution.py:518
  14.3 9.6 %operator.1 = (bf16[84,64,512]{2,1,0:T(8,128)(2,1)}, bf16[24,8,64,64]{3,2,1,0:T(8,128)(2,1)}, f32[8,84]{1,0:T(8,128)}, s32[8,128]{1,0:T(8,128)}) custom-call(s32[1]{0:T(128)S(6)} %mul.15.base_ref, s32[8,88]{1,0:T(8,128)} %get-tuple-element.21.order_ref, s32[8,24]{1,0:T(8,128)} %bitcast.11, s32[3,84]{1,0:T(4,128)} %bitcast.17, s32[7,84]{1,0:T(8,128)} %bitcast.14, ...), custom_call_target="tpu_custom_call" | custom-call | flops 4000000000 | bytes 18000000 | tf_op jit(solution)/shard_map/operator/pallas_call | solution.py:316
  24.0 1.4 %collective-permute-done.2.refs_3_ = bf16[29,16,256]{2,1,0:T(8,128)(2,1)S(1)} collective-permute-done((bf16[29,16,256]{2,1,0:T(8,128)(2,1)}, bf16[29,16,256]{2,1,0:T(8,128)(2,1)S(1)}, u32[]{:S(2)}, u32[]{:S(2)}) %collective-permute-start.2) | collective-permute-done | bytes 237600 | tf_op jit(solution)/shard_map/ppermute | solution.py:23
  25.4 0.0 copy-start.3
  25.4 0.0 collective-permute-done.refs_1_
  25.4 0.0 copy-start.1
  25.4 0.0 collective-permute-done.1.refs_2_
  25.4 0.0 copy-start.2
  25.4 1.7 %collective-permute-done.3.refs_4_ = bf16[85,16,256]{2,1,0:T(8,128)(2,1)S(1)} collective-permute-done((bf16[85,16,256]{2,1,0:T(8,128)(2,1)}, bf16[85,16,256]{2,1,0:T(8,128)(2,1)S(1)}, u32[]{:S(2)}, u32[]{:S(2)}) %collective-permute-start.3) | collective-permute-done | bytes 696352 | tf_op jit(solution)/shard_map/ppermute | solution.py:23
  27.1 0.0 copy-start
  27.1 0.0 copy-done.3
  27.1 0.0 copy-done.1
  27.1 0.0 copy-done.2
  27.1 0.9 %copy-done = bf16[85,16,256]{2,1,0:T(8,128)(2,1)} copy-done((bf16[85,16,256]{2,1,0:T(8,128)(2,1)}, bf16[85,16,256]{2,1,0:T(8,128)(2,1)S(1)}, u32[]{:S(2)}) %copy-start) | copy-done | bytes 696344
  28.0 5.4 %straddle.1 = (bf16[256,512]{1,0:T(8,128)(2,1)}, s32[8,128]{1,0:T(8,128)}, f32[88,512]{1,0:T(8,128)}) custom-call(s32[5]{0:T(128)} %stack.23.ids_ref, s32[7,84]{1,0:T(8,128)} %bitcast.15, f32[8,84]{1,0:T(8,128)} %get-tuple-element.24.local_ref, bf16[88,84]{1,0:T(8,128)(2,1)} %get-tuple-element.22.sel_ref, bf16[84,64,512]{2,1,0:T(8,128)(2,1)} %get-tuple-element.25.a_rows_hbm, ...), custom_call_target="tpu_custom_call" | custom-call | flops 300000000 | bytes 6000000 | tf_op jit(solution)/shard_map/straddle/pallas_call | solution.py:407
  33.4 0.1 collective-permute-start.4
  33.5 9.6 %sets.1 = (bf16[24,8,64,64]{3,2,1,0:T(8,128)(2,1)}, f32[256,512]{1,0:T(8,128)}) custom-call(s32[1]{0:T(128)S(6)} %mul.15.base_ref, s32[8,128]{1,0:T(8,128)} %get-tuple-element.30.src_ref, s32[8,128]{1,0:T(8,128)} %get-tuple-element.31.flag_ref, s32[8,24]{1,0:T(8,128)} %bitcast.12, ...), custom_call_target="tpu_custom_call", output_to_operand_aliasing={{0}: (11, {})} | custom-call | flops 2500000000 | bytes 12000000 | tf_op jit(solution)/shard_map/sets/pallas_call | solution.py:477
  43.1 1.8 %collective-permute-done.4.incoming_ref = bf16[256,512]{1,0:T(8,128)(2,1)S(1)} collective-permute-done((bf16[256,512]{1,0:T(8,128)(2,1)}, bf16[256,512]{1,0:T(8,128)(2,1)S(1)}, u32[]{:S(2)}, u32[]{:S(2)}) %collective-permute-start.4) | collective-permute-done | bytes 262176 | tf_op jit(solution)/shard_map/ppermute | solution.py:23
  44.8 0.0 copy-start.4
  44.8 0.7 %copy-done.4 = bf16[256,512]{1,0:T(8,128)(2,1)} copy-done((bf16[256,512]{1,0:T(8,128)(2,1)}, bf16[256,512]{1,0:T(8,128)(2,1)S(1)}, u32[]{:S(2)}) %copy-start.4) | copy-done | bytes 262168
  45.5 2.1 %finish.1 = bf16[24,8,64,64]{3,2,1,0:T(8,128)(2,1)} custom-call(s32[1]{0:T(128)S(6)} %mul.15.base_ref, s32[8,24]{1,0:T(8,128)} %bitcast.13, f32[256,512]{1,0:T(8,128)} %get-tuple-element.34.first_ref, bf16[256,512]{1,0:T(8,128)(2,1)} %copy-done.4, bf16[24,8,64,64]{3,2,1,0:T(8,128)(2,1)} %get-tuple-element.36._), custom_call_target="tpu_custom_call", output_to_operand_aliasing={{}: (4, {})} | custom-call | flops 1000000 | bytes 1500000 | tf_op jit(solution)/shard_map/finish/pallas_call | solution.py:504
Async XLA Ops:
  6.6 20.5 %collective-permute-start.3 = (bf16[85,16,256]{2,1,0:T(8,128)(2,1)}, bf16[85,16,256]{2,1,0:T(8,128)(2,1)S(1)}, u32[]{:S(2)}, u32[]{:S(2)}) collective-permute-start(bf16[85,16,256]{2,1,0:T(8,128)(2,1)} %get-tuple-element.29), channel_id=1, source_target_pairs={{1,0},{2,1},{3,2},{4,3},{5,4},{6,5},{7,6},{8,7},{9,8},{10,9},{11,1... | collective-permute-start | bytes 2088968 | tf_op jit(solution)/shard_map/ppermute | solution.py:23
  11.9 13.5 %collective-permute-start = (bf16[57,16,256]{2,1,0:T(8,128)(2,1)}, bf16[57,16,256]{2,1,0:T(8,128)(2,1)S(1)}, u32[]{:S(2)}, u32[]{:S(2)}) collective-permute-start(bf16[57,16,256]{2,1,0:T(8,128)(2,1)} %get-tuple-element.26), channel_id=1, source_target_pairs={{240,0},{0,16},{16,32},{32,48},{48,64},{64,80},{80,96},{96,112},{1... | collective-permute-start | bytes 1400840 | tf_op jit(solution)/shard_map/ppermute | solution.py:23
  11.9 13.5 %collective-permute-start.1 = (bf16[57,16,256]{2,1,0:T(8,128)(2,1)}, bf16[57,16,256]{2,1,0:T(8,128)(2,1)S(1)}, u32[]{:S(2)}, u32[]{:S(2)}) collective-permute-start(bf16[57,16,256]{2,1,0:T(8,128)(2,1)} %get-tuple-element.27), channel_id=1, source_target_pairs={{16,0},{32,16},{48,32},{64,48},{80,64},{96,80},{112,96},{128,112},... | collective-permute-start | bytes 1400840 | tf_op jit(solution)/shard_map/ppermute | solution.py:23
  13.7 11.7 %collective-permute-start.2 = (bf16[29,16,256]{2,1,0:T(8,128)(2,1)}, bf16[29,16,256]{2,1,0:T(8,128)(2,1)S(1)}, u32[]{:S(2)}, u32[]{:S(2)}) collective-permute-start(bf16[29,16,256]{2,1,0:T(8,128)(2,1)} %get-tuple-element.28), channel_id=1, source_target_pairs={{15,0},{0,1},{1,2},{2,3},{3,4},{4,5},{5,6},{6,7},{7,8},{8,9},{9,10... | collective-permute-start | bytes 712712 | tf_op jit(solution)/shard_map/ppermute | solution.py:23
  25.4 1.7 %copy-start.3 = (bf16[29,16,256]{2,1,0:T(8,128)(2,1)}, bf16[29,16,256]{2,1,0:T(8,128)(2,1)S(1)}, u32[]{:S(2)}) copy-start(bf16[29,16,256]{2,1,0:T(8,128)(2,1)S(1)} %collective-permute-done.2.refs_3_) | copy-start | bytes 712708
  25.4 1.7 %copy-start.1 = (bf16[57,16,256]{2,1,0:T(8,128)(2,1)}, bf16[57,16,256]{2,1,0:T(8,128)(2,1)S(1)}, u32[]{:S(2)}) copy-start(bf16[57,16,256]{2,1,0:T(8,128)(2,1)S(1)} %collective-permute-done.refs_1_) | copy-start | bytes 1400836
  25.4 1.7 %copy-start.2 = (bf16[57,16,256]{2,1,0:T(8,128)(2,1)}, bf16[57,16,256]{2,1,0:T(8,128)(2,1)S(1)}, u32[]{:S(2)}) copy-start(bf16[57,16,256]{2,1,0:T(8,128)(2,1)S(1)} %collective-permute-done.1.refs_2_) | copy-start | bytes 1400836
  27.1 0.9 %copy-start = (bf16[85,16,256]{2,1,0:T(8,128)(2,1)}, bf16[85,16,256]{2,1,0:T(8,128)(2,1)S(1)}, u32[]{:S(2)}) copy-start(bf16[85,16,256]{2,1,0:T(8,128)(2,1)S(1)} %collective-permute-done.3.refs_4_) | copy-start | bytes 2088964
  33.4 11.4 %collective-permute-start.4 = (bf16[256,512]{1,0:T(8,128)(2,1)}, bf16[256,512]{1,0:T(8,128)(2,1)S(1)}, u32[]{:S(2)}, u32[]{:S(2)}) collective-permute-start(bf16[256,512]{1,0:T(8,128)(2,1)} %get-tuple-element.35), channel_id=1, source_target_pairs={{15,0},{0,1},{1,2},{2,3},{3,4},{4,5},{5,6},{6,7},{7,8},{8,9},{9,10... | collective-permute-start | bytes 786440 | tf_op jit(solution)/shard_map/ppermute | solution.py:23
  44.8 0.7 %copy-start.4 = (bf16[256,512]{1,0:T(8,128)(2,1)}, bf16[256,512]{1,0:T(8,128)(2,1)S(1)}, u32[]{:S(2)}) copy-start(bf16[256,512]{1,0:T(8,128)(2,1)S(1)} %collective-permute-done.4.incoming_ref) | copy-start | bytes 786436

commit v3 on v2

v3 whole, which is shorter than its diff:
```python
import jax
import jax.numpy as jnp
from jax import lax
from jax.experimental import pallas as pl
from jax.experimental.pallas import tpu as pltpu
from jax.sharding import PartitionSpec as P

KG = 4
FS = 14
HALF = FS // 2
ROWS = 84
PAD = 88
SETS = 6
B = 64
POOL = ROWS + FS + FS + HALF + HALF + FS
F32 = jnp.float32
BF16 = jnp.bfloat16


def passed_along(block, axis, distance):
    n = lax.axis_size(axis)
    return lax.ppermute(block, axis, [((i - distance) % n, i) for i in range(n)])


def iota(shape, dim):
    return lax.broadcasted_iota(jnp.int32, shape, dim)


QUARTERS = 4
CHUNK = B // QUARTERS
STRIDE = 89
SENDS = (((70, 14),), ((56, 14),), ((7, 7),), ((0, 7), (14, 14)))
ANY = pl.BlockSpec(memory_space=pl.ANY)
HBM = pl.BlockSpec(memory_space=pltpu.HBM)


def call(kernel, name, ins, outs, scratch, flops, nbytes, vmem, aliases=None, grid=()):
    return pl.pallas_call(
        kernel,
        grid=grid,
        in_specs=ins,
        out_specs=[ANY] * len(outs),
        out_shape=[jax.ShapeDtypeStruct(*shape) for shape in outs],
        scratch_shapes=scratch,
        input_output_aliases=aliases or {},
        compiler_params=pltpu.CompilerParams(vmem_limit_bytes=vmem * 1024 * 1024),
        cost_estimate=pl.CostEstimate(flops=flops, bytes_accessed=nbytes, transcendentals=0),
        name=name,
    )


def devices():
    dom_count, sub_count = lax.axis_size("dom"), lax.axis_size("sub")
    dom, sub = lax.axis_index("dom"), lax.axis_index("sub")

    def number(d, s):
        return lax.rem(d, dom_count) * sub_count + lax.rem(s, sub_count)

    return [number(dom, sub), number(dom + dom_count - 1, sub), number(dom + 1, sub),
            number(dom, sub + sub_count - 1), number(dom, sub + 1)]


def begin(copies):
    for copy in copies:
        copy.start()


def finished(copies):
    for copy in copies:
        copy.wait()


def load_all(pairs, sems):
    return [pltpu.make_async_copy(src, dst, sems.at[n]) for n, (src, dst) in enumerate(pairs)]


def groups(lead, set_base):
    group = (lead >> 2) - set_base
    own = (group >= 0) & (group < SETS)
    return jnp.where(own, jnp.where(group > 0, group + 1, 0), 1)


def to_column(row):
    wide = jnp.broadcast_to(row, (ROWS, ROWS))
    diagonal = iota((ROWS, ROWS), 0) == iota((ROWS, ROWS), 1)
    return jnp.sum(jnp.where(diagonal, wide, 0.0), axis=1, keepdims=True)


def ranks(key):
    order = (key * 128 + iota((1, ROWS), 1)).astype(F32)
    return jnp.sum(jnp.where(to_column(order) < order, 1.0, 0.0), axis=0, keepdims=True)


def selector(rank):
    return jnp.where(rank.astype(jnp.int32) == iota((PAD, ROWS), 0), 1.0, 0.0).astype(BF16)


def sorted_order(sel):
    return nt(iota((16, ROWS), 1).astype(F32).astype(BF16), sel)


def nt(x, y):
    return lax.dot_general(x, y, (((1,), (1,)), ((), ())), preferred_element_type=F32)


def tn(x, y):
    return lax.dot_general(x, y, (((0,), (0,)), ((), ())), preferred_element_type=F32)


def quarter(c):
    return pl.ds(pl.multiple_of(c * CHUNK, CHUNK), CHUNK)


def send_copies(c, pool_ref, send_refs, sems):
    copies = []
    for ref, runs in zip(send_refs, SENDS):
        total = sum(n for _, n in runs)
        done = 0
        for first, n in runs:
            copies.append(pltpu.make_async_copy(
                pool_ref.at[pl.ds(first, n), quarter(c)],
                ref.at[pl.ds(c * total + done, n)],
                sems.at[c, len(copies)],
            ))
            done += n
    return copies


def prolong_kernel(cols_ref, p_ref, pool_hbm, up_hbm, down_hbm, fore_hbm, back_hbm,
                   sel_ref, pool_ref, ids_ref, t0_ref, t1_ref, out_sems, id_sems):
    c = pl.program_id(0)
    sends = (up_hbm, down_hbm, fore_hbm, back_hbm)

    def stores(c):
        whole = pltpu.make_async_copy(
            pool_ref.at[:, quarter(c)], pool_hbm.at[:, quarter(c)], out_sems.at[c, 5])
        return send_copies(c, pool_ref, sends, out_sems) + [whole]

    id_copies = [pltpu.make_async_copy(ids_ref, ref.at[ref.shape[0] - 1], id_sems.at[n])
                 for n, ref in enumerate(sends)]

    @pl.when(c == 0)
    def _():
        sel = selector(ranks(groups(cols_ref[0:1, :], devices()[0] * SETS)))
        sel_ref[...] = sel
        ids_ref[...] = jnp.zeros((16, KG * B), BF16)
        ids_ref[:, :PAD] = sorted_order(sel).astype(BF16)
        begin(id_copies)

    sel = sel_ref[...]
    place = cols_ref[...] & 3
    weights = [
        [jnp.where(place[q:q + 1, :] == r, 1.0, 0.0).astype(BF16) for q in range(3)]
        for r in range(KG)
    ]
    for b in range(CHUNK):
        x = [p_ref[q, b] for q in range(3)]
        y = [x[0] * w[0] + x[1] * w[1] + x[2] * w[2] for w in weights]
        t = nt(sel, jnp.concatenate(y, axis=0))
        t0_ref[b * STRIDE:b * STRIDE + PAD, :] = t[:, :128]
        t1_ref[b * STRIDE:b * STRIDE + PAD, :] = t[:, 128:]
    for i in range(ROWS):
        pool_ref[i, quarter(c), :] = jnp.concatenate(
            [t[pl.ds(i, CHUNK, stride=STRIDE), :] for t in (t0_ref, t1_ref)], axis=1
        ).astype(BF16)
    begin(stores(c))

    @pl.when(c == QUARTERS - 1)
    def _():
        finished(id_copies)
        for done in range(QUARTERS):
            finished(stores(done))


def prolong(cols_t, p_t):
    def rows(n):
        return (QUARTERS * n + 1, CHUNK, KG * B), BF16

    return call(
        prolong_kernel, "prolong",
        [pl.BlockSpec((3, ROWS), lambda c: (0, 0)),
         pl.BlockSpec((3, CHUNK, B, ROWS), lambda c: (0, c, 0, 0))],
        [((ROWS, B, KG * B), BF16), rows(14), rows(14), rows(7), rows(21)],
        [
            pltpu.VMEM((PAD, ROWS), BF16),
            pltpu.VMEM((ROWS, B, KG * B), BF16),
            pltpu.VMEM((16, KG * B), BF16),
            pltpu.VMEM((CHUNK * STRIDE, 128), F32),
            pltpu.VMEM((CHUNK * STRIDE, 128), F32),
            pltpu.SemaphoreType.DMA((QUARTERS, 6)),
            pltpu.SemaphoreType.DMA((4,)),
        ],
        6_000_000_000, 8_000_000, 56, grid=(QUARTERS,),
    )(cols_t, p_t)


def set_name(slot):
    name = jnp.where(slot < 7, 0.0, 1.0)
    for start, value in ((14, 2.0), (28, 3.0), (42, 4.0), (56, 5.0), (70, 6.0), (84, 7.0),
                         (98, 8.0), (112, 0.0), (119, 1.0), (126, 9.0)):
        name = jnp.where(slot >= start, value, name)
    return name


def own_mask(src, key, sel):
    own = jnp.where(set_name(src) == key, 1.0, 0.0)
    by_row = nt(sel, own.astype(BF16)).astype(BF16)
    spread = jnp.where(iota((8, 8 * B), 1) >> 6 == iota((8, 8 * B), 0), 1.0, 0.0).astype(BF16)
    return jnp.dot(by_row, spread, preferred_element_type=F32)


def sorted_slots(src, sel):
    return nt(jnp.maximum(src, 0.0).astype(BF16), sel).astype(jnp.int32)


def merge_row(i, place, row, src_ref, mask_ref, a_ref, pool_ref, merged_ref):
    index = [src_ref[k, row] for k in range(7)]
    w = jnp.concatenate([pool_ref[j] for j in index] + [pool_ref[index[0]]], axis=0)
    a = a_ref[i]
    mask = jnp.broadcast_to(mask_ref[pl.ds(row, 1), :], a.shape).astype(BF16)
    a_own = a * mask
    both = jnp.concatenate([a_own, a - a_own], axis=0)
    merged = jnp.dot(both, w, preferred_element_type=F32).astype(BF16)
    merged_ref[place * B:place * B + B, :KG * B] = merged[:B]
    merged_ref[place * B:place * B + B, KG * B:] = merged[B:]


def order_slots(c_cols_ref, set_id, first_row, place_ref):
    for r in range(KG):
        for s in range(8):
            c = c_cols_ref[s, first_row + r]
            u = (c & 3) + jnp.where((c >> 2) == set_id, 0, 4)
            place_ref[r, u] = s


def store_blocks(total, first_row, place_ref, out_ref):
    total = total.astype(BF16)
    for r in range(KG):
        for u in range(8):
            out_ref[first_row + r, place_ref[r, u]] = total[r * B:(r + 1) * B, u * B:(u + 1) * B]


def one_set(s, set_base, src_ref, c_cols_ref, mask_ref, a_ref, pool_ref, merged_ref, place_ref,
            blocks_ref):
    first = s * FS
    order_slots(c_cols_ref, set_base + s, s * KG, place_ref)
    for i in range(FS):
        merge_row(first + i, i, first + i, src_ref, mask_ref, a_ref, pool_ref, merged_ref)
    own = pool_ref[pl.ds(first, FS)].reshape(FS * B, KG * B)
    store_blocks(tn(own, merged_ref[...]), s * KG, place_ref, blocks_ref)


def operator_kernel(c_cols_hbm, cols_hbm, a_cols_hbm, a_hbm, pool_hbm,
                    a_rows_hbm, a_next_hbm, out_hbm, local_hbm, flags_hbm, sel_hbm,
                    c_cols_ref, cols_ref, a_cols_ref, a_ref, rows_ref, pool_ref, blocks_ref, merged_ref,
                    mask_ref, local_ref, sel_ref, order_v, src_v, flag_v, order_ref, src_ref, flag_s,
                    place_ref, t0, t1, t2, t3, in_sems, sems, keep_sems, out_sems):
    def fetch(c):
        return pltpu.make_async_copy(a_hbm.at[:, quarter(c)], a_ref.at[:, quarter(c)], in_sems.at[c])

    small = load_all(((cols_hbm, cols_ref), (a_cols_hbm, a_cols_ref), (c_cols_hbm, c_cols_ref)), sems)
    begin(small)
    for c in range(QUARTERS):
        fetch(c).start()
    load = pltpu.make_async_copy(pool_hbm, pool_ref, sems.at[3])
    load.start()
    finished(small)

    device = devices()[0]
    set_base = device * SETS
    key = groups(cols_ref[0:1, :], set_base)
    rank = ranks(key)
    sel = selector(rank)
    sel_ref[...] = sel
    order_v[:, :PAD] = sorted_order(sel)[:8].astype(jnp.int32)
    order_v[:, PAD:] = jnp.zeros((8, 128 - PAD), jnp.int32)
    rank = to_column(rank) + 1.0
    row = iota((ROWS, ROWS), 0)
    sources = [
        jnp.sum(jnp.where(a_cols_ref[k:k + 1, :] - device * ROWS == row, rank, 0.0), axis=0,
                keepdims=True) - 1.0
        for k in range(7)
    ]
    src = jnp.concatenate(sources + [sources[0]], axis=0)
    keys = key.astype(F32)
    eight = iota((8, ROWS), 0)
    local_ref[...] = jnp.where(eight < 7, src, keys)
    away = jnp.max(jnp.where(src < 0.0, 1.0, 0.0), axis=0, keepdims=True)
    away = jnp.sum(jnp.where(eight.astype(F32) == keys, away, 0.0), axis=1, keepdims=True)
    name = jnp.where((src >= 0.0) & (keys == 1.0), set_name(src), 99.0)
    read = jnp.zeros((8, ROWS), F32)
    for k in range(7):
        read = read + jnp.where(name[k:k + 1, :] == eight.astype(F32), 1.0, 0.0)
    read = jnp.sum(read, axis=1, keepdims=True)
    flag_v[...] = jnp.where(iota((8, 128), 1) < 64, away, read).astype(jnp.int32)
    src_v[:, :PAD] = sorted_slots(src, sel)
    src_v[:, PAD:] = jnp.zeros((8, 128 - PAD), jnp.int32)
    mask_ref[...] = own_mask(src, keys, sel)
    to_smem = load_all(((order_v, order_ref), (src_v, src_ref), (flag_v, flag_s),
                        (local_ref, local_hbm), (flag_v, flags_hbm), (sel_ref, sel_hbm)),
                       sems.at[pl.ds(4, 6)])
    begin(to_smem)
    finished(to_smem)

    def keep(c, s):
        rows = pl.ds(s * FS, FS)
        return pltpu.make_async_copy(
            rows_ref.at[rows, quarter(c)], a_rows_hbm.at[rows, quarter(c)], keep_sems.at[c, s])

    def keep_next(c):
        return pltpu.make_async_copy(
            rows_ref.at[pl.ds(HALF, HALF), quarter(c)], a_next_hbm.at[:, quarter(c)],
            keep_sems.at[c, SETS])

    def later(s):
        return (flag_s[s + 1, 0] != 0) | (s == 0)

    t_refs = (t0, t1, t2, t3)

    def step(c, carry):
        fetch(c).wait()
        for a in range(CHUNK):
            zero = jnp.zeros((B, ROWS), BF16)
            x = [a_ref[k, c * CHUNK + a] for k in range(7)] + [zero]
            for h in range(4):
                pair = jnp.concatenate(x[2 * h:2 * h + 2], axis=0)
                t_refs[h][a * STRIDE:a * STRIDE + ROWS, :] = jnp.transpose(pair).astype(F32)
        for i in range(ROWS):
            rows_ref[i, quarter(c), :] = jnp.concatenate(
                [t[pl.ds(order_ref[0, i], CHUNK, stride=STRIDE), :] for t in t_refs], axis=1
            ).astype(BF16)

        def store(s, carry):
            @pl.when(later(s))
            def _():
                keep(c, s).start()
            return carry

        keep_next(c).start()
        return lax.fori_loop(0, SETS, store, carry)

    lax.fori_loop(0, QUARTERS, step, 0)
    load.wait()

    def store(s):
        rows = pl.ds(s * KG, KG)
        return pltpu.make_async_copy(blocks_ref.at[rows], out_hbm.at[rows], out_sems.at[s])

    def work(s, carry):
        @pl.when(flag_s[s + 1, 0] == 0)
        def _():
            one_set(s, set_base, src_ref, c_cols_ref, mask_ref, rows_ref, pool_ref, merged_ref,
                    place_ref, blocks_ref)
            store(s).start()
        return carry

    lax.fori_loop(1, SETS, work, 0)

    def end(s, carry):
        @pl.when(later(s))
        def _():
            finished([keep(c, s) for c in range(QUARTERS)])

        @pl.when(jnp.logical_not(later(s)))
        def _():
            store(s).wait()
        return carry

    lax.fori_loop(0, SETS, end, 0)
    finished([keep_next(c) for c in range(QUARTERS)])


def operator(c_cols_t, cols_t, a_cols_t, a_t, pool):
    return call(
        operator_kernel, "operator", [HBM] * 4 + [ANY],
        [((ROWS, B, 8 * B), BF16), ((HALF, B, 8 * B), BF16), ((SETS * KG, 8, B, B), BF16), ((8, ROWS), F32),
         ((8, 128), jnp.int32), ((PAD, ROWS), BF16)],
        [
            pltpu.SMEM((8, SETS * KG), jnp.int32),
            pltpu.VMEM((3, ROWS), jnp.int32),
            pltpu.VMEM((7, ROWS), jnp.int32),
            pltpu.VMEM((7, B, B, ROWS), BF16),
            pltpu.VMEM((ROWS, B, 8 * B), BF16),
            pltpu.VMEM((ROWS, B, KG * B), BF16),
            pltpu.VMEM((SETS * KG, 8, B, B), BF16),
            pltpu.VMEM((FS * B, 8 * B), BF16),
            pltpu.VMEM((PAD, 8 * B), F32),
            pltpu.VMEM((8, ROWS), F32),
            pltpu.VMEM((PAD, ROWS), BF16),
            pltpu.VMEM((8, 128), jnp.int32),
            pltpu.VMEM((8, 128), jnp.int32),
            pltpu.VMEM((8, 128), jnp.int32),
            pltpu.SMEM((8, 128), jnp.int32),
            pltpu.SMEM((8, 128), jnp.int32),
            pltpu.SMEM((8, 128), jnp.int32),
            pltpu.SMEM((KG, 8), jnp.int32),
        ] + [pltpu.VMEM((CHUNK * STRIDE, 128), F32)] * 4 + [
            pltpu.SemaphoreType.DMA((QUARTERS,)),
            pltpu.SemaphoreType.DMA((10,)),
            pltpu.SemaphoreType.DMA((QUARTERS, SETS + 1)),
            pltpu.SemaphoreType.DMA((SETS,)),
        ],
        4_000_000_000, 18_000_000, 53,
    )(c_cols_t, cols_t, a_cols_t, a_t, pool)


def pool_copies(parts, pool_ref, sems):
    copies = []
    start = ROWS
    for n, part in enumerate(parts):
        rows = (part.shape[0] - 1) // QUARTERS
        for c in range(QUARTERS):
            copies.append(pltpu.make_async_copy(
                part.at[pl.ds(c * rows, rows)],
                pool_ref.at[pl.ds(start, rows), pl.ds(c * CHUNK, CHUNK)],
                sems.at[n, c],
            ))
        start += rows
    return copies


def straddle_kernel(a_cols_hbm, local_hbm, flags_hbm, sel_hbm, a_next_hbm, pool_hbm, *refs):
    parts = refs[:4]
    (out_hbm, src_hbm, mask_hbm, a_cols_ref, local_ref, flag_ref, sel_ref, pool_ref, rows_ref,
     names_ref, merged_ref, partial_ref, mask_ref, src_v, src_ref, sems, pool_sems, small_sems) = refs[4:]
    small = load_all(
        [(flags_hbm, flag_ref), (a_cols_hbm, a_cols_ref), (local_hbm, local_ref), (sel_hbm, sel_ref)]
        + [(part.at[part.shape[0] - 1], names_ref.at[n]) for n, part in enumerate(parts)], small_sems)
    begin(small)
    loads = pool_copies(parts, pool_ref, sems)
    loads.append(pltpu.make_async_copy(a_next_hbm, rows_ref, small_sems.at[8]))
    begin(loads)
    finished(small)
    ids = devices()

    def unit(u):
        first, rows = (0, 7) if u == 0 else (7, 7) if u == 1 else ((u - 1) * FS, FS)
        return pltpu.make_async_copy(
            pool_hbm.at[pl.ds(first, rows)], pool_ref.at[pl.ds(first, rows)], pool_sems.at[u])

    def read(u):
        return (flag_ref[u, 64] != 0) | (u == 1)

    for u in range(7):
        @pl.when(read(u))
        def _(u=u):
            unit(u).start()

    shifts = (((70, 84, 84 - 70),), ((56, 70, 98 - 56),), ((7, 14, 112 - 7),),
              ((0, 7, 119), (14, 28, 126 - 14)))
    near = ((64, 88), (56, 72), (0, 16), (0, 32))
    found = [jnp.zeros((1, ROWS), F32)] * 7
    for n in range(4):
        low, high = near[n]
        column = jnp.transpose(names_ref[n][:, :128].astype(F32))[low:high, 0:1].astype(jnp.int32)
        row = iota((high - low, 1), 0) + low
        slot = jnp.zeros((high - low, 1), jnp.int32)
        for first, last, shift in shifts[n]:
            slot = jnp.where((row >= first) & (row < last), row + shift + 1, slot)
        column = jnp.where(slot > 0, column + ids[n + 1] * ROWS, -1)
        slot = slot.astype(F32)
        for k in range(7):
            found[k] = found[k] + jnp.sum(
                jnp.where(a_cols_ref[k:k + 1, :] == column, slot, 0.0), axis=0, keepdims=True)
    local = local_ref[...]
    away = jnp.concatenate(found + [found[0]], axis=0) - 1.0
    src = jnp.where(local >= 0.0, local, away)
    src = jnp.where(iota((8, ROWS), 0) < 7, src, jnp.broadcast_to(src[0:1, :], (8, ROWS)))
    sel = sel_ref[...]
    src_v[:, :PAD] = sorted_slots(src, sel)
    src_v[:, PAD:] = jnp.zeros((8, 128 - PAD), jnp.int32)
    out = load_all(((src_v, src_ref), (src_v, src_hbm), (mask_ref, mask_hbm)),
                   small_sems.at[pl.ds(9, 3)])
    begin(out[:2])
    mask_ref[...] = own_mask(src, local[7:8, :], sel)
    out[2].start()
    finished(out[:1] + loads)
    for u in range(7):
        @pl.when(read(u))
        def _(u=u):
            unit(u).wait()
    for i in range(HALF):
        merge_row(i, i, HALF + i, src_ref, mask_ref, rows_ref, pool_ref, merged_ref)
    own = pool_ref[HALF:FS].reshape(HALF * B, KG * B)
    partial_ref[...] = tn(own, merged_ref[...]).astype(BF16)
    last = pltpu.make_async_copy(partial_ref, out_hbm, small_sems.at[12])
    last.start()
    finished(out[1:] + [last])


def straddle(a_cols_t, local, flags, sel, a_next, pool, parts):
    return call(
        straddle_kernel, "straddle", [HBM] + [ANY] * 9,
        [((KG * B, 8 * B), BF16), ((8, 128), jnp.int32), ((PAD, 8 * B), F32)],
        [
            pltpu.VMEM((7, ROWS), jnp.int32),
            pltpu.VMEM((8, ROWS), F32),
            pltpu.SMEM((8, 128), jnp.int32),
            pltpu.VMEM((PAD, ROWS), BF16),
            pltpu.VMEM((POOL, B, KG * B), BF16),
            pltpu.VMEM((HALF, B, 8 * B), BF16),
            pltpu.VMEM((4, 16, KG * B), BF16),
            pltpu.VMEM((HALF * B, 8 * B), BF16),
            pltpu.VMEM((KG * B, 8 * B), BF16),
            pltpu.VMEM((PAD, 8 * B), F32),
            pltpu.VMEM((8, 128), jnp.int32),
            pltpu.SMEM((8, 128), jnp.int32),
            pltpu.SemaphoreType.DMA((4, QUARTERS)),
            pltpu.SemaphoreType.DMA((7,)),
            pltpu.SemaphoreType.DMA((13,)),
        ],
        300_000_000, 6_000_000, 14,
    )(a_cols_t, local, flags, sel, a_next, pool, *parts)


def sets_kernel(src_hbm, flags_hbm, c_cols_hbm, mask_hbm, a_rows_hbm, pool_hbm, *refs):
    parts = refs[:4]
    (_, out_hbm, first_hbm, src_ref, flag_ref, c_cols_ref, mask_ref, first_ref, pool_ref, rows_ref,
     blocks_ref, merged_ref, place_ref, small_sems, sems, row_sems, out_sems) = refs[4:]
    small = load_all(((flags_hbm, flag_ref), (src_hbm, src_ref), (c_cols_hbm, c_cols_ref),
                      (mask_hbm, mask_ref)), small_sems)
    begin(small)
    loads = pool_copies(parts, pool_ref, sems) + [
        pltpu.make_async_copy(pool_hbm, pool_ref.at[pl.ds(0, ROWS)], small_sems.at[4])]
    set_base = devices()[0] * SETS

    def fetch(s):
        rows = pl.ds(s * FS, FS)
        return pltpu.make_async_copy(a_rows_hbm.at[rows], rows_ref.at[rows], row_sems.at[s])

    def store(s):
        rows = pl.ds(s * KG, KG)
        return pltpu.make_async_copy(blocks_ref.at[rows], out_hbm.at[rows], out_sems.at[s])

    def here(s):
        return flag_ref[s + 1, 0] != 0

    fetch(0).start()
    begin(loads)
    finished(small)
    for s in range(1, SETS):
        @pl.when(here(s))
        def _(s=s):
            fetch(s).start()
    fetch(0).wait()
    finished(loads)
    for i in range(HALF):
        merge_row(i, i, i, src_ref, mask_ref, rows_ref, pool_ref, merged_ref)
    own = pool_ref[:HALF].reshape(HALF * B, KG * B)
    first_ref[...] = tn(own, merged_ref[:HALF * B, :])
    first = pltpu.make_async_copy(first_ref, first_hbm, small_sems.at[5])
    first.start()

    def work(s, carry):
        @pl.when(here(s))
        def _():
            fetch(s).wait()
            one_set(s, set_base, src_ref, c_cols_ref, mask_ref, rows_ref, pool_ref, merged_ref,
                    place_ref, blocks_ref)
            store(s).start()
        return carry

    lax.fori_loop(1, SETS, work, 0)

    def end(s, carry):
        @pl.when(here(s))
        def _():
            store(s).wait()
        return carry

    lax.fori_loop(1, SETS, end, 0)
    first.wait()


def sets(src, flags, c_cols_t, mask, a_rows, pool, parts, whole):
    return call(
        sets_kernel, "sets", [ANY] * 2 + [HBM] + [ANY] * 8,
        [((SETS * KG, 8, B, B), BF16), ((KG * B, 8 * B), F32)],
        [
            pltpu.SMEM((8, 128), jnp.int32),
            pltpu.SMEM((8, 128), jnp.int32),
            pltpu.SMEM((8, SETS * KG), jnp.int32),
            pltpu.VMEM((PAD, 8 * B), F32),
            pltpu.VMEM((KG * B, 8 * B), F32),
            pltpu.VMEM((POOL, B, KG * B), BF16),
            pltpu.VMEM((ROWS, B, 8 * B), BF16),
            pltpu.VMEM((SETS * KG, 8, B, B), BF16),
            pltpu.VMEM((FS * B, 8 * B), BF16),
            pltpu.SMEM((KG, 8), jnp.int32),
            pltpu.SemaphoreType.DMA((6,)),
            pltpu.SemaphoreType.DMA((4, QUARTERS)),
            pltpu.SemaphoreType.DMA((SETS,)),
            pltpu.SemaphoreType.DMA((SETS,)),
        ],
        2_500_000_000, 12_000_000, 48, aliases={10: 0},
    )(src, flags, c_cols_t, mask, a_rows, pool, *parts, whole)


def finish_kernel(c_cols_hbm, first_hbm, incoming_hbm, _, out_hbm, c_cols_ref, first_ref, incoming_ref,
                  blocks_ref, place_ref, sems):
    loads = load_all(((c_cols_hbm, c_cols_ref), (first_hbm, first_ref), (incoming_hbm, incoming_ref)),
                     sems)
    begin(loads)
    finished(loads[:1])
    order_slots(c_cols_ref, devices()[0] * SETS, 0, place_ref)
    finished(loads[1:])
    store_blocks(first_ref[...] + incoming_ref[...].astype(F32), 0, place_ref, blocks_ref)
    copy = pltpu.make_async_copy(blocks_ref, out_hbm.at[pl.ds(0, KG)], sems.at[3])
    copy.start()
    copy.wait()


def finish(c_cols_t, first, incoming, whole):
    return call(
        finish_kernel, "finish", [HBM] + [ANY] * 3, [((SETS * KG, 8, B, B), BF16)],
        [
            pltpu.SMEM((8, SETS * KG), jnp.int32),
            pltpu.VMEM((KG * B, 8 * B), F32),
            pltpu.VMEM((KG * B, 8 * B), BF16),
            pltpu.VMEM((KG, 8, B, B), BF16),
            pltpu.SMEM((KG, 8), jnp.int32),
            pltpu.SemaphoreType.DMA((4,)),
        ],
        1_000_000, 1_500_000, 6, aliases={3: 0},
    )(c_cols_t, first, incoming, whole)[0]


def shards(a_blocks, a_cols, p_blocks, p_cols, c_cols):
    cols_t, a_cols_t, c_cols_t = p_cols.T, a_cols.T, c_cols.T
    moves = (("dom", 1), ("dom", -1), ("sub", 1), ("sub", -1))
    pool, *sends = prolong(cols_t, p_blocks.transpose(1, 2, 3, 0))
    parts = [passed_along(rows, axis, step) for rows, (axis, step) in zip(sends, moves)]
    a_rows, a_next, whole, local, flags, sel = operator(
        c_cols_t, cols_t, a_cols_t, a_blocks.transpose(1, 2, 3, 0), pool)
    partial, src, mask = straddle(a_cols_t, local, flags, sel, a_next, pool, parts)
    incoming = passed_along(partial, "sub", 1)
    whole, first = sets(src, flags, c_cols_t, mask, a_rows, pool, parts, whole)
    return finish(c_cols_t, first, incoming, whole)


def solution(mesh):
    spec4 = P(("dom", "sub"), None, None, None)
    spec2 = P(("dom", "sub"), None)
    return jax.shard_map(
        shards, mesh=mesh, in_specs=(spec4, spec2, spec4, spec2, spec2), out_specs=spec4,
        check_vma=False,
    )
```

time: 48.1 us -> 43.2 us (0.90)
  Pallas kernels: 33.3 us -> 26.5 us
  waiting for transfers between devices: 4.89 us -> 9.33 us
  local copies, waits for them, and re-layouts: 2.26 us -> 0.02 us
    pallas_call x5, Pallas kernels: 33.3 us -> 26.5 us  [the longest x1 8.67 us: operator(): call(operator_kernel, 'operator', [HBM] * 4 + [ANY], [((ROWS, B, 8 * B),...]
    ppermute x5, waiting for transfers between devices: 4.89 us -> 9.33 us  [passed_along(): lax.ppermute(block, axis, [((i - distance) % n, i) for i in range(n)])]
    unnamed x10 -> x8, local copies, waits for them, and re-layouts: 1.59 us -> 0.02 us
    another operation x1 -> x0, local copies, waits for them, and re-layouts: 0.67 us -> none  [shards(): jnp.stack([device, (dom + dom_count - 1) % dom_count * sub_count + sub, (...]
  transfers between devices with their start and end apart: 5 -> 5, of which waited for: 3 -> 3; matrix products, arithmetic and copies ran while one was open for 1% -> 0% of each run, Pallas kernels for 40% -> 35%
where the time goes in v3:
time: 43.2 us; the launch traced here: 43 us
  Pallas kernels  26.5 us (61%)
  waiting for transfers between devices  9.33 us (22%)
  starting transfers between devices  7.11 us (16%)
    ppermute x5, waiting for transfers between devices, passed_along(): lax.ppermute(block, axis, [((i - distance) % n, i) for i in range(n)])  9.33 us
    pallas_call x1, Pallas kernels, operator(): call(operator_kernel, 'operator', [HBM] * 4 + [ANY], [((ROWS, B, 8 * B),...  8.67 us
    ppermute x5, starting transfers between devices, passed_along(): lax.ppermute(block, axis, [((i - distance) % n, i) for i in range(n)])  7.11 us
    pallas_call x1, Pallas kernels, prolong(): call(prolong_kernel, 'prolong', [pl.BlockSpec((3, ROWS), lambda c: (0, 0)...  6.54 us
    pallas_call x1, Pallas kernels, sets(): call(sets_kernel, 'sets', [ANY] * 2 + [HBM] + [ANY] * 8, [((SETS * KG, 8,...  6.52 us
    pallas_call x1, Pallas kernels, straddle(): call(straddle_kernel, 'straddle', [HBM] + [ANY] * 9, [((KG * B, 8 * B), B...  2.96 us
    pallas_call x1, Pallas kernels, finish(): call(finish_kernel, 'finish', [HBM] + [ANY] * 3, [((SETS * KG, 8, B, B),...  1.76 us
  transfers between devices with their start and end apart: 5, of which 3 were waited for; matrix products, arithmetic and copies ran while one was open for 0% of the time, Pallas kernels for 35%

profile of v3, /device:TPU:96, one launch (start us, length us, event | category | flops | bytes accessed | tf_op | source)
XLA Modules:
  0.0 43.0 jit_solution(1824397656679185152)
XLA Ops:
  0.0 0.0 copy-start.1
  0.0 0.0 copy-start.2
  0.0 0.0 copy-start.3
  0.0 6.5 %prolong.1 = (bf16[84,64,256]{2,1,0:T(8,128)(2,1)}, bf16[57,16,256]{2,1,0:T(8,128)(2,1)}, bf16[57,16,256]{2,1,0:T(8,128)(2,1)}, bf16[29,16,256]{2,1,0:T(8,128)(2,1)}, bf16[85,16,256]{2,1,0:T(8,128)(2,1)}) custom-call(s32[3,84]{1,0:T(4,128)} %bitcast.10, bf16[3,64,64,84]{3,2,1,0:T(8,128)(2,1)} %bitcast.13), custom_call_target="tpu_custom_call" | custom-call | flops 6000000000 | bytes 8000000 | tf_op jit(solution)/shard_map/prolong/pallas_call | solution.py:179
  6.6 5.3 %collective-permute-start.3 = (bf16[85,16,256]{2,1,0:T(8,128)(2,1)}, bf16[85,16,256]{2,1,0:T(8,128)(2,1)S(1)}, u32[]{:S(2)}, u32[]{:S(2)}) collective-permute-start(bf16[85,16,256]{2,1,0:T(8,128)(2,1)} %get-tuple-element.29), channel_id=1, source_target_pairs={{1,0},{2,1},{3,2},{4,3},{5,4},{6,5},{7,6},{8,7},{9,8},{10,9},{11,1... | collective-permute-start | bytes 2088968 | tf_op jit(solution)/shard_map/ppermute | solution.py:22
  11.8 0.0 collective-permute-start
  11.8 1.7 %collective-permute-start.1 = (bf16[57,16,256]{2,1,0:T(8,128)(2,1)}, bf16[57,16,256]{2,1,0:T(8,128)(2,1)S(1)}, u32[]{:S(2)}, u32[]{:S(2)}) collective-permute-start(bf16[57,16,256]{2,1,0:T(8,128)(2,1)} %get-tuple-element.27), channel_id=1, source_target_pairs={{16,0},{32,16},{48,32},{64,48},{80,64},{96,80},{112,96},{128,112},... | collective-permute-start | bytes 1400840 | tf_op jit(solution)/shard_map/ppermute | solution.py:22
  13.6 0.0 collective-permute-start.2
  13.6 0.0 copy-done.1
  13.6 0.0 copy-done.2
  13.6 0.0 copy-done.3
  13.6 0.0 copy-start
  13.6 8.7 %operator.1 = (bf16[84,64,512]{2,1,0:T(8,128)(2,1)}, bf16[7,64,512]{2,1,0:T(8,128)(2,1)S(1)}, bf16[24,8,64,64]{3,2,1,0:T(8,128)(2,1)}, f32[8,84]{1,0:T(8,128)S(1...) custom-call(s32[8,24]{1,0:T(8,128)S(1)} %bitcast.5, s32[3,84]{1,0:T(4,128)S(1)} %bitcast.11, s32[7,84]{1,0:T(8,128)S(1)} %bitcast.8, ...), custom_call_target="tpu_custom_call" | custom-call | flops 4000000000 | bytes 18000000 | tf_op jit(solution)/shard_map/operator/pallas_call | solution.py:374
  22.3 3.0 %collective-permute-done.2.refs_2_ = bf16[29,16,256]{2,1,0:T(8,128)(2,1)S(1)} collective-permute-done((bf16[29,16,256]{2,1,0:T(8,128)(2,1)}, bf16[29,16,256]{2,1,0:T(8,128)(2,1)S(1)}, u32[]{:S(2)}, u32[]{:S(2)}) %collective-permute-start.2) | collective-permute-done | bytes 237600 | tf_op jit(solution)/shard_map/ppermute | solution.py:22
  25.3 0.0 collective-permute-done.refs_0_
  25.3 0.0 collective-permute-done.1.refs_1_
  25.3 1.7 %collective-permute-done.3.refs_3_ = bf16[85,16,256]{2,1,0:T(8,128)(2,1)S(1)} collective-permute-done((bf16[85,16,256]{2,1,0:T(8,128)(2,1)}, bf16[85,16,256]{2,1,0:T(8,128)(2,1)S(1)}, u32[]{:S(2)}, u32[]{:S(2)}) %collective-permute-start.3) | collective-permute-done | bytes 696352 | tf_op jit(solution)/shard_map/ppermute | solution.py:22
  27.0 0.0 copy-done
  27.0 3.0 %straddle.1 = (bf16[256,512]{1,0:T(8,128)(2,1)S(1)}, s32[8,128]{1,0:T(8,128)S(1)}, f32[88,512]{1,0:T(8,128)S(1)}) custom-call(s32[7,84]{1,0:T(8,128)S(1)} %bitcast.9, f32[8,84]{1,0:T(8,128)S(1)} %get-tuple-element.22.local_hbm, s32[8,128]{1,0:T(8,128)S(1)} %get-tuple-element.23.flags_hbm, bf16[88,84]{1,0:T(8,128)(2,1)S(1)} %get-tuple-element.24.sel_hbm, ...), custom_call_target="tpu_custom_call" | custom-call | flops 300000000 | bytes 6000000 | tf_op jit(solution)/shard_map/straddle/pallas_call | solution.py:492
  30.0 0.1 collective-permute-start.4
  30.1 6.5 %sets.1 = (bf16[24,8,64,64]{3,2,1,0:T(8,128)(2,1)}, f32[256,512]{1,0:T(8,128)S(1)}) custom-call(s32[8,128]{1,0:T(8,128)S(1)} %get-tuple-element.30.src_hbm, s32[8,128]{1,0:T(8,128)S(1)} %get-tuple-element.23.flags_hbm, s32[8,24]{1,0:T(8,128)S(1)} %bitcast.6, f32[88,512]{1,0:T(8,128)S(1)} %get-tuple-element.31.mask_hbm, ...), custom_call_target="tpu_custom_call", output_to_operand_aliasing={{0}: (10, {})} | custom-call | flops 2500000000 | bytes 12000000 | tf_op jit(solution)/shard_map/sets/pallas_call | solution.py:576
  36.6 4.6 %collective-permute-done.4.incoming_hbm = bf16[256,512]{1,0:T(8,128)(2,1)S(1)} collective-permute-done((bf16[256,512]{1,0:T(8,128)(2,1)S(1)}, bf16[256,512]{1,0:T(8,128)(2,1)S(1)}, u32[]{:S(2)}, u32[]{:S(2)}) %collective-permute-start.4) | collective-permute-done | bytes 262176 | tf_op jit(solution)/shard_map/ppermute | solution.py:22
  41.2 1.8 %finish.1 = bf16[24,8,64,64]{3,2,1,0:T(8,128)(2,1)} custom-call(s32[8,24]{1,0:T(8,128)S(1)} %bitcast.7, f32[256,512]{1,0:T(8,128)S(1)} %get-tuple-element.34.first_hbm, bf16[256,512]{1,0:T(8,128)(2,1)S(1)} %collective-permute-done.4.incoming_hbm, bf16[24,8,64,64]{3,2,1,0:T(8,128)(2,1)} %get-tuple-element.36._), custom_call_target="tpu_custom_call", output_to_operand_aliasing={{}: (3, {})} | custom-call | flops 1000000 | bytes 1500000 | tf_op jit(solution)/shard_map/finish/pallas_call | solution.py:614
Async XLA Ops:
  0.0 13.6 %copy-start.1 = (s32[24,8]{0,1:T(8,128)S(1)}, s32[24,8]{0,1:T(8,128)}, u32[]{:S(2)}) copy-start(s32[24,8]{0,1:T(8,128)} %param.9) | copy-start | bytes 2308
  0.0 13.6 %copy-start.2 = (s32[84,7]{0,1:T(8,128)S(1)}, s32[84,7]{0,1:T(8,128)}, u32[]{:S(2)}) copy-start(s32[84,7]{0,1:T(8,128)} %param.6) | copy-start | bytes 7060
  0.0 13.6 %copy-start.3 = (s32[84,3]{0,1:T(4,128)S(1)}, s32[84,3]{0,1:T(4,128)}, u32[]{:S(2)}) copy-start(s32[84,3]{0,1:T(4,128)} %param.8) | copy-start | bytes 3028
  6.6 20.5 %collective-permute-start.3 = (bf16[85,16,256]{2,1,0:T(8,128)(2,1)}, bf16[85,16,256]{2,1,0:T(8,128)(2,1)S(1)}, u32[]{:S(2)}, u32[]{:S(2)}) collective-permute-start(bf16[85,16,256]{2,1,0:T(8,128)(2,1)} %get-tuple-element.29), channel_id=1, source_target_pairs={{1,0},{2,1},{3,2},{4,3},{5,4},{6,5},{7,6},{8,7},{9,8},{10,9},{11,1... | collective-permute-start | bytes 2088968 | tf_op jit(solution)/shard_map/ppermute | solution.py:22
  11.8 13.5 %collective-permute-start = (bf16[57,16,256]{2,1,0:T(8,128)(2,1)}, bf16[57,16,256]{2,1,0:T(8,128)(2,1)S(1)}, u32[]{:S(2)}, u32[]{:S(2)}) collective-permute-start(bf16[57,16,256]{2,1,0:T(8,128)(2,1)} %get-tuple-element.26), channel_id=1, source_target_pairs={{240,0},{0,16},{16,32},{32,48},{48,64},{64,80},{80,96},{96,112},{1... | collective-permute-start | bytes 1400840 | tf_op jit(solution)/shard_map/ppermute | solution.py:22
  11.8 13.5 %collective-permute-start.1 = (bf16[57,16,256]{2,1,0:T(8,128)(2,1)}, bf16[57,16,256]{2,1,0:T(8,128)(2,1)S(1)}, u32[]{:S(2)}, u32[]{:S(2)}) collective-permute-start(bf16[57,16,256]{2,1,0:T(8,128)(2,1)} %get-tuple-element.27), channel_id=1, source_target_pairs={{16,0},{32,16},{48,32},{64,48},{80,64},{96,80},{112,96},{128,112},... | collective-permute-start | bytes 1400840 | tf_op jit(solution)/shard_map/ppermute | solution.py:22
  13.6 11.7 %collective-permute-start.2 = (bf16[29,16,256]{2,1,0:T(8,128)(2,1)}, bf16[29,16,256]{2,1,0:T(8,128)(2,1)S(1)}, u32[]{:S(2)}, u32[]{:S(2)}) collective-permute-start(bf16[29,16,256]{2,1,0:T(8,128)(2,1)} %get-tuple-element.28), channel_id=1, source_target_pairs={{15,0},{0,1},{1,2},{2,3},{3,4},{4,5},{5,6},{6,7},{7,8},{8,9},{9,10... | collective-permute-start | bytes 712712 | tf_op jit(solution)/shard_map/ppermute | solution.py:22
  13.6 13.4 %copy-start = (bf16[84,64,256]{2,1,0:T(8,128)(2,1)S(1)}, bf16[84,64,256]{2,1,0:T(8,128)(2,1)}, u32[]{:S(2)}) copy-start(bf16[84,64,256]{2,1,0:T(8,128)(2,1)} %get-tuple-element.21.pool_hbm) | copy-start | bytes 8257540
  30.0 11.2 %collective-permute-start.4 = (bf16[256,512]{1,0:T(8,128)(2,1)S(1)}, bf16[256,512]{1,0:T(8,128)(2,1)S(1)}, u32[]{:S(2)}, u32[]{:S(2)}) collective-permute-start(bf16[256,512]{1,0:T(8,128)(2,1)S(1)} %get-tuple-element.35), channel_id=1, source_target_pairs={{15,0},{0,1},{1,2},{2,3},{3,4},{4,5},{5,6},{6,7},{7,8},{8,9},{9,10... | collective-permute-start | bytes 786440 | tf_op jit(solution)/shard_map/ppermute | solution.py:22

commit v4 on v3

--- a/solution.py
+++ b/solution.py
@@ -29,7 +29,10 @@
 QUARTERS = 4
 CHUNK = B // QUARTERS
 STRIDE = 89
-SENDS = (((70, 14),), ((56, 14),), ((7, 7),), ((0, 7), (14, 14)))
+SENDS = (((70, 14),), ((56, 14),), ((7, 7),))
+BACK = HALF + FS
+NARROW = BACK + (BACK + 1) // 2
+AFTER = POOL - BACK
 ANY = pl.BlockSpec(memory_space=pl.ANY)
 HBM = pl.BlockSpec(memory_space=pltpu.HBM)
 
@@ -127,27 +130,43 @@
 
 
 def prolong_kernel(cols_ref, p_ref, pool_hbm, up_hbm, down_hbm, fore_hbm, back_hbm,
-                   sel_ref, pool_ref, ids_ref, t0_ref, t1_ref, out_sems, id_sems):
+                   sel_ref, back_sel_ref, pool_ref, back_ref, ids_ref, back_ids_ref,
+                   t0_ref, t1_ref, t2_ref, t3_ref, out_sems, id_sems):
     c = pl.program_id(0)
-    sends = (up_hbm, down_hbm, fore_hbm, back_hbm)
+    sends = (up_hbm, down_hbm, fore_hbm)
 
     def stores(c):
         whole = pltpu.make_async_copy(
             pool_ref.at[:, quarter(c)], pool_hbm.at[:, quarter(c)], out_sems.at[c, 5])
-        return send_copies(c, pool_ref, sends, out_sems) + [whole]
+        rows = pl.ds(c * NARROW, NARROW)
+        back = pltpu.make_async_copy(back_ref.at[rows], back_hbm.at[rows], out_sems.at[c, 4])
+        return [back] + send_copies(c, pool_ref, sends, out_sems) + [whole]
 
     id_copies = [pltpu.make_async_copy(ids_ref, ref.at[ref.shape[0] - 1], id_sems.at[n])
                  for n, ref in enumerate(sends)]
+    id_copies.append(pltpu.make_async_copy(
+        back_ids_ref, back_hbm.at[back_hbm.shape[0] - 1], id_sems.at[3]))
 
     @pl.when(c == 0)
     def _():
-        sel = selector(ranks(groups(cols_ref[0:1, :], devices()[0] * SETS)))
+        rank = ranks(groups(cols_ref[0:1, :], devices()[0] * SETS))
+        sel = selector(rank)
         sel_ref[...] = sel
+        back_rank = jnp.where(rank < 7.0, rank, jnp.where((rank >= 14.0) & (rank < 28.0), rank - 7.0, 99.0))
+        back_sel_ref[...] = jnp.where(
+            back_rank.astype(jnp.int32) == iota((32, ROWS), 0), 1.0, 0.0).astype(BF16)
+        notes = iota((16, ROWS), 1)
+        for q in range(3):
+            notes = jnp.where(iota((16, ROWS), 0) == q + 1, cols_ref[q:q + 1, :] & 3, notes)
+        notes = nt(notes.astype(F32).astype(BF16), sel).astype(BF16)
         ids_ref[...] = jnp.zeros((16, KG * B), BF16)
-        ids_ref[:, :PAD] = sorted_order(sel).astype(BF16)
+        ids_ref[:, :PAD] = notes
+        back_ids_ref[...] = jnp.zeros((16, 128), BF16)
+        back_ids_ref[:, :PAD] = notes
         begin(id_copies)
 
     sel = sel_ref[...]
+    back_sel = back_sel_ref[...]
     place = cols_ref[...] & 3
     weights = [
         [jnp.where(place[q:q + 1, :] == r, 1.0, 0.0).astype(BF16) for q in range(3)]
@@ -159,6 +178,16 @@
         t = nt(sel, jnp.concatenate(y, axis=0))
         t0_ref[b * STRIDE:b * STRIDE + PAD, :] = t[:, :128]
         t1_ref[b * STRIDE:b * STRIDE + PAD, :] = t[:, 128:]
+        t = nt(back_sel, jnp.concatenate(x + [x[2]], axis=0))
+        t2_ref[b * 33:b * 33 + 32, :] = t[:, :128]
+        t3_ref[b * 33:b * 33 + 32, :] = t[:, 128:]
+    left = iota((CHUNK, 128), 1) < B
+    for m in range(BACK):
+        back_ref[c * NARROW + m] = t2_ref[pl.ds(m, CHUNK, stride=33), :].astype(BF16)
+    for m in range(0, BACK, 2):
+        back_ref[c * NARROW + BACK + m // 2] = jnp.where(
+            left, t3_ref[pl.ds(m, CHUNK, stride=33), :], t3_ref[pl.ds(m + 1, CHUNK, stride=33), :]
+        ).astype(BF16)
     for i in range(ROWS):
         pool_ref[i, quarter(c), :] = jnp.concatenate(
             [t[pl.ds(i, CHUNK, stride=STRIDE), :] for t in (t0_ref, t1_ref)], axis=1
@@ -180,13 +209,19 @@
         prolong_kernel, "prolong",
         [pl.BlockSpec((3, ROWS), lambda c: (0, 0)),
          pl.BlockSpec((3, CHUNK, B, ROWS), lambda c: (0, c, 0, 0))],
-        [((ROWS, B, KG * B), BF16), rows(14), rows(14), rows(7), rows(21)],
+        [((ROWS, B, KG * B), BF16), rows(14), rows(14), rows(7),
+         ((QUARTERS * NARROW + 1, CHUNK, 128), BF16)],
         [
             pltpu.VMEM((PAD, ROWS), BF16),
+            pltpu.VMEM((32, ROWS), BF16),
             pltpu.VMEM((ROWS, B, KG * B), BF16),
+            pltpu.VMEM((QUARTERS * NARROW, CHUNK, 128), BF16),
             pltpu.VMEM((16, KG * B), BF16),
+            pltpu.VMEM((16, 128), BF16),
             pltpu.VMEM((CHUNK * STRIDE, 128), F32),
             pltpu.VMEM((CHUNK * STRIDE, 128), F32),
+            pltpu.VMEM((CHUNK * 33, 128), F32),
+            pltpu.VMEM((CHUNK * 33, 128), F32),
             pltpu.SemaphoreType.DMA((QUARTERS, 6)),
             pltpu.SemaphoreType.DMA((4,)),
         ],
@@ -225,25 +260,24 @@
     merged_ref[place * B:place * B + B, KG * B:] = merged[B:]
 
 
-def order_slots(c_cols_ref, set_id, first_row, place_ref):
-    for r in range(KG):
-        for s in range(8):
-            c = c_cols_ref[s, first_row + r]
-            u = (c & 3) + jnp.where((c >> 2) == set_id, 0, 4)
-            place_ref[r, u] = s
+def slot_places(c_cols, set_base):
+    row = iota(c_cols.shape, 1)
+    u = (c_cols & 3) + jnp.where((c_cols >> 2) == set_base + (row >> 2), 0, 4)
+    place = jnp.zeros(c_cols.shape, jnp.int32)
+    for slot in range(8):
+        place = place + jnp.where(u[slot:slot + 1, :] == iota(c_cols.shape, 0), slot, 0)
+    return place
 
 
 def store_blocks(total, first_row, place_ref, out_ref):
     total = total.astype(BF16)
     for r in range(KG):
         for u in range(8):
-            out_ref[first_row + r, place_ref[r, u]] = total[r * B:(r + 1) * B, u * B:(u + 1) * B]
-
-
-def one_set(s, set_base, src_ref, c_cols_ref, mask_ref, a_ref, pool_ref, merged_ref, place_ref,
-            blocks_ref):
+            out_ref[first_row + r, place_ref[u, first_row + r]] = total[r * B:(r + 1) * B, u * B:(u + 1) * B]
+
+
+def one_set(s, src_ref, mask_ref, a_ref, pool_ref, merged_ref, place_ref, blocks_ref):
     first = s * FS
-    order_slots(c_cols_ref, set_base + s, s * KG, place_ref)
     for i in range(FS):
         merge_row(first + i, i, first + i, src_ref, mask_ref, a_ref, pool_ref, merged_ref)
     own = pool_ref[pl.ds(first, FS)].reshape(FS * B, KG * B)
@@ -251,9 +285,9 @@
 
 
 def operator_kernel(c_cols_hbm, cols_hbm, a_cols_hbm, a_hbm, pool_hbm,
-                    a_rows_hbm, a_next_hbm, out_hbm, local_hbm, flags_hbm, sel_hbm,
+                    a_rows_hbm, a_next_hbm, out_hbm, local_hbm, flags_hbm, sel_hbm, places_hbm,
                     c_cols_ref, cols_ref, a_cols_ref, a_ref, rows_ref, pool_ref, blocks_ref, merged_ref,
-                    mask_ref, local_ref, sel_ref, order_v, src_v, flag_v, order_ref, src_ref, flag_s,
+                    mask_ref, local_ref, sel_ref, order_v, src_v, flag_v, place_v, order_ref, src_ref, flag_s,
                     place_ref, t0, t1, t2, t3, in_sems, sems, keep_sems, out_sems):
     def fetch(c):
         return pltpu.make_async_copy(a_hbm.at[:, quarter(c)], a_ref.at[:, quarter(c)], in_sems.at[c])
@@ -295,12 +329,14 @@
     flag_v[...] = jnp.where(iota((8, 128), 1) < 64, away, read).astype(jnp.int32)
     src_v[:, :PAD] = sorted_slots(src, sel)
     src_v[:, PAD:] = jnp.zeros((8, 128 - PAD), jnp.int32)
+    place_v[:, :SETS * KG] = slot_places(c_cols_ref[...], set_base)
+    place_v[:, SETS * KG:] = jnp.zeros((8, 128 - SETS * KG), jnp.int32)
     mask_ref[...] = own_mask(src, keys, sel)
     to_smem = load_all(((order_v, order_ref), (src_v, src_ref), (flag_v, flag_s),
-                        (local_ref, local_hbm), (flag_v, flags_hbm), (sel_ref, sel_hbm)),
-                       sems.at[pl.ds(4, 6)])
+                        (place_v, place_ref), (local_ref, local_hbm), (flag_v, flags_hbm),
+                        (sel_ref, sel_hbm), (place_v, places_hbm)),
+                       sems.at[pl.ds(4, 8)])
     begin(to_smem)
-    finished(to_smem)
 
     def keep(c, s):
         rows = pl.ds(s * FS, FS)
@@ -325,6 +361,11 @@
             for h in range(4):
                 pair = jnp.concatenate(x[2 * h:2 * h + 2], axis=0)
                 t_refs[h][a * STRIDE:a * STRIDE + ROWS, :] = jnp.transpose(pair).astype(F32)
+
+        @pl.when(c == 0)
+        def _():
+            finished(to_smem)
+
         for i in range(ROWS):
             rows_ref[i, quarter(c), :] = jnp.concatenate(
                 [t[pl.ds(order_ref[0, i], CHUNK, stride=STRIDE), :] for t in t_refs], axis=1
@@ -349,8 +390,7 @@
     def work(s, carry):
         @pl.when(flag_s[s + 1, 0] == 0)
         def _():
-            one_set(s, set_base, src_ref, c_cols_ref, mask_ref, rows_ref, pool_ref, merged_ref,
-                    place_ref, blocks_ref)
+            one_set(s, src_ref, mask_ref, rows_ref, pool_ref, merged_ref, place_ref, blocks_ref)
             store(s).start()
         return carry
 
@@ -374,9 +414,9 @@
     return call(
         operator_kernel, "operator", [HBM] * 4 + [ANY],
         [((ROWS, B, 8 * B), BF16), ((HALF, B, 8 * B), BF16), ((SETS * KG, 8, B, B), BF16), ((8, ROWS), F32),
-         ((8, 128), jnp.int32), ((PAD, ROWS), BF16)],
+         ((8, 128), jnp.int32), ((PAD, ROWS), BF16), ((8, 128), jnp.int32)],
         [
-            pltpu.SMEM((8, SETS * KG), jnp.int32),
+            pltpu.VMEM((8, SETS * KG), jnp.int32),
             pltpu.VMEM((3, ROWS), jnp.int32),
             pltpu.VMEM((7, ROWS), jnp.int32),
             pltpu.VMEM((7, B, B, ROWS), BF16),
@@ -390,13 +430,14 @@
             pltpu.VMEM((8, 128), jnp.int32),
             pltpu.VMEM((8, 128), jnp.int32),
             pltpu.VMEM((8, 128), jnp.int32),
-            pltpu.SMEM((8, 128), jnp.int32),
-            pltpu.SMEM((8, 128), jnp.int32),
-            pltpu.SMEM((8, 128), jnp.int32),
-            pltpu.SMEM((KG, 8), jnp.int32),
+            pltpu.VMEM((8, 128), jnp.int32),
+            pltpu.SMEM((8, 128), jnp.int32),
+            pltpu.SMEM((8, 128), jnp.int32),
+            pltpu.SMEM((8, 128), jnp.int32),
+            pltpu.SMEM((8, 128), jnp.int32),
         ] + [pltpu.VMEM((CHUNK * STRIDE, 128), F32)] * 4 + [
             pltpu.SemaphoreType.DMA((QUARTERS,)),
-            pltpu.SemaphoreType.DMA((10,)),
+            pltpu.SemaphoreType.DMA((12,)),
             pltpu.SemaphoreType.DMA((QUARTERS, SETS + 1)),
             pltpu.SemaphoreType.DMA((SETS,)),
         ],
@@ -420,17 +461,27 @@
 
 
 def straddle_kernel(a_cols_hbm, local_hbm, flags_hbm, sel_hbm, a_next_hbm, pool_hbm, *refs):
-    parts = refs[:4]
-    (out_hbm, src_hbm, mask_hbm, a_cols_ref, local_ref, flag_ref, sel_ref, pool_ref, rows_ref,
-     names_ref, merged_ref, partial_ref, mask_ref, src_v, src_ref, sems, pool_sems, small_sems) = refs[4:]
+    *parts, back_hbm = refs[:4]
+    (out_hbm, src_hbm, mask_hbm, after_hbm, a_cols_ref, local_ref, flag_ref, sel_ref, pool_ref, rows_ref,
+     names_ref, back_names_ref, narrow_ref, merged_ref, partial_ref, mask_ref, src_v, src_ref, places_v,
+     places_ref, sems, pool_sems, small_sems) = refs[4:]
     small = load_all(
         [(flags_hbm, flag_ref), (a_cols_hbm, a_cols_ref), (local_hbm, local_ref), (sel_hbm, sel_ref)]
-        + [(part.at[part.shape[0] - 1], names_ref.at[n]) for n, part in enumerate(parts)], small_sems)
+        + [(part.at[part.shape[0] - 1], names_ref.at[n]) for n, part in enumerate(parts)]
+        + [(back_hbm.at[back_hbm.shape[0] - 1], back_names_ref)], small_sems)
     begin(small)
     loads = pool_copies(parts, pool_ref, sems)
     loads.append(pltpu.make_async_copy(a_next_hbm, rows_ref, small_sems.at[8]))
-    begin(loads)
+    narrow = [
+        pltpu.make_async_copy(back_hbm.at[pl.ds(c * NARROW, NARROW)],
+                              narrow_ref.at[:, pl.ds(c * CHUNK, CHUNK)], sems.at[3, c])
+        for c in range(QUARTERS)
+    ]
+    begin(narrow + loads)
     finished(small)
+    places_v[...] = back_names_ref[...].astype(F32).astype(jnp.int32)
+    places = pltpu.make_async_copy(places_v, places_ref, small_sems.at[13])
+    places.start()
     ids = devices()
 
     def unit(u):
@@ -452,7 +503,8 @@
     found = [jnp.zeros((1, ROWS), F32)] * 7
     for n in range(4):
         low, high = near[n]
-        column = jnp.transpose(names_ref[n][:, :128].astype(F32))[low:high, 0:1].astype(jnp.int32)
+        name = names_ref[n][:, :128] if n < 3 else back_names_ref[...]
+        column = jnp.transpose(name.astype(F32))[low:high, 0:1].astype(jnp.int32)
         row = iota((high - low, 1), 0) + low
         slot = jnp.zeros((high - low, 1), jnp.int32)
         for first, last, shift in shifts[n]:
@@ -474,6 +526,19 @@
     begin(out[:2])
     mask_ref[...] = own_mask(src, local[7:8, :], sel)
     out[2].start()
+    finished(narrow + [places])
+    one = (iota((B, KG * B), 1) & (B - 1)) == iota((B, KG * B), 0)
+    at = iota((B, KG * B), 1) >> 6
+    none = jnp.zeros((B, KG * B), BF16)
+    for m in range(BACK):
+        row = m if m < HALF else m + HALF
+        put = [jnp.where(one & (at == places_ref[1 + q, row]), 1.0, 0.0).astype(BF16) for q in range(3)]
+        put = put[:2] + ([put[2], none] if m % 2 == 0 else [none, put[2]])
+        blocks = jnp.concatenate([narrow_ref[m], narrow_ref[BACK + m // 2]], axis=1)
+        pool_ref[AFTER + m] = jnp.dot(
+            blocks, jnp.concatenate(put, axis=0), preferred_element_type=F32).astype(BF16)
+    wide = pltpu.make_async_copy(pool_ref.at[pl.ds(AFTER, BACK)], after_hbm, small_sems.at[14])
+    wide.start()
     finished(out[:1] + loads)
     for u in range(7):
         @pl.when(read(u))
@@ -485,13 +550,14 @@
     partial_ref[...] = tn(own, merged_ref[...]).astype(BF16)
     last = pltpu.make_async_copy(partial_ref, out_hbm, small_sems.at[12])
     last.start()
-    finished(out[1:] + [last])
+    finished(out[1:] + [wide, last])
 
 
 def straddle(a_cols_t, local, flags, sel, a_next, pool, parts):
     return call(
         straddle_kernel, "straddle", [HBM] + [ANY] * 9,
-        [((KG * B, 8 * B), BF16), ((8, 128), jnp.int32), ((PAD, 8 * B), F32)],
+        [((KG * B, 8 * B), BF16), ((8, 128), jnp.int32), ((PAD, 8 * B), F32),
+         ((BACK, B, KG * B), BF16)],
         [
             pltpu.VMEM((7, ROWS), jnp.int32),
             pltpu.VMEM((8, ROWS), F32),
@@ -499,30 +565,34 @@
             pltpu.VMEM((PAD, ROWS), BF16),
             pltpu.VMEM((POOL, B, KG * B), BF16),
             pltpu.VMEM((HALF, B, 8 * B), BF16),
-            pltpu.VMEM((4, 16, KG * B), BF16),
+            pltpu.VMEM((3, 16, KG * B), BF16),
+            pltpu.VMEM((16, 128), BF16),
+            pltpu.VMEM((NARROW, B, 128), BF16),
             pltpu.VMEM((HALF * B, 8 * B), BF16),
             pltpu.VMEM((KG * B, 8 * B), BF16),
             pltpu.VMEM((PAD, 8 * B), F32),
             pltpu.VMEM((8, 128), jnp.int32),
             pltpu.SMEM((8, 128), jnp.int32),
+            pltpu.VMEM((16, 128), jnp.int32),
+            pltpu.SMEM((16, 128), jnp.int32),
             pltpu.SemaphoreType.DMA((4, QUARTERS)),
             pltpu.SemaphoreType.DMA((7,)),
-            pltpu.SemaphoreType.DMA((13,)),
+            pltpu.SemaphoreType.DMA((15,)),
         ],
-        300_000_000, 6_000_000, 14,
+        600_000_000, 6_000_000, 16,
     )(a_cols_t, local, flags, sel, a_next, pool, *parts)
 
 
-def sets_kernel(src_hbm, flags_hbm, c_cols_hbm, mask_hbm, a_rows_hbm, pool_hbm, *refs):
-    parts = refs[:4]
-    (_, out_hbm, first_hbm, src_ref, flag_ref, c_cols_ref, mask_ref, first_ref, pool_ref, rows_ref,
-     blocks_ref, merged_ref, place_ref, small_sems, sems, row_sems, out_sems) = refs[4:]
-    small = load_all(((flags_hbm, flag_ref), (src_hbm, src_ref), (c_cols_hbm, c_cols_ref),
+def sets_kernel(src_hbm, flags_hbm, places_hbm, mask_hbm, a_rows_hbm, pool_hbm, *refs):
+    *parts, after_hbm = refs[:4]
+    (_, out_hbm, first_hbm, src_ref, flag_ref, place_ref, mask_ref, first_ref, pool_ref, rows_ref,
+     blocks_ref, merged_ref, small_sems, sems, row_sems, out_sems) = refs[4:]
+    small = load_all(((flags_hbm, flag_ref), (src_hbm, src_ref), (places_hbm, place_ref),
                       (mask_hbm, mask_ref)), small_sems)
     begin(small)
     loads = pool_copies(parts, pool_ref, sems) + [
-        pltpu.make_async_copy(pool_hbm, pool_ref.at[pl.ds(0, ROWS)], small_sems.at[4])]
-    set_base = devices()[0] * SETS
+        pltpu.make_async_copy(pool_hbm, pool_ref.at[pl.ds(0, ROWS)], small_sems.at[4]),
+        pltpu.make_async_copy(after_hbm, pool_ref.at[pl.ds(AFTER, BACK)], sems.at[3, 0])]
 
     def fetch(s):
         rows = pl.ds(s * FS, FS)
@@ -555,8 +625,7 @@
         @pl.when(here(s))
         def _():
             fetch(s).wait()
-            one_set(s, set_base, src_ref, c_cols_ref, mask_ref, rows_ref, pool_ref, merged_ref,
-                    place_ref, blocks_ref)
+            one_set(s, src_ref, mask_ref, rows_ref, pool_ref, merged_ref, place_ref, blocks_ref)
             store(s).start()
         return carry
 
@@ -572,57 +641,53 @@
     first.wait()
 
 
-def sets(src, flags, c_cols_t, mask, a_rows, pool, parts, whole):
+def sets(src, flags, places, mask, a_rows, pool, parts, whole):
     return call(
-        sets_kernel, "sets", [ANY] * 2 + [HBM] + [ANY] * 8,
+        sets_kernel, "sets", [ANY] * 11,
         [((SETS * KG, 8, B, B), BF16), ((KG * B, 8 * B), F32)],
         [
             pltpu.SMEM((8, 128), jnp.int32),
             pltpu.SMEM((8, 128), jnp.int32),
-            pltpu.SMEM((8, SETS * KG), jnp.int32),
+            pltpu.SMEM((8, 128), jnp.int32),
             pltpu.VMEM((PAD, 8 * B), F32),
             pltpu.VMEM((KG * B, 8 * B), F32),
             pltpu.VMEM((POOL, B, KG * B), BF16),
             pltpu.VMEM((ROWS, B, 8 * B), BF16),
             pltpu.VMEM((SETS * KG, 8, B, B), BF16),
             pltpu.VMEM((FS * B, 8 * B), BF16),
-            pltpu.SMEM((KG, 8), jnp.int32),
             pltpu.SemaphoreType.DMA((6,)),
             pltpu.SemaphoreType.DMA((4, QUARTERS)),
             pltpu.SemaphoreType.DMA((SETS,)),
             pltpu.SemaphoreType.DMA((SETS,)),
         ],
         2_500_000_000, 12_000_000, 48, aliases={10: 0},
-    )(src, flags, c_cols_t, mask, a_rows, pool, *parts, whole)
-
-
-def finish_kernel(c_cols_hbm, first_hbm, incoming_hbm, _, out_hbm, c_cols_ref, first_ref, incoming_ref,
-                  blocks_ref, place_ref, sems):
-    loads = load_all(((c_cols_hbm, c_cols_ref), (first_hbm, first_ref), (incoming_hbm, incoming_ref)),
+    )(src, flags, places, mask, a_rows, pool, *parts, whole)
+
+
+def finish_kernel(places_hbm, first_hbm, incoming_hbm, _, out_hbm, place_ref, first_ref, incoming_ref,
+                  blocks_ref, sems):
+    loads = load_all(((places_hbm, place_ref), (first_hbm, first_ref), (incoming_hbm, incoming_ref)),
                      sems)
     begin(loads)
-    finished(loads[:1])
-    order_slots(c_cols_ref, devices()[0] * SETS, 0, place_ref)
-    finished(loads[1:])
+    finished(loads)
     store_blocks(first_ref[...] + incoming_ref[...].astype(F32), 0, place_ref, blocks_ref)
     copy = pltpu.make_async_copy(blocks_ref, out_hbm.at[pl.ds(0, KG)], sems.at[3])
     copy.start()
     copy.wait()
 
 
-def finish(c_cols_t, first, incoming, whole):
+def finish(places, first, incoming, whole):
     return call(
-        finish_kernel, "finish", [HBM] + [ANY] * 3, [((SETS * KG, 8, B, B), BF16)],
+        finish_kernel, "finish", [ANY] * 4, [((SETS * KG, 8, B, B), BF16)],
         [
-            pltpu.SMEM((8, SETS * KG), jnp.int32),
+            pltpu.SMEM((8, 128), jnp.int32),
             pltpu.VMEM((KG * B, 8 * B), F32),
             pltpu.VMEM((KG * B, 8 * B), BF16),
             pltpu.VMEM((KG, 8, B, B), BF16),
-            pltpu.SMEM((KG, 8), jnp.int32),
             pltpu.SemaphoreType.DMA((4,)),
         ],
         1_000_000, 1_500_000, 6, aliases={3: 0},
-    )(c_cols_t, first, incoming, whole)[0]
+    )(places, first, incoming, whole)[0]
 
 
 def shards(a_blocks, a_cols, p_blocks, p_cols, c_cols):
@@ -630,12 +695,13 @@
     moves = (("dom", 1), ("dom", -1), ("sub", 1), ("sub", -1))
     pool, *sends = prolong(cols_t, p_blocks.transpose(1, 2, 3, 0))
     parts = [passed_along(rows, axis, step) for rows, (axis, step) in zip(sends, moves)]
-    a_rows, a_next, whole, local, flags, sel = operator(
+    a_rows, a_next, whole, local, flags, sel, places = operator(
         c_cols_t, cols_t, a_cols_t, a_blocks.transpose(1, 2, 3, 0), pool)
-    partial, src, mask = straddle(a_cols_t, local, flags, sel, a_next, pool, parts)
+    partial, src, mask, after = straddle(a_cols_t, local, flags, sel, a_next, pool, parts)
     incoming = passed_along(partial, "sub", 1)
-    whole, first = sets(src, flags, c_cols_t, mask, a_rows, pool, parts, whole)
-    return finish(c_cols_t, first, incoming, whole)
+    whole, first = sets(
+        src, flags, places, mask, a_rows, pool, parts[:3] + [after], whole)
+    return finish(places, first, incoming, whole)
 
 
 def solution(mesh):

time: 43.2 us -> 42.8 us (level)
  waiting for transfers between devices: 9.33 us -> 8.19 us
  Pallas kernels: 26.5 us -> 27.2 us
    ppermute x5, waiting for transfers between devices: 9.33 us -> 8.19 us  [passed_along(): lax.ppermute(block, axis, [((i - distance) % n, i) for i in range(n)])]
    pallas_call x1, Pallas kernels: 2.96 us -> 3.65 us  [straddle(): call(straddle_kernel, 'straddle', [HBM] + [ANY] * 9, [((KG * B, 8 * B), B...]
  transfers between devices with their start and end apart: 5 -> 5, of which waited for: 3 -> 2; matrix products, arithmetic and copies ran while one was open for 0% -> 0% of each run, Pallas kernels for 35% -> 36%
where the time goes in v4:
time: 42.8 us; the launch traced here: 42.6 us
  Pallas kernels  27.2 us (64%)
  waiting for transfers between devices  8.19 us (19%)
  starting transfers between devices  7.12 us (17%)
    pallas_call x1, Pallas kernels, operator(): call(operator_kernel, 'operator', [HBM] * 4 + [ANY], [((ROWS, B, 8 * B),...  8.62 us
    ppermute x5, waiting for transfers between devices, passed_along(): lax.ppermute(block, axis, [((i - distance) % n, i) for i in range(n)])  8.19 us
    ppermute x5, starting transfers between devices, passed_along(): lax.ppermute(block, axis, [((i - distance) % n, i) for i in range(n)])  7.12 us
    pallas_call x1, Pallas kernels, sets(): call(sets_kernel, 'sets', [ANY] * 11, [((SETS * KG, 8, B, B), BF16), ((KG...  6.68 us
    pallas_call x1, Pallas kernels, prolong(): call(prolong_kernel, 'prolong', [pl.BlockSpec((3, ROWS), lambda c: (0, 0)...  6.62 us
    pallas_call x1, Pallas kernels, straddle(): call(straddle_kernel, 'straddle', [HBM] + [ANY] * 9, [((KG * B, 8 * B), B...  3.65 us
    pallas_call x1, Pallas kernels, finish(): call(finish_kernel, 'finish', [ANY] * 4, [((SETS * KG, 8, B, B), BF16)],...  1.63 us
  transfers between devices with their start and end apart: 5, of which 2 were waited for; matrix products, arithmetic and copies ran while one was open for 0% of the time, Pallas kernels for 36%

profile of v4, /device:TPU:96, one launch (start us, length us, event | category | flops | bytes accessed | tf_op | source)
XLA Modules:
  0.0 42.6 jit_solution(162117522328877659)
XLA Ops:
  0.0 0.0 copy-start.1
  0.0 0.0 copy-start.2
  0.0 0.0 copy-start.3
  0.0 6.6 %prolong.1 = (bf16[84,64,256]{2,1,0:T(8,128)(2,1)}, bf16[57,16,256]{2,1,0:T(8,128)(2,1)}, bf16[57,16,256]{2,1,0:T(8,128)(2,1)}, bf16[29,16,256]{2,1,0:T(8,128)(2,1)}, bf16[129,16,128]{2,1,0:T(8,128)(2,1)}) custom-call(s32[3,84]{1,0:T(4,128)} %bitcast.8, bf16[3,64,64,84]{3,2,1,0:T(8,128)(2,1)} %bitcast.11), custom_call_target="tpu_custom_call" | custom-call | flops 6000000000 | bytes 8000000 | tf_op jit(solution)/shard_map/prolong/pallas_call | solution.py:208
  6.6 5.3 %collective-permute-start.3 = (bf16[129,16,128]{2,1,0:T(8,128)(2,1)}, bf16[129,16,128]{2,1,0:T(8,128)(2,1)S(1)}, u32[]{:S(2)}, u32[]{:S(2)}) collective-permute-start(bf16[129,16,128]{2,1,0:T(8,128)(2,1)} %get-tuple-element.32), channel_id=1, source_target_pairs={{1,0},{2,1},{3,2},{4,3},{5,4},{6,5},{7,6},{8,7},{9,8},{10,9},{11,1... | collective-permute-start | bytes 1585160 | tf_op jit(solution)/shard_map/ppermute | solution.py:22
  11.9 0.0 collective-permute-start
  11.9 1.7 %collective-permute-start.1 = (bf16[57,16,256]{2,1,0:T(8,128)(2,1)}, bf16[57,16,256]{2,1,0:T(8,128)(2,1)S(1)}, u32[]{:S(2)}, u32[]{:S(2)}) collective-permute-start(bf16[57,16,256]{2,1,0:T(8,128)(2,1)} %get-tuple-element.30), channel_id=1, source_target_pairs={{16,0},{32,16},{48,32},{64,48},{80,64},{96,80},{112,96},{128,112},... | collective-permute-start | bytes 1400840 | tf_op jit(solution)/shard_map/ppermute | solution.py:22
  13.7 0.0 collective-permute-start.2
  13.7 0.0 copy-done.1
  13.7 0.0 copy-done.2
  13.7 0.0 copy-done.3
  13.7 0.0 copy-start
  13.7 8.6 %operator.1 = (bf16[84,64,512]{2,1,0:T(8,128)(2,1)}, bf16[7,64,512]{2,1,0:T(8,128)(2,1)S(1)}, bf16[24,8,64,64]{3,2,1,0:T(8,128)(2,1)}, f32[8,84]{1,0:T(8,128)S(1...) custom-call(s32[8,24]{1,0:T(8,128)S(1)} %bitcast.7, s32[3,84]{1,0:T(4,128)S(1)} %bitcast.9, ...), custom_call_target="tpu_custom_call" | custom-call | flops 4000000000 | bytes 18000000 | tf_op jit(solution)/shard_map/operator/pallas_call | solution.py:414
  22.3 3.1 %collective-permute-done.2.refs_2_ = bf16[29,16,256]{2,1,0:T(8,128)(2,1)S(1)} collective-permute-done((bf16[29,16,256]{2,1,0:T(8,128)(2,1)}, bf16[29,16,256]{2,1,0:T(8,128)(2,1)S(1)}, u32[]{:S(2)}, u32[]{:S(2)}) %collective-permute-start.2) | collective-permute-done | bytes 237600 | tf_op jit(solution)/shard_map/ppermute | solution.py:22
  25.4 0.0 collective-permute-done.refs_0_
  25.4 0.0 collective-permute-done.1.refs_1_
  25.4 0.0 collective-permute-done.3.refs_3_
  25.4 0.0 copy-done
  25.4 3.6 %straddle.1 = (bf16[256,512]{1,0:T(8,128)(2,1)S(1)}, s32[8,128]{1,0:T(8,128)S(1)}, f32[88,512]{1,0:T(8,128)S(1)}, bf16[21,64,256]{2,1,0:T(8,128)(2,1)S(1)}) custom-call(s32[7,84]{1,0:T(8,128)S(1)} %bitcast.6, f32[8,84]{1,0:T(8,128)S(1)} %get-tuple-element.25.local_hbm, s32[8,128]{1,0:T(8,128)S(1)} %get-tuple-element.26.flags_hbm, ...), custom_call_target="tpu_custom_call" | custom-call | flops 600000000 | bytes 6000000 | tf_op jit(solution)/shard_map/straddle/pallas_call | solution.py:557
  29.1 0.1 collective-permute-start.4
  29.2 6.7 %sets.1 = (bf16[24,8,64,64]{3,2,1,0:T(8,128)(2,1)}, f32[256,512]{1,0:T(8,128)S(1)}) custom-call(s32[8,128]{1,0:T(8,128)S(1)} %get-tuple-element.33.src_hbm, s32[8,128]{1,0:T(8,128)S(1)} %get-tuple-element.26.flags_hbm, s32[8,128]{1,0:T(8,128)S(1)} %get-tuple-element.24.places_hbm, ...), custom_call_target="tpu_custom_call", output_to_operand_aliasing={{0}: (10, {})} | custom-call | flops 2500000000 | bytes 12000000 | tf_op jit(solution)/shard_map/sets/pallas_call | solution.py:645
  35.8 5.1 %collective-permute-done.4.incoming_hbm = bf16[256,512]{1,0:T(8,128)(2,1)S(1)} collective-permute-done((bf16[256,512]{1,0:T(8,128)(2,1)S(1)}, bf16[256,512]{1,0:T(8,128)(2,1)S(1)}, u32[]{:S(2)}, u32[]{:S(2)}) %collective-permute-start.4) | collective-permute-done | bytes 262176 | tf_op jit(solution)/shard_map/ppermute | solution.py:22
  41.0 1.6 %finish.1 = bf16[24,8,64,64]{3,2,1,0:T(8,128)(2,1)} custom-call(s32[8,128]{1,0:T(8,128)S(1)} %get-tuple-element.24.places_hbm, f32[256,512]{1,0:T(8,128)S(1)} %get-tuple-element.38.first_hbm, bf16[256,512]{1,0:T(8,128)(2,1)S(1)} %collective-permute-done.4.incoming_hbm, bf16[24,8,64,64]{3,2,1,0:T(8,128)(2,1)} %get-tuple-element.40._), custom_call_target="tpu_custom_call", output_to_operand_aliasing={{}: (3, {})} | custom-call | flops 1000000 | bytes 1500000 | tf_op jit(solution)/shard_map/finish/pallas_call | solution.py:680
Async XLA Ops:
  0.0 13.7 %copy-start.1 = (s32[84,7]{0,1:T(8,128)S(1)}, s32[84,7]{0,1:T(8,128)}, u32[]{:S(2)}) copy-start(s32[84,7]{0,1:T(8,128)} %param.6) | copy-start | bytes 7060
  0.0 13.7 %copy-start.2 = (s32[24,8]{0,1:T(8,128)S(1)}, s32[24,8]{0,1:T(8,128)}, u32[]{:S(2)}) copy-start(s32[24,8]{0,1:T(8,128)} %param.9) | copy-start | bytes 2308
  0.0 13.7 %copy-start.3 = (s32[84,3]{0,1:T(4,128)S(1)}, s32[84,3]{0,1:T(4,128)}, u32[]{:S(2)}) copy-start(s32[84,3]{0,1:T(4,128)} %param.8) | copy-start | bytes 3028
  6.6 18.8 %collective-permute-start.3 = (bf16[129,16,128]{2,1,0:T(8,128)(2,1)}, bf16[129,16,128]{2,1,0:T(8,128)(2,1)S(1)}, u32[]{:S(2)}, u32[]{:S(2)}) collective-permute-start(bf16[129,16,128]{2,1,0:T(8,128)(2,1)} %get-tuple-element.32), channel_id=1, source_target_pairs={{1,0},{2,1},{3,2},{4,3},{5,4},{6,5},{7,6},{8,7},{9,8},{10,9},{11,1... | collective-permute-start | bytes 1585160 | tf_op jit(solution)/shard_map/ppermute | solution.py:22
  11.9 13.5 %collective-permute-start = (bf16[57,16,256]{2,1,0:T(8,128)(2,1)}, bf16[57,16,256]{2,1,0:T(8,128)(2,1)S(1)}, u32[]{:S(2)}, u32[]{:S(2)}) collective-permute-start(bf16[57,16,256]{2,1,0:T(8,128)(2,1)} %get-tuple-element.29), channel_id=1, source_target_pairs={{240,0},{0,16},{16,32},{32,48},{48,64},{64,80},{80,96},{96,112},{1... | collective-permute-start | bytes 1400840 | tf_op jit(solution)/shard_map/ppermute | solution.py:22
  11.9 13.5 %collective-permute-start.1 = (bf16[57,16,256]{2,1,0:T(8,128)(2,1)}, bf16[57,16,256]{2,1,0:T(8,128)(2,1)S(1)}, u32[]{:S(2)}, u32[]{:S(2)}) collective-permute-start(bf16[57,16,256]{2,1,0:T(8,128)(2,1)} %get-tuple-element.30), channel_id=1, source_target_pairs={{16,0},{32,16},{48,32},{64,48},{80,64},{96,80},{112,96},{128,112},... | collective-permute-start | bytes 1400840 | tf_op jit(solution)/shard_map/ppermute | solution.py:22
  13.7 11.7 %collective-permute-start.2 = (bf16[29,16,256]{2,1,0:T(8,128)(2,1)}, bf16[29,16,256]{2,1,0:T(8,128)(2,1)S(1)}, u32[]{:S(2)}, u32[]{:S(2)}) collective-permute-start(bf16[29,16,256]{2,1,0:T(8,128)(2,1)} %get-tuple-element.31), channel_id=1, source_target_pairs={{15,0},{0,1},{1,2},{2,3},{3,4},{4,5},{5,6},{6,7},{7,8},{8,9},{9,10... | collective-permute-start | bytes 712712 | tf_op jit(solution)/shard_map/ppermute | solution.py:22
  13.7 11.7 %copy-start = (bf16[84,64,256]{2,1,0:T(8,128)(2,1)S(1)}, bf16[84,64,256]{2,1,0:T(8,128)(2,1)}, u32[]{:S(2)}) copy-start(bf16[84,64,256]{2,1,0:T(8,128)(2,1)} %get-tuple-element.23.pool_hbm) | copy-start | bytes 8257540
  29.1 11.9 %collective-permute-start.4 = (bf16[256,512]{1,0:T(8,128)(2,1)S(1)}, bf16[256,512]{1,0:T(8,128)(2,1)S(1)}, u32[]{:S(2)}, u32[]{:S(2)}) collective-permute-start(bf16[256,512]{1,0:T(8,128)(2,1)S(1)} %get-tuple-element.39), channel_id=1, source_target_pairs={{15,0},{0,1},{1,2},{2,3},{3,4},{4,5},{5,6},{6,7},{7,8},{8,9},{9,10... | collective-permute-start | bytes 786440 | tf_op jit(solution)/shard_map/ppermute | solution.py:22

commit v5 on v4

--- a/solution.py
+++ b/solution.py
@@ -435,7 +435,7 @@
             pltpu.SMEM((8, 128), jnp.int32),
             pltpu.SMEM((8, 128), jnp.int32),
             pltpu.SMEM((8, 128), jnp.int32),
-        ] + [pltpu.VMEM((CHUNK * STRIDE, 128), F32)] * 4 + [
+        ] + [pltpu.VMEM(((CHUNK + 1) * STRIDE, 128), F32)] * 4 + [
             pltpu.SemaphoreType.DMA((QUARTERS,)),
             pltpu.SemaphoreType.DMA((12,)),
             pltpu.SemaphoreType.DMA((QUARTERS, SETS + 1)),

time: 42.8 us -> 42.8 us (level)
  no operation moved by 1% of the time
where the time goes in v5:
time: 42.8 us; the launch traced here: 42.6 us
  Pallas kernels  27.2 us (64%)
  waiting for transfers between devices  8.19 us (19%)
  starting transfers between devices  7.12 us (17%)
    pallas_call x1, Pallas kernels, operator(): call(operator_kernel, 'operator', [HBM] * 4 + [ANY], [((ROWS, B, 8 * B),...  8.62 us
    ppermute x5, waiting for transfers between devices, passed_along(): lax.ppermute(block, axis, [((i - distance) % n, i) for i in range(n)])  8.19 us
    ppermute x5, starting transfers between devices, passed_along(): lax.ppermute(block, axis, [((i - distance) % n, i) for i in range(n)])  7.12 us
    pallas_call x1, Pallas kernels, sets(): call(sets_kernel, 'sets', [ANY] * 11, [((SETS * KG, 8, B, B), BF16), ((KG...  6.68 us
    pallas_call x1, Pallas kernels, prolong(): call(prolong_kernel, 'prolong', [pl.BlockSpec((3, ROWS), lambda c: (0, 0)...  6.62 us
    pallas_call x1, Pallas kernels, straddle(): call(straddle_kernel, 'straddle', [HBM] + [ANY] * 9, [((KG * B, 8 * B), B...  3.65 us
    pallas_call x1, Pallas kernels, finish(): call(finish_kernel, 'finish', [ANY] * 4, [((SETS * KG, 8, B, B), BF16)],...  1.63 us
  transfers between devices with their start and end apart: 5, of which 2 were waited for; matrix products, arithmetic and copies ran while one was open for 0% of the time, Pallas kernels for 36%

profile of v5, /device:TPU:96, one launch (start us, length us, event | category | flops | bytes accessed | tf_op | source)
XLA Modules:
  0.0 42.6 jit_solution(2786831907113472371)
XLA Ops:
  0.0 0.0 copy-start.1
  0.0 0.0 copy-start.2
  0.0 0.0 copy-start.3
  0.0 6.6 %prolong.1 = (bf16[84,64,256]{2,1,0:T(8,128)(2,1)}, bf16[57,16,256]{2,1,0:T(8,128)(2,1)}, bf16[57,16,256]{2,1,0:T(8,128)(2,1)}, bf16[29,16,256]{2,1,0:T(8,128)(2,1)}, bf16[129,16,128]{2,1,0:T(8,128)(2,1)}) custom-call(s32[3,84]{1,0:T(4,128)} %bitcast.8, bf16[3,64,64,84]{3,2,1,0:T(8,128)(2,1)} %bitcast.11), custom_call_target="tpu_custom_call" | custom-call | flops 6000000000 | bytes 8000000 | tf_op jit(solution)/shard_map/prolong/pallas_call | solution.py:208
  6.6 5.3 %collective-permute-start.3 = (bf16[129,16,128]{2,1,0:T(8,128)(2,1)}, bf16[129,16,128]{2,1,0:T(8,128)(2,1)S(1)}, u32[]{:S(2)}, u32[]{:S(2)}) collective-permute-start(bf16[129,16,128]{2,1,0:T(8,128)(2,1)} %get-tuple-element.32), channel_id=1, source_target_pairs={{1,0},{2,1},{3,2},{4,3},{5,4},{6,5},{7,6},{8,7},{9,8},{10,9},{11,1... | collective-permute-start | bytes 1585160 | tf_op jit(solution)/shard_map/ppermute | solution.py:22
  11.9 0.0 collective-permute-start
  11.9 1.7 %collective-permute-start.1 = (bf16[57,16,256]{2,1,0:T(8,128)(2,1)}, bf16[57,16,256]{2,1,0:T(8,128)(2,1)S(1)}, u32[]{:S(2)}, u32[]{:S(2)}) collective-permute-start(bf16[57,16,256]{2,1,0:T(8,128)(2,1)} %get-tuple-element.30), channel_id=1, source_target_pairs={{16,0},{32,16},{48,32},{64,48},{80,64},{96,80},{112,96},{128,112},... | collective-permute-start | bytes 1400840 | tf_op jit(solution)/shard_map/ppermute | solution.py:22
  13.7 0.0 collective-permute-start.2
  13.7 0.0 copy-done.1
  13.7 0.0 copy-done.2
  13.7 0.0 copy-done.3
  13.7 0.0 copy-start
  13.7 8.6 %operator.1 = (bf16[84,64,512]{2,1,0:T(8,128)(2,1)}, bf16[7,64,512]{2,1,0:T(8,128)(2,1)S(1)}, bf16[24,8,64,64]{3,2,1,0:T(8,128)(2,1)}, f32[8,84]{1,0:T(8,128)S(1...) custom-call(s32[8,24]{1,0:T(8,128)S(1)} %bitcast.7, s32[3,84]{1,0:T(4,128)S(1)} %bitcast.9, ...), custom_call_target="tpu_custom_call" | custom-call | flops 4000000000 | bytes 18000000 | tf_op jit(solution)/shard_map/operator/pallas_call | solution.py:414
  22.3 3.1 %collective-permute-done.2.refs_2_ = bf16[29,16,256]{2,1,0:T(8,128)(2,1)S(1)} collective-permute-done((bf16[29,16,256]{2,1,0:T(8,128)(2,1)}, bf16[29,16,256]{2,1,0:T(8,128)(2,1)S(1)}, u32[]{:S(2)}, u32[]{:S(2)}) %collective-permute-start.2) | collective-permute-done | bytes 237600 | tf_op jit(solution)/shard_map/ppermute | solution.py:22
  25.4 0.0 collective-permute-done.refs_0_
  25.4 0.0 collective-permute-done.1.refs_1_
  25.4 0.0 collective-permute-done.3.refs_3_
  25.4 0.0 copy-done
  25.4 3.6 %straddle.1 = (bf16[256,512]{1,0:T(8,128)(2,1)S(1)}, s32[8,128]{1,0:T(8,128)S(1)}, f32[88,512]{1,0:T(8,128)S(1)}, bf16[21,64,256]{2,1,0:T(8,128)(2,1)S(1)}) custom-call(s32[7,84]{1,0:T(8,128)S(1)} %bitcast.6, f32[8,84]{1,0:T(8,128)S(1)} %get-tuple-element.25.local_hbm, s32[8,128]{1,0:T(8,128)S(1)} %get-tuple-element.26.flags_hbm, ...), custom_call_target="tpu_custom_call" | custom-call | flops 600000000 | bytes 6000000 | tf_op jit(solution)/shard_map/straddle/pallas_call | solution.py:557
  29.1 0.1 collective-permute-start.4
  29.2 6.7 %sets.1 = (bf16[24,8,64,64]{3,2,1,0:T(8,128)(2,1)}, f32[256,512]{1,0:T(8,128)S(1)}) custom-call(s32[8,128]{1,0:T(8,128)S(1)} %get-tuple-element.33.src_hbm, s32[8,128]{1,0:T(8,128)S(1)} %get-tuple-element.26.flags_hbm, s32[8,128]{1,0:T(8,128)S(1)} %get-tuple-element.24.places_hbm, ...), custom_call_target="tpu_custom_call", output_to_operand_aliasing={{0}: (10, {})} | custom-call | flops 2500000000 | bytes 12000000 | tf_op jit(solution)/shard_map/sets/pallas_call | solution.py:645
  35.8 5.1 %collective-permute-done.4.incoming_hbm = bf16[256,512]{1,0:T(8,128)(2,1)S(1)} collective-permute-done((bf16[256,512]{1,0:T(8,128)(2,1)S(1)}, bf16[256,512]{1,0:T(8,128)(2,1)S(1)}, u32[]{:S(2)}, u32[]{:S(2)}) %collective-permute-start.4) | collective-permute-done | bytes 262176 | tf_op jit(solution)/shard_map/ppermute | solution.py:22
  41.0 1.6 %finish.1 = bf16[24,8,64,64]{3,2,1,0:T(8,128)(2,1)} custom-call(s32[8,128]{1,0:T(8,128)S(1)} %get-tuple-element.24.places_hbm, f32[256,512]{1,0:T(8,128)S(1)} %get-tuple-element.38.first_hbm, bf16[256,512]{1,0:T(8,128)(2,1)S(1)} %collective-permute-done.4.incoming_hbm, bf16[24,8,64,64]{3,2,1,0:T(8,128)(2,1)} %get-tuple-element.40._), custom_call_target="tpu_custom_call", output_to_operand_aliasing={{}: (3, {})} | custom-call | flops 1000000 | bytes 1500000 | tf_op jit(solution)/shard_map/finish/pallas_call | solution.py:680
Async XLA Ops:
  0.0 13.7 %copy-start.1 = (s32[84,7]{0,1:T(8,128)S(1)}, s32[84,7]{0,1:T(8,128)}, u32[]{:S(2)}) copy-start(s32[84,7]{0,1:T(8,128)} %param.6) | copy-start | bytes 7060
  0.0 13.7 %copy-start.2 = (s32[24,8]{0,1:T(8,128)S(1)}, s32[24,8]{0,1:T(8,128)}, u32[]{:S(2)}) copy-start(s32[24,8]{0,1:T(8,128)} %param.9) | copy-start | bytes 2308
  0.0 13.7 %copy-start.3 = (s32[84,3]{0,1:T(4,128)S(1)}, s32[84,3]{0,1:T(4,128)}, u32[]{:S(2)}) copy-start(s32[84,3]{0,1:T(4,128)} %param.8) | copy-start | bytes 3028
  6.6 18.8 %collective-permute-start.3 = (bf16[129,16,128]{2,1,0:T(8,128)(2,1)}, bf16[129,16,128]{2,1,0:T(8,128)(2,1)S(1)}, u32[]{:S(2)}, u32[]{:S(2)}) collective-permute-start(bf16[129,16,128]{2,1,0:T(8,128)(2,1)} %get-tuple-element.32), channel_id=1, source_target_pairs={{1,0},{2,1},{3,2},{4,3},{5,4},{6,5},{7,6},{8,7},{9,8},{10,9},{11,1... | collective-permute-start | bytes 1585160 | tf_op jit(solution)/shard_map/ppermute | solution.py:22
  11.9 13.5 %collective-permute-start = (bf16[57,16,256]{2,1,0:T(8,128)(2,1)}, bf16[57,16,256]{2,1,0:T(8,128)(2,1)S(1)}, u32[]{:S(2)}, u32[]{:S(2)}) collective-permute-start(bf16[57,16,256]{2,1,0:T(8,128)(2,1)} %get-tuple-element.29), channel_id=1, source_target_pairs={{240,0},{0,16},{16,32},{32,48},{48,64},{64,80},{80,96},{96,112},{1... | collective-permute-start | bytes 1400840 | tf_op jit(solution)/shard_map/ppermute | solution.py:22
  11.9 13.5 %collective-permute-start.1 = (bf16[57,16,256]{2,1,0:T(8,128)(2,1)}, bf16[57,16,256]{2,1,0:T(8,128)(2,1)S(1)}, u32[]{:S(2)}, u32[]{:S(2)}) collective-permute-start(bf16[57,16,256]{2,1,0:T(8,128)(2,1)} %get-tuple-element.30), channel_id=1, source_target_pairs={{16,0},{32,16},{48,32},{64,48},{80,64},{96,80},{112,96},{128,112},... | collective-permute-start | bytes 1400840 | tf_op jit(solution)/shard_map/ppermute | solution.py:22
  13.7 11.7 %collective-permute-start.2 = (bf16[29,16,256]{2,1,0:T(8,128)(2,1)}, bf16[29,16,256]{2,1,0:T(8,128)(2,1)S(1)}, u32[]{:S(2)}, u32[]{:S(2)}) collective-permute-start(bf16[29,16,256]{2,1,0:T(8,128)(2,1)} %get-tuple-element.31), channel_id=1, source_target_pairs={{15,0},{0,1},{1,2},{2,3},{3,4},{4,5},{5,6},{6,7},{7,8},{8,9},{9,10... | collective-permute-start | bytes 712712 | tf_op jit(solution)/shard_map/ppermute | solution.py:22
  13.7 11.7 %copy-start = (bf16[84,64,256]{2,1,0:T(8,128)(2,1)S(1)}, bf16[84,64,256]{2,1,0:T(8,128)(2,1)}, u32[]{:S(2)}) copy-start(bf16[84,64,256]{2,1,0:T(8,128)(2,1)} %get-tuple-element.23.pool_hbm) | copy-start | bytes 8257540
  29.1 11.9 %collective-permute-start.4 = (bf16[256,512]{1,0:T(8,128)(2,1)S(1)}, bf16[256,512]{1,0:T(8,128)(2,1)S(1)}, u32[]{:S(2)}, u32[]{:S(2)}) collective-permute-start(bf16[256,512]{1,0:T(8,128)(2,1)S(1)} %get-tuple-element.39), channel_id=1, source_target_pairs={{15,0},{0,1},{1,2},{2,3},{3,4},{4,5},{5,6},{6,7},{7,8},{8,9},{9,10... | collective-permute-start | bytes 786440 | tf_op jit(solution)/shard_map/ppermute | solution.py:22
